TPU v7x, 256 devices: a whole 4x4x8 slice. The times are simulated.
256 devices in a mesh: space: 128 (over z, y, x), col: 2 (over core).
Axes of the slice: x: 4, y: 4, z: 8, core: 2. Of those that a mesh axis runs over, the one named last changes fastest.
Arguments:
- block: float32 [96, 3, 512, 16, 128], P('col', None, 'space'), may hold values from -40 to 40, as said below
- material: int32 [512, 16, 128], P('space'), may hold values from 0 to 7
- eps_table: float32 [8], replicated, may hold values from 1 to 12
- edge_mask: int32 [3, 512, 16, 128], P(None, 'space'), may hold values 0 or 1
Outputs:
- residual: float32 [96, 3, 512, 16, 128], P('col', None, 'space')
- gram_a: float32 [96, 96], P('col')
- gram_b: float32 [96, 96], P('col')
- gram_flux: float32 [96, 96], P('col')
Inputs may be any that keep to these rules, and one draw needn't show every extreme that they name: Entries of the block are bounded.
All inputs are finite; a program needn't handle non-finite values. No bound on the sum of `edge_mask` on one device may be relied on, other than what follows from the above.
Results may differ from a plain program's by a relative error of at most 0.000094.
Values sent between devices are 32-bit elements; how exact they have to be, the bound alone decides.
No kernel may reach another device: no remote copies, remote signals or barrier semaphores. Data moves between devices by JAX's collectives and lax.ppermute only.
A program may use at most 128 MiB of HBM per device.

v0:
```python
import jax
import jax.numpy as jnp
from jax import lax
from jax.sharding import PartitionSpec as P


def with_halo(cells, sides, width):
    for axis, dim in sides:
        count = lax.axis_size(axis)
        ends = count - 1
        head = lax.slice_in_dim(cells, 0, width, axis=dim)
        tail = lax.slice_in_dim(cells, cells.shape[dim] - width, cells.shape[dim], axis=dim)
        cells = jnp.concatenate(
            [
                lax.ppermute(tail, axis, [(i, (i + 1) % count) for i in range(ends)]),
                cells,
                lax.ppermute(head, axis, [((i + 1) % count, i) for i in range(ends)]),
            ],
            axis=dim,
        )
    return cells


def forward_diff(field, axis):
    size = field.shape[axis]
    ahead = lax.slice_in_dim(field, 1, size, axis=axis)
    widths = [(0, 0)] * field.ndim
    widths[axis] = (0, 1)
    return jnp.pad(ahead, widths) - field


def backward_diff(field, axis):
    size = field.shape[axis]
    behind = lax.slice_in_dim(field, 0, size - 1, axis=axis)
    widths = [(0, 0)] * field.ndim
    widths[axis] = (1, 0)
    return jnp.pad(behind, widths) - field


def curl_curl(padded):
    ex_low, ey_low, ez_low = (padded[:, 0, :-1], padded[:, 1, :-1], padded[:, 2, :-1])
    ex_up, ey_up = (padded[:, 0, 1:], padded[:, 1, 1:])
    hx_field = forward_diff(ez_low, 2) - (ey_up - ey_low)
    hy_field = ex_up - ex_low - forward_diff(ez_low, 3)
    hz_field = forward_diff(ey_low, 3) - forward_diff(ex_low, 2)
    kx_field = hy_field[:, :-1] - hy_field[:, 1:] - backward_diff(hz_field[:, 1:], 2)
    ky_field = backward_diff(hz_field[:, 1:], 3) - (hx_field[:, :-1] - hx_field[:, 1:])
    kz_field = backward_diff(hx_field[:, 1:], 2) - backward_diff(hy_field[:, 1:], 3)
    return jnp.stack([kx_field, ky_field, kz_field], axis=1)


def lookup(material, eps_table):
    eps = jnp.zeros(material.shape, jnp.float32)
    for index in range(eps_table.shape[0]):
        eps = eps + jnp.where(material == index, eps_table[index], jnp.float32(0.0))
    return eps


def inner(left, right):
    return jnp.dot(
        left.reshape(left.shape[0], -1),
        right.reshape(right.shape[0], -1).T,
        precision=lax.Precision.HIGHEST,
        preferred_element_type=jnp.float32,
    )


def shards(block, material, eps_table, edge_mask):
    ncol = block.shape[0]
    total_cols = ncol * lax.axis_size("col")
    keep = edge_mask.astype(jnp.float32)
    eps = lookup(material, eps_table)
    mass = eps[None] * keep
    inv_mass = keep / eps[None]
    masked = block * keep
    padded = with_halo(masked, (("space", 2),), 1)
    image = curl_curl(padded) * keep
    mass_image = block * mass
    scale = 1.0 / (3.0 * block.shape[2] * lax.axis_size("space") * block.shape[3] * block.shape[4])
    flux = image * inv_mass
    block_piece = lax.all_gather(block, "col", axis=0, tiled=True)
    image_piece = lax.all_gather(image, "col", axis=0, tiled=True)
    terms = jnp.stack(
        [inner(image, block_piece), inner(mass_image, block_piece), inner(flux, image_piece)],
        axis=0,
    )
    grams = lax.psum(terms, "space")
    grams = grams * scale
    offset = lax.axis_index("col") * ncol
    row_ids = lax.broadcasted_iota(jnp.int32, (ncol, total_cols), 0)
    col_ids = lax.broadcasted_iota(jnp.int32, (ncol, total_cols), 1)
    on_diag = (col_ids == row_ids + offset).astype(jnp.float32)
    diag_a = jnp.sum(grams[0] * on_diag, axis=1)
    diag_b = jnp.sum(grams[1] * on_diag, axis=1)
    theta = diag_a / diag_b
    residual = image - theta[:, None, None, None, None] * mass_image
    return (residual, grams[0], grams[1], grams[2])


def solution(mesh):
    in_specs = (
        P("col", None, "space", None, None),
        P("space", None, None),
        P(),
        P(None, "space", None, None),
    )
    out_specs = (
        P("col", None, "space", None, None),
        P("col", None),
        P("col", None),
        P("col", None),
    )
    return jax.shard_map(shards, mesh=mesh, in_specs=in_specs, out_specs=out_specs, check_vma=False)
```

profile of v0, /device:TPU:8, one launch (start us, length us, event | category | flops | bytes accessed | tf_op | source)
XLA Modules:
  0.0 804.3 jit_solution(13511130568080091090)
XLA Ops:
  7.2 0.9 convert_element_type.16
  8.1 9.3 %fusion.29 = (f32[48,3,4,16,128]{4,0,3,2,1:T(8,128)}, f32[48,3,4,16,128]{4,0,3,2,1:T(8,128)}) fusion(f32[48,3,4,16,128]{4,3,2,1,0:T(8,128)} %param.4, f32[3,4,16,128]{3,2,1,0:T(8,128)S(1)} %convert_element_type.16), kind=kLoop, calls=%fused_computation.50 | loop fusion | flops 1179648 | bytes 14254080 | tf_op args[0]
  17.5 2.0 fusion.30
  19.5 3.5 collective-permute-start.1
  23.0 4.7 collective-permute-start
  27.8 23.6 %collective-permute-done.1 = f32[48,3,1,16,128]{4,0,3,2,1:T(8,128)S(1)} collective-permute-done((f32[48,3,1,16,128]{4,0,3,2,1:T(8,128)S(1)}, f32[48,3,1,16,128]{4,0,3,2,1:T(8,128)S(1)}, u32[]{:S(2)}, u32[]{:S(2)}) %collective-permute-start.1) | collective-permute-done | bytes 1179680 | tf_op jit(solution)/shard_map/ppermute | solution.py:15
  51.7 0.6 slice.144
  52.5 1.1 fusion.12
  53.8 0.6 slice.147
  54.3 0.5 subtract_subtract_fusion
  55.4 1.3 fusion.19
  56.7 1.2 copy-done.2
  57.9 2.8 maximum_multiply_fusion
  60.7 0.6 copy-done.5
  61.3 0.7 fusion.31
  62.0 4.9 select_add_fusion
  67.0 13.2 %convolution_bitcast_fusion = f32[1,48,96]{2,1,0:T(8,128)S(1)} fusion(f32[48,3,4,16,128]{4,0,3,2,1:T(8,128)} %maximum_multiply_fusion, f32[96,3,4,16,128]{4,0,3,2,1:T(8,128)} %all-gather.3.cloned.1.call-done), kind=kOutput, calls=%fused_computation.36 | convolution fusion | flops 1358954496 | bytes 14174208 | tf_op jit(solution)/shard_map/dot_general | solution.py:60
  80.2 13.7 %fusion.20 = f32[1,48,96]{2,1,0:T(8,128)S(1)} fusion(f32[96,3,4,16,128]{4,0,3,2,1:T(8,128)S(1)} %copy-done.1, f32[3,4,16,128]{3,2,1,0:T(8,128)S(1)} %get-tuple-element.25, f32[48,3,4,16,128]{4,3,2,1,0:T(8,128)} %param.4), kind=kOutput, calls=%fused_computation.34 | convolution fusion | flops 1360134144 | bytes 14272512 | tf_op jit(solution)/shard_map/dot_general | solution.py:60
  94.4 13.0 %fusion.23 = f32[1,48,96]{2,1,0:T(8,128)S(1)} fusion(f32[96,3,4,16,128]{4,0,3,2,1:T(8,128)} %all-gather.5.cloned.1.call-done, f32[48,3,4,16,128]{4,0,3,2,1:T(8,128)} %maximum_multiply_fusion, f32[3,4,16,128]{3,2,1,0:T(8,128)S(1)} %get-tuple-element.26), kind=kOutput, calls=%fused_computation.35 | convolution fusion | flops 1360134144 | bytes 14272512 | tf_op jit(solution)/shard_map/dot_general | solution.py:60
  107.5 679.4 %psum.7 = f32[3,48,96]{2,1,0:T(8,128)S(1)} all-reduce(f32[3,48,96]{2,1,0:T(8,128)S(1)} %pad_maximum_fusion.2), channel_id=1, replica_groups=mesh['space'=128,'col'=2] {'space'}, use_global_device_ids=true, to_apply=%region_0.1 | all-reduce | flops 13824 | bytes 110592 | tf_op jit(solution)/shard_map/psum | solution.py:87
  786.9 0.6 slice_bitcast_fusion
  787.5 0.7 select_reduce_fusion
  788.2 5.6 multiply_subtract_fusion
  793.9 3.6 copy.11
  (29 shorter events, 1.9 us)
Async XLA Ops:
  7.2 59.8 %all-gather.3.cloned.1.call-start = ((), (), s32[]{:S(2)}) async-start(), calls=%async_computation | async-start | bytes 14155776 | tf_op jit(solution)/shard_map/all_gather | solution.py:81
  17.4 77.0 %all-gather.5.cloned.1.call-start = ((), (), s32[]{:S(2)}) async-start(), calls=%async_computation.1 | async-start | bytes 14155776 | tf_op jit(solution)/shard_map/all_gather | solution.py:82
  17.5 33.9 %copy-start = (f32[48,3,4,16,128]{4,0,3,2,1:T(8,128)S(1)}, f32[48,3,4,16,128]{4,0,3,2,1:T(8,128)}, u32[]{:S(2)}) copy-start(f32[48,3,4,16,128]{4,0,3,2,1:T(8,128)} %get-tuple-element.19) | copy-start | bytes 14155780
  19.5 31.8 %collective-permute-start.1 = (f32[48,3,1,16,128]{4,0,3,2,1:T(8,128)S(1)}, f32[48,3,1,16,128]{4,0,3,2,1:T(8,128)S(1)}, u32[]{:S(2)}, u32[]{:S(2)}) collective-permute-start(f32[48,3,1,16,128]{4,0,3,2,1:T(8,128)S(1)} %get-tuple-element.20), channel_id=1, source_target_pairs={{0,2},{2,4},{4,6},{6,8},{8,10},{10,12},{12,14},{14,16},{16,18},{18... | collective-permute-start | bytes 3538952 | tf_op jit(solution)/shard_map/ppermute | solution.py:15
  23.0 29.5 %collective-permute-start = (f32[48,3,1,16,128]{4,0,3,2,1:T(8,128)S(1)}, f32[48,3,1,16,128]{4,0,3,2,1:T(8,128)S(1)}, u32[]{:S(2)}, u32[]{:S(2)}) collective-permute-start(f32[48,3,1,16,128]{4,0,3,2,1:T(8,128)S(1)} %get-tuple-element.21), channel_id=1, source_target_pairs={{2,0},{4,2},{6,4},{8,6},{10,8},{12,10},{14,12},{16,14},{18,16},{20... | collective-permute-start | bytes 3538952 | tf_op jit(solution)/shard_map/ppermute | solution.py:17
  56.7 1.2 copy-start.2
  60.7 0.7 copy-start.5
  60.7 1.3 copy-start.4
  60.7 6.2 copy-start.3
  67.0 13.2 %copy-start.1 = (f32[96,3,4,16,128]{4,0,3,2,1:T(8,128)S(1)}, f32[96,3,4,16,128]{4,0,3,2,1:T(8,128)}, u32[]{:S(2)}) copy-start(f32[96,3,4,16,128]{4,0,3,2,1:T(8,128)} %all-gather.3.cloned.1.call-done) | copy-start | bytes 28311556
Sparse Core Ops, SparseCore 0:
  17.5 30.0 all-gather.2
  60.8 33.5 all-gather.4
where the time goes:
time: 817 us; the launch traced here: 804 us
  blocking collectives  679 us (83%)
  matrix products  39.9 us (5%)
  other arithmetic  27.4 us (3%)
  waiting for transfers between devices  24.3 us (3%)
  between operations  14.3 us (2%)
  local copies, waits for them, and re-layouts  10.6 us (1%)
  starting transfers between devices  8.34 us (1%)
    psum x1, blocking collectives, shards(): grams = lax.psum(terms, 'space')  679 us
    dot_general x3, matrix products, inner(): jnp.dot(left.reshape(left.shape[0], -1), right.reshape(right.shape[0], -1...  39.9 us
    ppermute x1, waiting for transfers between devices, with_halo(): lax.ppermute(tail, axis, [(i, (i + 1) % count) for i in range(ends)])  23.6 us
  transfers between devices with their start and end apart: 4, of which 3 were waited for; matrix products, arithmetic and copies ran while one was open for 5% of the time, Pallas kernels for 0%

commit v1 on v0

v1 whole, which is shorter than its diff:
```python
import functools

import jax
import jax.numpy as jnp
from jax import lax
from jax.experimental import pallas as pl
from jax.experimental.pallas import tpu as pltpu
from jax.sharding import PartitionSpec as P

MIB = 1 << 20
GRIDS = {128: (8, 4, 4), 8: (2, 2, 2)}
F32 = jnp.float32
BF16 = jnp.bfloat16
NT = (((1,), (1,)), ((), ()))


def forward(field, axis):
    size = field.shape[axis]
    ahead = pltpu.roll(field, size - 1, axis)
    at = lax.broadcasted_iota(jnp.int32, field.shape, axis)
    return jnp.where(at == size - 1, 0.0, ahead) - field


def backward(field, axis):
    size = field.shape[axis]
    behind = pltpu.roll(field, 1, axis)
    at = lax.broadcasted_iota(jnp.int32, field.shape, axis)
    return jnp.where(at == 0, 0.0, behind) - field


def lookup(material, table_ref):
    eps = jnp.zeros(material.shape, F32)
    for index in range(table_ref.shape[0]):
        eps = jnp.where(material == index, table_ref[index], eps)
    return eps


def split(value):
    high = value.astype(BF16)
    return high, (value - high.astype(F32)).astype(BF16)


def edges_kernel(first_ref, last_ref, keep_first_ref, keep_last_ref, one_ref, two_ref):
    core = lax.axis_index("col")
    kf = keep_first_ref[...].astype(F32)
    kl = keep_last_ref[...].astype(F32)
    down0 = first_ref[:, 0, 0] * kf[0, 0]
    down1 = first_ref[:, 1, 0] * kf[1, 0]
    ex = last_ref[:, 0, 0] * kl[0, 0]
    ey = last_ref[:, 1, 0] * kl[1, 0]
    ez = last_ref[:, 2, 0] * kl[2, 0]
    up0 = ex + forward(ez, 2)
    up1 = ey + forward(ez, 1)
    swap = core == 1
    one_ref[:, 0] = jnp.where(swap, down0, up0)
    one_ref[:, 1] = jnp.where(swap, down1, up1)
    two_ref[:, 0] = jnp.where(swap, up0, down0)
    two_ref[:, 1] = jnp.where(swap, up1, down1)


def edges(block, mask, chunk=8):
    ncol, _, nz, ny, nx = block.shape
    shape = jax.ShapeDtypeStruct((ncol, 2, ny, nx), F32)
    return pl.pallas_call(
        edges_kernel,
        grid=(ncol // chunk,),
        out_shape=(shape, shape),
        in_specs=[
            pl.BlockSpec((chunk, 3, 1, ny, nx), lambda i: (i, 0, 0, 0, 0)),
            pl.BlockSpec((chunk, 3, 1, ny, nx), lambda i: (i, 0, nz - 1, 0, 0)),
            pl.BlockSpec((3, 1, ny, nx), lambda i: (0, 0, 0, 0)),
            pl.BlockSpec((3, 1, ny, nx), lambda i: (0, nz - 1, 0, 0)),
        ],
        out_specs=[pl.BlockSpec((chunk, 2, ny, nx), lambda i: (i, 0, 0, 0))] * 2,
        compiler_params=pltpu.CompilerParams(vmem_limit_bytes=32 * MIB),
    )(block, block, mask, mask)


CHUNK = 16
LANES = 512


def store_rows(tmp_ref, dst_ref, row, ny, nx):
    per = LANES // nx
    for comp in range(3):
        for y in range(ny):
            rows = tmp_ref[comp, pl.ds(y, CHUNK, stride=ny), :]
            high, low = split(rows)
            at = (comp * ny + y) // per
            lanes = pl.ds(((comp * ny + y) % per) * nx, nx)
            dst_ref[at, pl.ds(row, CHUNK), lanes] = high
            dst_ref[at, pl.ds(128 + row, CHUNK), lanes] = low


def dots(left_ref, right_ref, acc_ref, steps, ncols, low):
    def step(k, carry):
        right = right_ref[k]
        acc = lax.dot_general(left_ref[k, 0:ncols, :], right, NT, preferred_element_type=F32)
        if low:
            acc += lax.dot_general(left_ref[k, 128 : 128 + ncols, :], right, NT, preferred_element_type=F32)
        acc_ref[...] += acc
        return carry

    lax.fori_loop(0, steps, step, 0)


def middle_kernel(
    own_ref, other_ref, mask_ref, material_ref, table_ref,
    near_own_ref, near_other_ref, edge_u_ref, acc_a_ref, acc_b_ref, acc_f_ref,
    keep_ref, root_ref, scale_ref, tmp_v, tmp_u, tmp_e, mid_u, mid_v,
):
    core = lax.axis_index("col")
    upper = core == 1
    step = pl.program_id(0)
    _, nz, ny, nx = mask_ref.shape
    ncols = 2 * CHUNK * pl.num_programs(0)
    half = near_own_ref.shape[0] * 3

    @pl.when(step == 0)
    def _():
        keep = mask_ref[...].astype(F32)
        root = jnp.sqrt(lookup(material_ref[...], table_ref))
        keep_ref[...] = keep
        root_ref[...] = root
        scale_ref[...] = keep / root[None]
        acc_a_ref[...] = jnp.zeros_like(acc_a_ref)
        acc_b_ref[...] = jnp.zeros_like(acc_b_ref)
        acc_f_ref[...] = jnp.zeros_like(acc_f_ref)

    def column(src_ref, near_ref, j):
        def e(comp, layer):
            return src_ref[j, comp, layer] * keep_ref[comp, layer]

        def dx(f):
            return forward(f, 1)

        def dy(f):
            return forward(f, 0)

        def bx(f):
            return backward(f, 1)

        def by(f):
            return backward(f, 0)

        x0, y0, z0 = (e(comp, core) for comp in range(3))
        x1, y1, z1 = (e(comp, core + 1) for comp in range(3))
        x2, y2 = (e(comp, core + 2) for comp in range(2))
        h01x = dy(z0) - (y1 - y0)
        h01y = (x1 - x0) - dx(z0)
        h12x = dy(z1) - (y2 - y1)
        h12y = (x2 - x1) - dx(z1)
        h1z = dx(y1) - dy(x1)
        rows = pl.ds(pl.multiple_of(j * ny, ny), ny)
        mid = core + 1
        tmp_v[0, rows, :] = ((h01y - h12y) - by(h1z)) * scale_ref[0, mid]
        tmp_v[1, rows, :] = (bx(h1z) - (h01x - h12x)) * scale_ref[1, mid]
        tmp_v[2, rows, :] = (by(h12x) - bx(h12y)) * scale_ref[2, mid]
        root = root_ref[mid]
        tmp_u[0, rows, :] = x1 * root
        tmp_u[1, rows, :] = y1 * root
        tmp_u[2, rows, :] = z1 * root
        edge = 3 * core
        xb, yb, zb = (e(comp, edge) for comp in range(3))
        hbz = dx(yb) - dy(xb)
        lowx = jnp.where(upper, h12x, -yb)
        lowy = jnp.where(upper, h12y, xb)
        topx = jnp.where(upper, dy(zb) + yb, h01x)
        topy = jnp.where(upper, -xb - dx(zb), h01y)
        near_ref[j, 0] = ((lowy - topy) - by(hbz)) * scale_ref[0, edge]
        near_ref[j, 1] = (bx(hbz) - (lowx - topx)) * scale_ref[1, edge]
        near_ref[j, 2] = (by(topx) - bx(topy)) * scale_ref[2, edge]
        root = root_ref[edge]
        tmp_e[0, rows, :] = xb * root
        tmp_e[1, rows, :] = yb * root
        tmp_e[2, rows, :] = zb * root

    total = edge_u_ref.shape[0]
    for src_ref, near_ref, side in ((own_ref, near_own_ref, core), (other_ref, near_other_ref, 1 - core)):
        def body(j, carry, src_ref=src_ref, near_ref=near_ref):
            column(src_ref, near_ref, j)
            return carry

        lax.fori_loop(0, CHUNK, body, 0)
        row = pl.multiple_of(side * half + step * CHUNK, CHUNK)
        store_rows(tmp_v, mid_v, row, ny, nx)
        store_rows(tmp_u, mid_u, row, ny, nx)
        store_rows(tmp_e, edge_u_ref, row, ny, nx)

    @pl.when(step == pl.num_programs(0) - 1)
    def _():
        n = 2 * half
        dots(mid_u, mid_v, acc_a_ref, total, n, True)
        dots(mid_v, mid_v, acc_f_ref, total, n, False)
        dots(mid_u, mid_u, acc_b_ref, total, n, False)
        dots(edge_u_ref, edge_u_ref, acc_b_ref, total, n, False)


def middle(block, other, mask, material, table):
    ncol, _, nz, ny, nx = block.shape
    total = 3 * ny * nx // LANES
    near = jax.ShapeDtypeStruct((ncol, 3, ny, nx), F32)
    acc = jax.ShapeDtypeStruct((2 * ncol, 256), F32)
    whole = lambda *shape: pl.BlockSpec(shape, lambda i: (0,) * len(shape))
    block_spec = pl.BlockSpec((CHUNK, 3, nz, ny, nx), lambda i: (i, 0, 0, 0, 0))
    near_spec = pl.BlockSpec((CHUNK, 3, ny, nx), lambda i: (i, 0, 0, 0))
    return pl.pallas_call(
        middle_kernel,
        grid=(ncol // CHUNK,),
        out_shape=(near, near, jax.ShapeDtypeStruct((total, 256, LANES), BF16), acc, acc, acc),
        in_specs=[
            block_spec, block_spec,
            whole(3, nz, ny, nx), whole(nz, ny, nx),
            pl.BlockSpec(memory_space=pltpu.SMEM),
        ],
        out_specs=[near_spec, near_spec, whole(total, 256, LANES)] + [whole(2 * ncol, 256)] * 3,
        scratch_shapes=[
            pltpu.VMEM((3, nz, ny, nx), F32),
            pltpu.VMEM((nz, ny, nx), F32),
            pltpu.VMEM((3, nz, ny, nx), F32),
            pltpu.VMEM((3, CHUNK * ny, nx), F32),
            pltpu.VMEM((3, CHUNK * ny, nx), F32),
            pltpu.VMEM((3, CHUNK * ny, nx), F32),
            pltpu.VMEM((total, 256, LANES), BF16),
            pltpu.VMEM((total, 256, LANES), BF16),
        ],
        compiler_params=pltpu.CompilerParams(vmem_limit_bytes=48 * MIB),
        cost_estimate=pl.CostEstimate(flops=2 * 10**9, bytes_accessed=16 * 10**6, transcendentals=0),
    )(block, other, mask, material, table)


def finish_kernel(
    near_own_ref, near_other_ref, halo_own_ref, halo_other_ref, mask_ref, material_ref, table_ref,
    edge_u_ref, acc_a_ref, acc_b_ref, acc_f_ref,
    keep_rows_ref, send_rows_ref,
    scale_ref, tmp_v, edge_v, sum_a, sum_f,
):
    core = lax.axis_index("col")
    step = pl.program_id(0)
    ny, nx = mask_ref.shape[2:]
    half = keep_rows_ref.shape[1]

    @pl.when(step == 0)
    def _():
        root = jnp.sqrt(lookup(material_ref[3 * core], table_ref))
        for comp in range(3):
            scale_ref[comp] = mask_ref[comp, 3 * core].astype(F32) / root
        sum_a[...] = acc_a_ref[...]
        sum_f[...] = acc_f_ref[...]

    weight = core.astype(F32)
    for near_ref, halo_ref, side in (
        (near_own_ref, halo_own_ref, core),
        (near_other_ref, halo_other_ref, 1 - core),
    ):
        def body(j, carry, near_ref=near_ref, halo_ref=halo_ref):
            h0 = halo_ref[j, 0]
            h1 = halo_ref[j, 1]
            rows = pl.ds(pl.multiple_of(j * ny, ny), ny)
            tmp_v[0, rows, :] = near_ref[j, 0] - h0 * scale_ref[0]
            tmp_v[1, rows, :] = near_ref[j, 1] - h1 * scale_ref[1]
            tmp_v[2, rows, :] = near_ref[j, 2] - (backward(h1, 0) + backward(h0, 1)) * (scale_ref[2] * weight)
            return carry

        lax.fori_loop(0, CHUNK, body, 0)
        store_rows(tmp_v, edge_v, pl.multiple_of(side * half + step * CHUNK, CHUNK), ny, nx)

    @pl.when(step == pl.num_programs(0) - 1)
    def _():
        n = 2 * half
        total = edge_v.shape[0]
        dots(edge_u_ref, edge_v, sum_a, total, n, True)
        dots(edge_v, edge_v, sum_f, total, n, False)
        sum_a[:, 0:n] = sum_a[:, 0:n] + sum_a[:, 128 : 128 + n]
        for ref, out in ((acc_b_ref, sum_a.at[:, 128:256]), (sum_f, sum_f.at[:, 0:128])):
            high = ref[:, 0:n]
            cross = ref[:, 128 : 128 + n]
            out[:, 0:n] = high + (cross + cross.T)
        own = pl.ds(pl.multiple_of(core * half, 8), half)
        its = pl.ds(pl.multiple_of((1 - core) * half, 8), half)
        for rows, out_ref in ((own, keep_rows_ref), (its, send_rows_ref)):
            out_ref[0] = sum_a[rows, 0:n]
            out_ref[1] = sum_a[rows, 128 : 128 + n]
            out_ref[2] = sum_f[rows, 0:n]


def finish(near_own, near_other, halo_own, halo_other, mask, material, table, edge_u, accs):
    ncol, _, ny, nx = near_own.shape
    nz = mask.shape[1]
    total = edge_u.shape[0]
    rows = jax.ShapeDtypeStruct((3, ncol, 2 * ncol), F32)
    whole = lambda *shape: pl.BlockSpec(shape, lambda i: (0,) * len(shape))
    near_spec = pl.BlockSpec((CHUNK, 3, ny, nx), lambda i: (i, 0, 0, 0))
    halo_spec = pl.BlockSpec((CHUNK, 2, ny, nx), lambda i: (i, 0, 0, 0))
    return pl.pallas_call(
        finish_kernel,
        grid=(ncol // CHUNK,),
        out_shape=(rows, rows),
        in_specs=[
            near_spec, near_spec, halo_spec, halo_spec,
            whole(3, nz, ny, nx), whole(nz, ny, nx),
            pl.BlockSpec(memory_space=pltpu.SMEM),
            whole(total, 256, LANES),
        ] + [whole(2 * ncol, 256)] * 3,
        out_specs=[whole(3, ncol, 2 * ncol)] * 2,
        scratch_shapes=[
            pltpu.VMEM((3, ny, nx), F32),
            pltpu.VMEM((3, CHUNK * ny, nx), F32),
            pltpu.VMEM((total, 256, LANES), BF16),
            pltpu.VMEM((2 * ncol, 256), F32),
            pltpu.VMEM((2 * ncol, 256), F32),
        ],
        compiler_params=pltpu.CompilerParams(vmem_limit_bytes=40 * MIB),
    )(near_own, near_other, halo_own, halo_other, mask, material, table, edge_u, *accs)


def image_kernel(block_ref, one_ref, two_ref, mask_ref, image_ref, keep_ref):
    core = lax.axis_index("col")
    upper = core == 1
    _, nz, ny, nx = mask_ref.shape

    @pl.when(pl.program_id(0) == 0)
    def _():
        keep_ref[...] = mask_ref[...].astype(F32)

    def body(j, carry):
        def e(comp, layer):
            return block_ref[j, comp, layer] * keep_ref[comp, layer]

        one0, one1, two0, two1 = one_ref[j, 0], one_ref[j, 1], two_ref[j, 0], two_ref[j, 1]
        x, y, z = (e(comp, 0) for comp in range(3))
        lowy = x - jnp.where(upper, two0, one0)
        lowx = jnp.where(upper, two1, one1) - y
        for layer in range(nz):
            if layer + 1 < nz:
                xn, yn, zn = (e(comp, layer + 1) for comp in range(3))
            else:
                xn, yn, zn = jnp.where(upper, one0, two0), jnp.where(upper, one1, two1), None
            topx = forward(z, 0) - (yn - y)
            topy = (xn - x) - forward(z, 1)
            hz = forward(y, 1) - forward(x, 0)
            image_ref[j, 0, layer] = ((lowy - topy) - backward(hz, 0)) * keep_ref[0, layer]
            image_ref[j, 1, layer] = (backward(hz, 1) - (lowx - topx)) * keep_ref[1, layer]
            image_ref[j, 2, layer] = (backward(topx, 0) - backward(topy, 1)) * keep_ref[2, layer]
            x, y, z, lowx, lowy = xn, yn, zn, topx, topy
        return carry

    lax.fori_loop(0, block_ref.shape[0], body, 0)


def image_of(block, one, two, mask, chunk=8):
    ncol, _, nz, ny, nx = block.shape
    block_spec = pl.BlockSpec((chunk, 3, nz, ny, nx), lambda i: (i, 0, 0, 0, 0))
    halo_spec = pl.BlockSpec((chunk, 2, ny, nx), lambda i: (i, 0, 0, 0))
    return pl.pallas_call(
        image_kernel,
        grid=(ncol // chunk,),
        out_shape=jax.ShapeDtypeStruct(block.shape, F32),
        in_specs=[
            block_spec, halo_spec, halo_spec,
            pl.BlockSpec((3, nz, ny, nx), lambda i: (0, 0, 0, 0)),
        ],
        out_specs=block_spec,
        scratch_shapes=[pltpu.VMEM((3, nz, ny, nx), F32)],
        compiler_params=pltpu.CompilerParams(vmem_limit_bytes=32 * MIB),
        cost_estimate=pl.CostEstimate(flops=10**9, bytes_accessed=11 * 10**6, transcendentals=0),
    )(block, one, two, mask)


def residual_kernel(
    scale, grams_ref, block_ref, image_ref, mask_ref, material_ref, table_ref,
    out_ref, ga_ref, gb_ref, gf_ref, mass_ref, theta_ref,
):
    core = lax.axis_index("col")
    step = pl.program_id(0)
    half, total = ga_ref.shape
    chunk = block_ref.shape[0]

    @pl.when(step == 0)
    def _():
        mass_ref[...] = lookup(material_ref[...], table_ref)[None] * mask_ref[...].astype(F32)
        ga = grams_ref[0] * scale
        gb = grams_ref[1] * scale
        ga_ref[...] = ga
        gb_ref[...] = gb
        gf_ref[...] = grams_ref[2] * scale
        rows = lax.broadcasted_iota(jnp.int32, (half, total), 0)
        cols = lax.broadcasted_iota(jnp.int32, (half, total), 1)
        here = cols == rows + core * half
        diag_a = jnp.sum(jnp.where(here, ga, 0.0), axis=1, keepdims=True)
        diag_b = jnp.sum(jnp.where(here, gb, 0.0), axis=1, keepdims=True)
        theta_ref[...] = jnp.broadcast_to(diag_a / diag_b, theta_ref.shape)

    def body(j, carry):
        theta = theta_ref[pl.ds(step * chunk + j, 1), :]
        out_ref[j] = image_ref[j] - theta[None, None] * (mass_ref[...] * block_ref[j])
        return carry

    lax.fori_loop(0, chunk, body, 0)


def residual_of(grams, block, image, mask, material, table, scale, chunk=8):
    ncol, _, nz, ny, nx = block.shape
    whole = lambda *shape: pl.BlockSpec(shape, lambda i: (0,) * len(shape))
    block_spec = pl.BlockSpec((chunk, 3, nz, ny, nx), lambda i: (i, 0, 0, 0, 0))
    gram = jax.ShapeDtypeStruct((ncol, 2 * ncol), F32)
    return pl.pallas_call(
        functools.partial(residual_kernel, scale),
        grid=(ncol // chunk,),
        out_shape=(jax.ShapeDtypeStruct(block.shape, F32), gram, gram, gram),
        in_specs=[
            whole(3, ncol, 2 * ncol), block_spec, block_spec,
            whole(3, nz, ny, nx), whole(nz, ny, nx),
            pl.BlockSpec(memory_space=pltpu.SMEM),
        ],
        out_specs=[block_spec] + [whole(ncol, 2 * ncol)] * 3,
        scratch_shapes=[pltpu.VMEM((3, nz, ny, nx), F32), pltpu.VMEM((ncol, nx), F32)],
        compiler_params=pltpu.CompilerParams(vmem_limit_bytes=32 * MIB),
        cost_estimate=pl.CostEstimate(flops=2 * 10**7, bytes_accessed=15 * 10**6, transcendentals=0),
    )(grams, block, image, mask, material, table)


def pair_rounds(slabs):
    nz, ny, nx = GRIDS[slabs]
    rounds = []
    for size, stride in ((nx, 1), (ny, nx), (nz, nx * ny)):
        for flip in {2: (1,), 4: (1, 3), 8: (1, 2, 7)}[size]:
            partner = lambda i: i + (((i // stride % size) ^ flip) - i // stride % size) * stride
            rounds.append([(i, partner(i)) for i in range(slabs)])
    return rounds


def shards(block, material, table, mask):
    slabs = lax.axis_size("space")
    ncol, _, nz, ny, nx = block.shape
    scale = 1.0 / (3.0 * nz * slabs * ny * nx)
    swap = [(0, 1), (1, 0)]
    other = lax.ppermute(block, "col", swap)
    one, two = edges(block, mask)
    ups = [(2 * i, 2 * i + 2) for i in range(slabs - 1)] + [(2 * i + 3, 2 * i + 1) for i in range(slabs - 1)]
    crossed = [(2 * i + 1, 2 * i + 2) for i in range(slabs - 1)] + [(2 * i + 2, 2 * i + 1) for i in range(slabs - 1)]
    halo_own = lax.ppermute(one, ("space", "col"), ups)
    halo_other = lax.ppermute(two, ("space", "col"), crossed)
    near_own, near_other, edge_u, *accs = middle(block, other, mask, material, table)
    keep_rows, send_rows = finish(near_own, near_other, halo_own, halo_other, mask, material, table, edge_u, accs)
    grams = keep_rows + lax.ppermute(send_rows, "col", swap)
    halo_far = lax.ppermute(halo_other, "col", swap)
    image = image_of(block, halo_own, halo_far, mask)
    for pairs in pair_rounds(slabs):
        grams = grams + lax.ppermute(grams, "space", pairs)
    return residual_of(grams, block, image, mask, material, table, scale)


def solution(mesh):
    in_specs = (
        P("col", None, "space", None, None),
        P("space", None, None),
        P(),
        P(None, "space", None, None),
    )
    out_specs = (
        P("col", None, "space", None, None),
        P("col", None),
        P("col", None),
        P("col", None),
    )
    return jax.shard_map(shards, mesh=mesh, in_specs=in_specs, out_specs=out_specs, check_vma=False)
```

time: 817 us -> 127 us (0.16)
  the two profiles are of different devices: /device:TPU:8 before, /device:TPU:62 now
where the time goes in v1:
time: 127 us
  Pallas kernels  59.9 us (47%)
  waiting for transfers between devices  36.5 us (29%)
  starting transfers between devices  26.5 us (21%)
  local copies, waits for them, and re-layouts  3.25 us (3%)
    pallas_call x1, Pallas kernels, middle(): pl.pallas_call(middle_kernel, grid=(ncol // CHUNK,), out_shape=(near, nea...  31.4 us
    ppermute x7, waiting for transfers between devices, shards(): grams = grams + lax.ppermute(grams, 'space', pairs)  26.9 us
    pallas_call x1, Pallas kernels, finish(): pl.pallas_call(finish_kernel, grid=(ncol // CHUNK,), out_shape=(rows, row...  15.3 us
    ppermute x7, starting transfers between devices, shards(): grams = grams + lax.ppermute(grams, 'space', pairs)  10.7 us
    ppermute x1, waiting for transfers between devices, shards(): halo_other = lax.ppermute(two, ('space', 'col'), crossed)  8.35 us
    pallas_call x1, Pallas kernels, image_of(): pl.pallas_call(image_kernel, grid=(ncol // chunk,), out_shape=jax.ShapeDt...  8.2 us
    ppermute x1, starting transfers between devices, shards(): halo_own = lax.ppermute(one, ('space', 'col'), ups)  7.32 us
    ppermute x1, starting transfers between devices, shards(): halo_far = lax.ppermute(halo_other, 'col', swap)  5.4 us
  transfers between devices with their start and end apart: 12, of which 8 were waited for; matrix products, arithmetic and copies ran while one was open for 0% of the time, Pallas kernels for 44%

profile of v1, /device:TPU:62, one launch (start us, length us, event | category | flops | bytes accessed | tf_op | source)
XLA Modules:
  0.0 126.9 jit_solution(4374590106147436362)
XLA Ops:
  0.6 0.1 collective-permute-start
  0.7 2.3 %copy-done = f32[48,3,4,16,128]{4,3,2,1,0:T(8,128)S(1)} copy-done((f32[48,3,4,16,128]{4,3,2,1,0:T(8,128)S(1)}, f32[48,3,4,16,128]{4,3,2,1,0:T(8,128)}, u32[]{:S(2)}) %copy-start) | copy-done | bytes 4718616
  3.1 0.9 copy-done.1
  4.0 0.9 shard_map.76
  4.8 2.8 %collective-permute-start.2 = (f32[48,2,16,128]{3,2,1,0:T(8,128)S(1)}, f32[48,2,16,128]{3,2,1,0:T(8,128)S(1)}, u32[]{:S(2)}, u32[]{:S(2)}) collective-permute-start(f32[48,2,16,128]{3,2,1,0:T(8,128)S(1)} %get-tuple-element.17), channel_id=1, source_target_pairs={{1,2},{3,4},{5,6},{7,8},{9,10},{11,12},{13,14},{15,16},{17,18},{19... | collective-permute-start | bytes 2359304 | tf_op jit(solution)/shard_map/ppermute | solution.py:443
  7.7 7.3 %collective-permute-start.1 = (f32[48,2,16,128]{3,2,1,0:T(8,128)S(1)}, f32[48,2,16,128]{3,2,1,0:T(8,128)S(1)}, u32[]{:S(2)}, u32[]{:S(2)}) collective-permute-start(f32[48,2,16,128]{3,2,1,0:T(8,128)S(1)} %get-tuple-element.16), channel_id=1, source_target_pairs={{0,2},{2,4},{4,6},{6,8},{8,10},{10,12},{12,14},{14,16},{16,18},{18... | collective-permute-start | bytes 2359304 | tf_op jit(solution)/shard_map/ppermute | solution.py:442
  15.0 8.3 %collective-permute-done.2.halo_other_ref = f32[48,2,16,128]{3,2,1,0:T(8,128)S(1)} collective-permute-done((f32[48,2,16,128]{3,2,1,0:T(8,128)S(1)}, f32[48,2,16,128]{3,2,1,0:T(8,128)S(1)}, u32[]{:S(2)}, u32[]{:S(2)}) %collective-permute-start.2) | collective-permute-done | bytes 786464 | tf_op jit(solution)/shard_map/ppermute | solution.py:443
  23.4 5.4 %collective-permute-start.11 = (f32[48,2,16,128]{3,2,1,0:T(8,128)S(1)}, f32[48,2,16,128]{3,2,1,0:T(8,128)S(1)}, u32[]{:S(2)}, u32[]{:S(2)}) collective-permute-start(f32[48,2,16,128]{3,2,1,0:T(8,128)S(1)} %collective-permute-done.2.halo_other_ref), channel_id=1, source_target_pairs={{0,1},{1,0},{2,3},{3,2},{4,5},{5,4},{6,7},{7,6},{8,9},{9,8},{10,11... | collective-permute-start | bytes 2359304 | tf_op jit(solution)/shard_map/ppermute | solution.py:447
  28.8 31.4 %shard_map.75 = (f32[48,3,16,128]{3,2,1,0:T(8,128)S(1)}, f32[48,3,16,128]{3,2,1,0:T(8,128)S(1)}, bf16[12,256,512]{2,1,0:T(8,128)(2,1)S(1)}, f32[96,256]{1,0:T(8,...) custom-call(f32[48,3,4,16,128]{4,3,2,1,0:T(8,128)} %block_ref.3, ...), custom_call_target="tpu_custom_call" | custom-call | flops 2000000000 | bytes 16000000 | tf_op jit(solution)/shard_map/pallas_call | solution.py:207
  60.2 15.3 %shard_map.77 = (f32[3,48,96]{2,1,0:T(8,128)S(1)}, f32[3,48,96]{2,1,0:T(8,128)S(1)}) custom-call(f32[48,3,16,128]{3,2,1,0:T(8,128)S(1)} %get-tuple-element.14.near_own_ref, f32[48,3,16,128]{3,2,1,0:T(8,128)S(1)} %get-tuple-element.15.near_other_ref, f32[48,2,16,128]{3,2,1,0:T(8,128)S(1)} %collective-permute-done.1.halo_own_ref.one_ref, ...), custom_call_target="tpu_custom_call" | custom-call | tf_op jit(solution)/shard_map/pallas_call | solution.py:295
  75.5 0.1 collective-permute-start.3
  75.6 1.2 collective-permute-done.3
  76.8 0.1 collective-permute-start.4
  76.9 4.3 %collective-permute-done.4 = f32[3,48,96]{2,1,0:T(8,128)S(1)} collective-permute-done((f32[3,48,96]{2,1,0:T(8,128)S(1)}, f32[3,48,96]{2,1,0:T(8,128)S(1)}, u32[]{:S(2)}, u32[]{:S(2)}) %collective-permute-start.4) | collective-permute-done | bytes 55328 | tf_op jit(solution)/shard_map/ppermute | solution.py:450
  81.4 5.5 %collective-permute-done.5 = f32[3,48,96]{2,1,0:T(8,128)S(1)} collective-permute-done((f32[3,48,96]{2,1,0:T(8,128)S(1)}, f32[3,48,96]{2,1,0:T(8,128)S(1)}, u32[]{:S(2)}, u32[]{:S(2)}) %collective-permute-start.5) | collective-permute-done | bytes 55328 | tf_op jit(solution)/shard_map/ppermute | solution.py:450
  87.1 4.3 %collective-permute-done.6 = f32[3,48,96]{2,1,0:T(8,128)S(1)} collective-permute-done((f32[3,48,96]{2,1,0:T(8,128)S(1)}, f32[3,48,96]{2,1,0:T(8,128)S(1)}, u32[]{:S(2)}, u32[]{:S(2)}) %collective-permute-start.6) | collective-permute-done | bytes 55328 | tf_op jit(solution)/shard_map/ppermute | solution.py:450
  91.5 5.5 %collective-permute-done.7 = f32[3,48,96]{2,1,0:T(8,128)S(1)} collective-permute-done((f32[3,48,96]{2,1,0:T(8,128)S(1)}, f32[3,48,96]{2,1,0:T(8,128)S(1)}, u32[]{:S(2)}, u32[]{:S(2)}) %collective-permute-start.7) | collective-permute-done | bytes 55328 | tf_op jit(solution)/shard_map/ppermute | solution.py:450
  97.1 0.2 collective-permute-start.8
  97.3 4.7 %collective-permute-done.8 = f32[3,48,96]{2,1,0:T(8,128)S(1)} collective-permute-done((f32[3,48,96]{2,1,0:T(8,128)S(1)}, f32[3,48,96]{2,1,0:T(8,128)S(1)}, u32[]{:S(2)}, u32[]{:S(2)}) %collective-permute-start.8) | collective-permute-done | bytes 55328 | tf_op jit(solution)/shard_map/ppermute | solution.py:450
  102.0 3.2 %collective-permute-start.9 = (f32[3,48,96]{2,1,0:T(8,128)S(1)}, f32[3,48,96]{2,1,0:T(8,128)S(1)}, u32[]{:S(2)}, u32[]{:S(2)}) collective-permute-start(f32[3,48,96]{2,1,0:T(8,128)S(1)} %add.29), channel_id=1, source_target_pairs={{0,64},{2,66},{4,68},{6,70},{8,72},{10,74},{12,76},{14,78},{16,80}... | collective-permute-start | bytes 165896 | tf_op jit(solution)/shard_map/ppermute | solution.py:450
  105.2 2.3 %collective-permute-done.9 = f32[3,48,96]{2,1,0:T(8,128)S(1)} collective-permute-done((f32[3,48,96]{2,1,0:T(8,128)S(1)}, f32[3,48,96]{2,1,0:T(8,128)S(1)}, u32[]{:S(2)}, u32[]{:S(2)}) %collective-permute-start.9) | collective-permute-done | bytes 55328 | tf_op jit(solution)/shard_map/ppermute | solution.py:450
  107.5 7.0 %collective-permute-start.10 = (f32[3,48,96]{2,1,0:T(8,128)S(1)}, f32[3,48,96]{2,1,0:T(8,128)S(1)}, u32[]{:S(2)}, u32[]{:S(2)}) collective-permute-start(f32[3,48,96]{2,1,0:T(8,128)S(1)} %add.30), channel_id=1, source_target_pairs={{0,224},{2,226},{4,228},{6,230},{8,232},{10,234},{12,236},{14,238}... | collective-permute-start | bytes 165896 | tf_op jit(solution)/shard_map/ppermute | solution.py:450
  114.5 8.2 %shard_map.78.image_ref = f32[48,3,4,16,128]{4,3,2,1,0:T(8,128)S(1)} custom-call(f32[48,3,4,16,128]{4,3,2,1,0:T(8,128)S(1)} %bitcast.1, f32[48,2,16,128]{3,2,1,0:T(8,128)S(1)} %collective-permute-done.1.halo_own_ref.one_ref, f32[48,2,16,128]{3,2,1,0:T(8,128)S(1)} %collective-permute-done.11.two_ref, s32[3,4,16,128]{3,2,1,0:T(8,128)S(1)} %copy-done.2), custom_call_target="tpu_custom_call" | custom-call | flops 1000000000 | bytes 11000000 | tf_op jit(solution)/shard_map/pallas_call | solution.py:355
  122.8 4.2 %shard_map.79 = (f32[48,3,4,16,128]{4,3,2,1,0:T(8,128)}, f32[48,96]{1,0:T(8,128)}, f32[48,96]{1,0:T(8,128)}, f32[48,96]{1,0:T(8,128)}) custom-call(f32[3,48,96]{2,1,0:T(8,128)S(1)} %add.31.grams_ref, f32[48,3,4,16,128]{4,3,2,1,0:T(8,128)S(1)} %bitcast.1, f32[48,3,4,16,128]{4,3,2,1,0:T(8,128)S(1)} %shard_map.78.image_ref, s32[3,4,16,128]{3,2,1,0:T(8,128)S(1)} %copy-done.2, ...), custom_call_target="tpu_custom_call" | custom-call | flops 20000000 | bytes 15000000 | tf_op jit(solution)/shard_map/pallas_call | solution.py:407
  (28 shorter events, 0.4 us)
Async XLA Ops:
  0.6 28.1 %collective-permute-start = (f32[48,3,4,16,128]{4,3,2,1,0:T(8,128)}, f32[48,3,4,16,128]{4,3,2,1,0:T(8,128)}, u32[]{:S(2)}, u32[]{:S(2)}) collective-permute-start(f32[48,3,4,16,128]{4,3,2,1,0:T(8,128)} %block_ref.3), channel_id=1, source_target_pairs={{0,1},{1,0},{2,3},{3,2},{4,5},{5,4},{6,7},{7,6},{8,9},{9,8},{10,11... | collective-permute-start | bytes 14155784 | tf_op jit(solution)/shard_map/ppermute | solution.py:438
  0.7 2.3 %copy-start = (f32[48,3,4,16,128]{4,3,2,1,0:T(8,128)S(1)}, f32[48,3,4,16,128]{4,3,2,1,0:T(8,128)}, u32[]{:S(2)}) copy-start(f32[48,3,4,16,128]{4,3,2,1,0:T(8,128)} %block_ref.3) | copy-start | bytes 14155780
  3.1 0.9 copy-start.1
  4.0 24.8 %copy-start.2 = (s32[3,4,16,128]{3,2,1,0:T(8,128)S(1)}, s32[3,4,16,128]{3,2,1,0:T(8,128)}, u32[]{:S(2)}) copy-start(s32[3,4,16,128]{3,2,1,0:T(8,128)} %mask_ref.7) | copy-start | bytes 294916
  4.0 24.8 %copy-start.3 = (s32[4,16,128]{2,1,0:T(8,128)S(1)}, s32[4,16,128]{2,1,0:T(8,128)}, u32[]{:S(2)}) copy-start(s32[4,16,128]{2,1,0:T(8,128)} %material_ref.5) | copy-start | bytes 98308
  4.0 24.8 %copy-start.4 = (f32[8]{0:T(128)S(1)}, f32[8]{0:T(128)}, u32[]{:S(2)}) copy-start(f32[8]{0:T(128)} %table_ref.5) | copy-start | bytes 100
  4.8 18.5 %collective-permute-start.2 = (f32[48,2,16,128]{3,2,1,0:T(8,128)S(1)}, f32[48,2,16,128]{3,2,1,0:T(8,128)S(1)}, u32[]{:S(2)}, u32[]{:S(2)}) collective-permute-start(f32[48,2,16,128]{3,2,1,0:T(8,128)S(1)} %get-tuple-element.17), channel_id=1, source_target_pairs={{1,2},{3,4},{5,6},{7,8},{9,10},{11,12},{13,14},{15,16},{17,18},{19... | collective-permute-start | bytes 2359304 | tf_op jit(solution)/shard_map/ppermute | solution.py:443
  7.7 52.5 %collective-permute-start.1 = (f32[48,2,16,128]{3,2,1,0:T(8,128)S(1)}, f32[48,2,16,128]{3,2,1,0:T(8,128)S(1)}, u32[]{:S(2)}, u32[]{:S(2)}) collective-permute-start(f32[48,2,16,128]{3,2,1,0:T(8,128)S(1)} %get-tuple-element.16), channel_id=1, source_target_pairs={{0,2},{2,4},{4,6},{6,8},{8,10},{10,12},{12,14},{14,16},{16,18},{18... | collective-permute-start | bytes 2359304 | tf_op jit(solution)/shard_map/ppermute | solution.py:442
  23.4 91.1 %collective-permute-start.11 = (f32[48,2,16,128]{3,2,1,0:T(8,128)S(1)}, f32[48,2,16,128]{3,2,1,0:T(8,128)S(1)}, u32[]{:S(2)}, u32[]{:S(2)}) collective-permute-start(f32[48,2,16,128]{3,2,1,0:T(8,128)S(1)} %collective-permute-done.2.halo_other_ref), channel_id=1, source_target_pairs={{0,1},{1,0},{2,3},{3,2},{4,5},{5,4},{6,7},{7,6},{8,9},{9,8},{10,11... | collective-permute-start | bytes 2359304 | tf_op jit(solution)/shard_map/ppermute | solution.py:447
  60.1 54.4 %slice-start = ((s8[4718592]{0:T(1024)(128)(4,1)}), s8[4194304]{0:T(1024)(128)(4,1)S(1)}, s32[]{:S(2)}) async-start(s8[4718592]{0:T(1024)(128)(4,1)} %bitcast), calls=%async_computation | async-start | bytes 8388608
  60.2 54.3 %slice-start.1 = ((s8[4718592]{0:T(1024)(128)(4,1)}), s8[524288]{0:T(1024)(128)(4,1)S(1)}, s32[]{:S(2)}) async-start(s8[4718592]{0:T(1024)(128)(4,1)} %bitcast), calls=%async_computation.1 | async-start | bytes 1048576
  75.5 1.4 %collective-permute-start.3 = (f32[3,48,96]{2,1,0:T(8,128)S(1)}, f32[3,48,96]{2,1,0:T(8,128)S(1)}, u32[]{:S(2)}, u32[]{:S(2)}) collective-permute-start(f32[3,48,96]{2,1,0:T(8,128)S(1)} %get-tuple-element.23), channel_id=1, source_target_pairs={{0,1},{1,0},{2,3},{3,2},{4,5},{5,4},{6,7},{7,6},{8,9},{9,8},{10,11... | collective-permute-start | bytes 165896 | tf_op jit(solution)/shard_map/ppermute | solution.py:446
  76.8 4.4 %collective-permute-start.4 = (f32[3,48,96]{2,1,0:T(8,128)S(1)}, f32[3,48,96]{2,1,0:T(8,128)S(1)}, u32[]{:S(2)}, u32[]{:S(2)}) collective-permute-start(f32[3,48,96]{2,1,0:T(8,128)S(1)} %add.24), channel_id=1, source_target_pairs={{0,2},{2,0},{4,6},{6,4},{8,10},{10,8},{12,14},{14,12},{16,18},{18,... | collective-permute-start | bytes 165896 | tf_op jit(solution)/shard_map/ppermute | solution.py:450
  81.3 5.7 %collective-permute-start.5 = (f32[3,48,96]{2,1,0:T(8,128)S(1)}, f32[3,48,96]{2,1,0:T(8,128)S(1)}, u32[]{:S(2)}, u32[]{:S(2)}) collective-permute-start(f32[3,48,96]{2,1,0:T(8,128)S(1)} %add.25), channel_id=1, source_target_pairs={{0,6},{2,4},{4,2},{6,0},{8,14},{10,12},{12,10},{14,8},{16,22},{18,... | collective-permute-start | bytes 165896 | tf_op jit(solution)/shard_map/ppermute | solution.py:450
  87.0 4.4 %collective-permute-start.6 = (f32[3,48,96]{2,1,0:T(8,128)S(1)}, f32[3,48,96]{2,1,0:T(8,128)S(1)}, u32[]{:S(2)}, u32[]{:S(2)}) collective-permute-start(f32[3,48,96]{2,1,0:T(8,128)S(1)} %add.26), channel_id=1, source_target_pairs={{0,8},{2,10},{4,12},{6,14},{8,0},{10,2},{12,4},{14,6},{16,24},{18,... | collective-permute-start | bytes 165896 | tf_op jit(solution)/shard_map/ppermute | solution.py:450
  91.4 5.7 %collective-permute-start.7 = (f32[3,48,96]{2,1,0:T(8,128)S(1)}, f32[3,48,96]{2,1,0:T(8,128)S(1)}, u32[]{:S(2)}, u32[]{:S(2)}) collective-permute-start(f32[3,48,96]{2,1,0:T(8,128)S(1)} %add.27), channel_id=1, source_target_pairs={{0,24},{2,26},{4,28},{6,30},{8,16},{10,18},{12,20},{14,22},{16,8},... | collective-permute-start | bytes 165896 | tf_op jit(solution)/shard_map/ppermute | solution.py:450
  97.1 4.9 %collective-permute-start.8 = (f32[3,48,96]{2,1,0:T(8,128)S(1)}, f32[3,48,96]{2,1,0:T(8,128)S(1)}, u32[]{:S(2)}, u32[]{:S(2)}) collective-permute-start(f32[3,48,96]{2,1,0:T(8,128)S(1)} %add.28), channel_id=1, source_target_pairs={{0,32},{2,34},{4,36},{6,38},{8,40},{10,42},{12,44},{14,46},{16,48}... | collective-permute-start | bytes 165896 | tf_op jit(solution)/shard_map/ppermute | solution.py:450
  102.0 5.5 %collective-permute-start.9 = (f32[3,48,96]{2,1,0:T(8,128)S(1)}, f32[3,48,96]{2,1,0:T(8,128)S(1)}, u32[]{:S(2)}, u32[]{:S(2)}) collective-permute-start(f32[3,48,96]{2,1,0:T(8,128)S(1)} %add.29), channel_id=1, source_target_pairs={{0,64},{2,66},{4,68},{6,70},{8,72},{10,74},{12,76},{14,78},{16,80}... | collective-permute-start | bytes 165896 | tf_op jit(solution)/shard_map/ppermute | solution.py:450
  107.5 15.2 %collective-permute-start.10 = (f32[3,48,96]{2,1,0:T(8,128)S(1)}, f32[3,48,96]{2,1,0:T(8,128)S(1)}, u32[]{:S(2)}, u32[]{:S(2)}) collective-permute-start(f32[3,48,96]{2,1,0:T(8,128)S(1)} %add.30), channel_id=1, source_target_pairs={{0,224},{2,226},{4,228},{6,230},{8,232},{10,234},{12,236},{14,238}... | collective-permute-start | bytes 165896 | tf_op jit(solution)/shard_map/ppermute | solution.py:450

commit v2 on v0

v2 whole, which is shorter than its diff:
```python
import functools

import jax
import jax.numpy as jnp
from jax import lax
from jax.experimental import pallas as pl
from jax.experimental.pallas import tpu as pltpu
from jax.sharding import PartitionSpec as P

MIB = 1 << 20
GRIDS = {128: (8, 4, 4), 8: (2, 2, 2)}
F32 = jnp.float32
BF16 = jnp.bfloat16
NT = (((1,), (1,)), ((), ()))
VMEM = pl.BlockSpec(memory_space=pltpu.VMEM)
SMEM = pl.BlockSpec(memory_space=pltpu.SMEM)
HBM = pl.BlockSpec(memory_space=pltpu.HBM)
GROUP = 16
LANES = 512


def lookup(material, table_ref):
    eps = jnp.zeros(material.shape, F32)
    for index in range(table_ref.shape[0]):
        eps = jnp.where(material == index, table_ref[index], eps)
    return eps


def split(value):
    high = value.astype(BF16)
    return high, (value - high.astype(F32)).astype(BF16)


def ahead_x(field):
    at = lax.broadcasted_iota(jnp.int32, field.shape, 1)
    size = field.shape[1]
    return jnp.where(at == size - 1, 0.0, pltpu.roll(field, size - 1, 1)) - field


def behind_x(field):
    at = lax.broadcasted_iota(jnp.int32, field.shape, 1)
    return jnp.where(at == 0, 0.0, pltpu.roll(field, 1, 1)) - field


def minus(left, right):
    return -right if left is None else left - right


def edges_kernel(block_ref, mask_ref, one_ref, two_ref, first_ref, last_ref, mask_first, mask_last, sems):
    ncol, _, nz, ny, nx = block_ref.shape
    copies = [
        pltpu.make_async_copy(mask_ref.at[0:2, 0], mask_first, sems.at[0]),
        pltpu.make_async_copy(mask_ref.at[:, nz - 1], mask_last, sems.at[1]),
        pltpu.make_async_copy(block_ref.at[:, 0:2, 0], first_ref, sems.at[2]),
        pltpu.make_async_copy(block_ref.at[:, :, nz - 1], last_ref, sems.at[3]),
    ]
    for copy in copies:
        copy.start()
    for copy in copies:
        copy.wait()
    swap = lax.axis_index("col") == 1
    first = first_ref.reshape(ncol * 2 * ny, nx)
    last = last_ref.reshape(ncol * 3 * ny, nx)

    def low(comp, y):
        keep = mask_first[comp, y : y + 1, :].astype(F32)
        return first[pl.ds(comp * ny + y, ncol, stride=2 * ny), :] * keep

    def high(comp, y):
        keep = mask_last[comp, y : y + 1, :].astype(F32)
        return last[pl.ds(comp * ny + y, ncol, stride=3 * ny), :] * keep

    ez = high(2, 0)
    for y in range(ny):
        ez_next = high(2, y + 1) if y + 1 < ny else None
        up0 = high(0, y) + ahead_x(ez)
        up1 = high(1, y) + minus(ez_next, ez)
        down0 = low(0, y)
        down1 = low(1, y)
        one_ref[0, y] = jnp.where(swap, down0, up0)
        one_ref[1, y] = jnp.where(swap, down1, up1)
        two_ref[0, y] = jnp.where(swap, up0, down0)
        two_ref[1, y] = jnp.where(swap, up1, down1)
        ez = ez_next


def edges(block, mask):
    ncol, _, nz, ny, nx = block.shape
    shape = jax.ShapeDtypeStruct((2, ny, ncol, nx), F32)
    return pl.pallas_call(
        edges_kernel,
        out_shape=(shape, shape),
        in_specs=[HBM, HBM],
        out_specs=[VMEM, VMEM],
        scratch_shapes=[
            pltpu.VMEM((ncol, 2, ny, nx), F32),
            pltpu.VMEM((ncol, 3, ny, nx), F32),
            pltpu.VMEM((2, ny, nx), jnp.int32),
            pltpu.VMEM((3, ny, nx), jnp.int32),
            pltpu.SemaphoreType.DMA((4,)),
        ],
        compiler_params=pltpu.CompilerParams(vmem_limit_bytes=61 * MIB),
    )(block, mask)


def place(comp, y, ny, nx):
    at = (comp * ny + y) * nx
    return at // LANES, pl.ds(at % LANES, nx)


def put_v(ref, row, comp, y, ny, value):
    at, lanes = place(comp, y, ny, value.shape[1])
    high, low = split(value)
    ref[at, pl.ds(row, GROUP), lanes] = low
    ref[at, pl.ds(128 + row, GROUP), lanes] = high


def put_u(ref, row, comp, y, ny, half, value):
    at, lanes = place(comp, y, ny, value.shape[1])
    high, low = split(value)
    ref[at, pl.ds(row, GROUP), lanes] = high
    ref[at, pl.ds(2 * half + row, GROUP), lanes] = low


def dots_uv(u_ref, v_ref, acc_ref, half):
    def step(k, carry):
        left = jnp.concatenate([v_ref[k, 128 : 128 + 2 * half, :], u_ref[k]], axis=0)
        acc_ref[...] += lax.dot_general(left, v_ref[k], NT, preferred_element_type=F32)
        return carry

    lax.fori_loop(0, u_ref.shape[0], step, 0, unroll=4)


def dots_uu(u_ref, acc_ref, half):
    def step(k, carry):
        acc_ref[...] += lax.dot_general(u_ref[k, 0 : 2 * half, :], u_ref[k], NT, preferred_element_type=F32)
        return carry

    lax.fori_loop(0, u_ref.shape[0], step, 0, unroll=4)


def middle_kernel(
    own_ref, other_ref, mask_ref, material_ref, table_ref,
    near_ref, edge_u_ref, acc_v_ref, acc_u_ref,
    keep_ref, root_ref, scale_ref, mid_u, mid_v,
):
    core = lax.axis_index("col")
    upper = core == 1
    step = pl.program_id(0)
    _, nz, ny, nx = mask_ref.shape
    half = near_ref.shape[2] // 2
    edge = 3 * core

    @pl.when(step == 0)
    def _():
        keep = mask_ref[...].astype(F32)
        root = jnp.sqrt(lookup(material_ref[...], table_ref))
        keep_ref[...] = keep
        root_ref[...] = root
        scale_ref[...] = keep / root[None]
        acc_v_ref[...] = jnp.zeros_like(acc_v_ref)
        acc_u_ref[...] = jnp.zeros_like(acc_u_ref)
        mid_v[...] = jnp.zeros_like(mid_v)

    for src, side in ((own_ref, core), (other_ref, 1 - core)):
        cells = src.reshape(GROUP * 3 * nz * ny, nx)
        row = pl.multiple_of(side * half + step * GROUP, GROUP)

        def e(comp, layer, y):
            value = cells[pl.ds((comp * nz + layer) * ny + y, GROUP, stride=3 * nz * ny), :]
            return value * keep_ref[comp, layer, y : y + 1, :]

        def row_of(y):
            window = [[e(comp, core + w, y) for comp in range(3)] for w in range(2)]
            window.append([e(comp, core + 2, y) for comp in range(2)])
            return window, [e(comp, edge, y) for comp in range(3)]

        here = row_of(0)
        last = (None,) * 5
        for y in range(ny):
            if y + 1 < ny:
                after = row_of(y + 1)
                (_, _, z0n), (x1n, _, z1n), _ = after[0]
                xbn, _, zbn = after[1]
            else:
                after, z0n, x1n, z1n, xbn, zbn = (None,) * 6
            ((x0, y0, z0), (x1, y1, z1), (x2, y2)), (xb, yb, zb) = here
            h01x = minus(z0n, z0) - (y1 - y0)
            h01y = (x1 - x0) - ahead_x(z0)
            h12x = minus(z1n, z1) - (y2 - y1)
            h12y = (x2 - x1) - ahead_x(z1)
            h1z = ahead_x(y1) - minus(x1n, x1)
            hbz = ahead_x(yb) - minus(xbn, xb)
            lowx = jnp.where(upper, h12x, -yb)
            lowy = jnp.where(upper, h12y, xb)
            topx = jnp.where(upper, minus(zbn, zb) + yb, h01x)
            topy = jnp.where(upper, -xb - ahead_x(zb), h01y)
            h1z_last, h12x_last, hbz_last, topx_last, _ = last
            mid = core + 1
            k = (
                (h01y - h12y) - minus(h1z_last, h1z),
                behind_x(h1z) - (h01x - h12x),
                minus(h12x_last, h12x) - behind_x(h12y),
            )
            kb = (
                (lowy - topy) - minus(hbz_last, hbz),
                behind_x(hbz) - (lowx - topx),
                minus(topx_last, topx) - behind_x(topy),
            )
            root_mid = root_ref[mid, y : y + 1, :]
            root_edge = root_ref[edge, y : y + 1, :]
            for comp in range(3):
                put_v(mid_v, row, comp, y, ny, k[comp] * scale_ref[comp, mid, y : y + 1, :])
                put_u(mid_u, row, comp, y, ny, half, (x1, y1, z1)[comp] * root_mid)
                near_ref[comp, y, pl.ds(row, GROUP), :] = kb[comp] * scale_ref[comp, edge, y : y + 1, :]
                put_u(edge_u_ref, row, comp, y, ny, half, (xb, yb, zb)[comp] * root_edge)
            last = (h1z, h12x, hbz, topx, None)
            here = after

    @pl.when(step == pl.num_programs(0) - 1)
    def _():
        dots_uv(mid_u, mid_v, acc_v_ref, half)
        dots_uu(mid_u, acc_u_ref, half)
        dots_uu(edge_u_ref, acc_u_ref, half)


def middle(block, other, mask, material, table):
    ncol, _, nz, ny, nx = block.shape
    total = 3 * ny * nx // LANES
    near = jax.ShapeDtypeStruct((3, ny, 2 * ncol, nx), F32)
    whole = lambda *shape: pl.BlockSpec(shape, lambda i: (0,) * len(shape))
    block_spec = pl.BlockSpec((GROUP, 3, nz, ny, nx), lambda i: (i, 0, 0, 0, 0))
    outs = [
        jax.ShapeDtypeStruct((3, ny, 2 * ncol, nx), F32),
        jax.ShapeDtypeStruct((total, 4 * ncol, LANES), BF16),
        jax.ShapeDtypeStruct((6 * ncol, 256), F32),
        jax.ShapeDtypeStruct((2 * ncol, 4 * ncol), F32),
    ]
    return pl.pallas_call(
        middle_kernel,
        grid=(ncol // GROUP,),
        out_shape=outs,
        in_specs=[block_spec, block_spec, whole(3, nz, ny, nx), whole(nz, ny, nx), SMEM],
        out_specs=[whole(*out.shape) for out in outs],
        scratch_shapes=[
            pltpu.VMEM((3, nz, ny, nx), F32),
            pltpu.VMEM((nz, ny, nx), F32),
            pltpu.VMEM((3, nz, ny, nx), F32),
            pltpu.VMEM((total, 4 * ncol, LANES), BF16),
            pltpu.VMEM((total, 256, LANES), BF16),
        ],
        compiler_params=pltpu.CompilerParams(vmem_limit_bytes=36 * MIB),
        cost_estimate=pl.CostEstimate(flops=2 * 10**9, bytes_accessed=16 * 10**6, transcendentals=0),
    )(block, other, mask, material, table)


def pack(core, swap, ga, gb, gf, rows, half):
    out = []
    for gram in (ga, gb, gf):
        part = gram[rows, :]
        left, right = part[:, 0:half], part[:, half : 2 * half]
        out.append((jnp.where(swap, right, left), jnp.where(swap, left, right)))
    down = lax.broadcasted_iota(jnp.int32, (half, half), 0)
    across = lax.broadcasted_iota(jnp.int32, (half, half), 1)
    (aa, ab), (ba, bb), (fa, fb) = out
    diag = jnp.sum(jnp.where(down == across, ba, 0.0), axis=1, keepdims=True)
    mixed = jnp.where(across <= down, aa, ba)
    return jnp.concatenate([mixed, fa, ab, bb, fb, jnp.broadcast_to(diag, (half, 256 - 5 * half))], axis=1)


def finish_kernel(
    near_ref, halo_own_ref, halo_other_ref, mask_ref, material_ref, table_ref,
    edge_u_ref, acc_v_ref, acc_u_ref,
    keep_rows_ref, send_rows_ref,
    scale_ref, edge_v, sum_v, grams_ref,
):
    core = lax.axis_index("col")
    ny, nx = mask_ref.shape[2:]
    half = near_ref.shape[2] // 2
    n = 2 * half
    root = jnp.sqrt(lookup(material_ref[3 * core], table_ref))
    for comp in range(3):
        scale_ref[comp] = mask_ref[comp, 3 * core].astype(F32) / root
    scale_ref[2] = scale_ref[2] * core.astype(F32)
    edge_v[...] = jnp.zeros_like(edge_v)
    for halo_ref, side in ((halo_own_ref, core), (halo_other_ref, 1 - core)):
        for group in range(half // GROUP):
            row = pl.multiple_of(side * half + group * GROUP, GROUP)
            from_ = pl.ds(group * GROUP, GROUP)
            h1_last = None
            for y in range(ny):
                h0 = halo_ref[0, y, from_, :]
                h1 = halo_ref[1, y, from_, :]
                change = (h0, h1, minus(h1_last, h1) + behind_x(h0))
                for comp in range(3):
                    value = near_ref[comp, y, pl.ds(row, GROUP), :] - change[comp] * scale_ref[comp, y : y + 1, :]
                    put_v(edge_v, row, comp, y, ny, value)
                h1_last = h1
    sum_v[...] = acc_v_ref[...]
    dots_uv(edge_u_ref, edge_v, sum_v, half)
    cross = sum_v[0:n, 0:n]
    grams_ref[2] = sum_v[0:n, 128 : 128 + n] + (cross + cross.T)
    cross = acc_u_ref[:, n : 2 * n]
    grams_ref[1] = acc_u_ref[:, 0:n] + (cross + cross.T)
    rows = sum_v[n : 2 * n, :] + sum_v[2 * n : 3 * n, :]
    grams_ref[0] = rows[:, 0:n] + rows[:, 128 : 128 + n]
    for side, out_ref in ((core, keep_rows_ref), (1 - core, send_rows_ref)):
        at = pl.ds(pl.multiple_of(side * half, 8), half)
        out_ref[...] = pack(core, side == 1, grams_ref.at[0], grams_ref.at[1], grams_ref.at[2], at, half)


def finish(near, halo_own, halo_other, mask, material, table, edge_u, acc_v, acc_u):
    _, ny, n, nx = near.shape
    total = edge_u.shape[0]
    rows = jax.ShapeDtypeStruct((n // 2, 256), F32)
    return pl.pallas_call(
        finish_kernel,
        out_shape=(rows, rows),
        in_specs=[VMEM, VMEM, VMEM, VMEM, VMEM, SMEM, VMEM, VMEM, VMEM],
        out_specs=[VMEM, VMEM],
        scratch_shapes=[
            pltpu.VMEM((3, ny, nx), F32),
            pltpu.VMEM((total, 256, LANES), BF16),
            pltpu.VMEM(acc_v.shape, F32),
            pltpu.VMEM((3, n, n), F32),
        ],
        compiler_params=pltpu.CompilerParams(vmem_limit_bytes=36 * MIB),
    )(near, halo_own, halo_other, mask, material, table, edge_u, acc_v, acc_u)


def ahead(field, axis):
    size = field.shape[axis]
    at = lax.broadcasted_iota(jnp.int32, field.shape, axis)
    return jnp.where(at == size - 1, 0.0, pltpu.roll(field, size - 1, axis)) - field


def behind(field, axis):
    at = lax.broadcasted_iota(jnp.int32, field.shape, axis)
    return jnp.where(at == 0, 0.0, pltpu.roll(field, 1, axis)) - field


def image_kernel(first, block_ref, one_ref, two_ref, mask_ref, image_ref, keep_ref):
    upper = lax.axis_index("col") == 1
    ncol, _, nz, ny, nx = block_ref.shape
    keep_ref[...] = mask_ref[...].astype(F32)
    ones = one_ref.reshape(2 * ny * ncol, nx)
    twos = two_ref.reshape(2 * ny * ncol, nx)

    def body(j, carry):
        col = first + j

        def e(comp, layer):
            return block_ref[col, comp, layer] * keep_ref[comp, layer]

        at0 = pl.ds(col, ny, stride=ncol)
        at1 = pl.ds(ny * ncol + col, ny, stride=ncol)
        one0, one1, two0, two1 = ones[at0, :], ones[at1, :], twos[at0, :], twos[at1, :]
        x, y, z = (e(comp, 0) for comp in range(3))
        lowy = x - jnp.where(upper, two0, one0)
        lowx = jnp.where(upper, two1, one1) - y
        for layer in range(nz):
            if layer + 1 < nz:
                xn, yn, zn = (e(comp, layer + 1) for comp in range(3))
            else:
                xn, yn, zn = jnp.where(upper, one0, two0), jnp.where(upper, one1, two1), None
            topx = ahead(z, 0) - (yn - y)
            topy = (xn - x) - ahead(z, 1)
            hz = ahead(y, 1) - ahead(x, 0)
            image_ref[j, 0, layer] = ((lowy - topy) - behind(hz, 0)) * keep_ref[0, layer]
            image_ref[j, 1, layer] = (behind(hz, 1) - (lowx - topx)) * keep_ref[1, layer]
            image_ref[j, 2, layer] = (behind(topx, 0) - behind(topy, 1)) * keep_ref[2, layer]
            x, y, z, lowx, lowy = xn, yn, zn, topx, topy
        return carry

    lax.fori_loop(0, image_ref.shape[0], body, 0, unroll=4)


def image_of(block, one, two, mask, first, count):
    _, _, nz, ny, nx = block.shape
    return pl.pallas_call(
        functools.partial(image_kernel, first),
        out_shape=jax.ShapeDtypeStruct((count,) + block.shape[1:], F32),
        in_specs=[VMEM] * 4,
        out_specs=VMEM,
        scratch_shapes=[pltpu.VMEM((3, nz, ny, nx), F32)],
        compiler_params=pltpu.CompilerParams(vmem_limit_bytes=16 * MIB),
        cost_estimate=pl.CostEstimate(flops=10**7, bytes_accessed=3 * 10**6, transcendentals=0),
    )(block, one, two, mask)


PARTS = 4
PIECES = 8


def residual_kernel(
    scale, rows_ref, block_ref, image0_ref, image1_ref, image2_ref, image3_ref, mask_ref, material_ref, table_ref,
    out_ref, ga_ref, gb_ref, gf_ref, mass_ref, theta_ref, buffer, sems,
):
    swap = lax.axis_index("col") == 1
    half, total = ga_ref.shape
    down = lax.broadcasted_iota(jnp.int32, (half, half), 0)
    across = lax.broadcasted_iota(jnp.int32, (half, half), 1)
    rows = rows_ref[...] * scale
    mixed, fa, ab, bb, fb = (rows[:, k * half : (k + 1) * half] for k in range(5))
    diag_b = rows[:, 5 * half : 5 * half + 1]
    diag_a = jnp.sum(jnp.where(down == across, mixed, 0.0), axis=1, keepdims=True)
    theta_ref[...] = jnp.broadcast_to(diag_a / diag_b, theta_ref.shape)
    mass_ref[...] = lookup(material_ref[...], table_ref)[None] * mask_ref[...].astype(F32)
    ncol = block_ref.shape[0]
    per = ncol // PIECES
    images = (image0_ref, image1_ref, image2_ref, image3_ref)
    copies = []
    for piece in range(PIECES):
        part, start = divmod(piece * per, ncol // PARTS)
        for j in range(per):
            col = piece * per + j
            theta = theta_ref[col : col + 1, :]
            buffer[col] = images[part][start + j] - theta[None, None] * (mass_ref[...] * block_ref[col])
        some = pl.ds(piece * per, per)
        copies.append(pltpu.make_async_copy(buffer.at[some], out_ref.at[some], sems.at[piece]))
        copies[-1].start()
    flat = mixed.T
    aa = jnp.where(across <= down, mixed, flat)
    ba = jnp.where(across == down, diag_b, jnp.where(across > down, mixed, flat))
    for ref, a, b in ((ga_ref, aa, ab), (gb_ref, ba, bb), (gf_ref, fa, fb)):
        ref[...] = jnp.concatenate([jnp.where(swap, b, a), jnp.where(swap, a, b)], axis=1)
    for copy in copies:
        copy.wait()


def residual_of(rows, block, images, mask, material, table, scale):
    ncol, _, nz, ny, nx = block.shape
    gram = jax.ShapeDtypeStruct((ncol, 2 * ncol), F32)
    return pl.pallas_call(
        functools.partial(residual_kernel, scale),
        out_shape=(jax.ShapeDtypeStruct(block.shape, F32), gram, gram, gram),
        in_specs=[VMEM] * (PARTS + 4) + [SMEM],
        out_specs=[HBM] + [VMEM] * 3,
        scratch_shapes=[
            pltpu.VMEM((3, nz, ny, nx), F32),
            pltpu.VMEM((ncol, nx), F32),
            pltpu.VMEM(block.shape, F32),
            pltpu.SemaphoreType.DMA((PIECES,)),
        ],
        compiler_params=pltpu.CompilerParams(vmem_limit_bytes=24 * MIB),
        cost_estimate=pl.CostEstimate(flops=2 * 10**7, bytes_accessed=15 * 10**6, transcendentals=0),
    )(rows, block, *images, mask, material, table)


def exchange_rounds(slabs):
    nz, ny, nx = GRIDS[slabs]
    rounds = []
    for size, stride in ((nx, 1), (ny, nx), (nz, nx * ny)):
        for flip in {2: (1,), 4: (1, 3), 8: (1, 2, 7)}[size]:
            rounds.append([i + ((i // stride % size) ^ flip) * stride - i // stride % size * stride for i in range(slabs)])
    shift = {2: 1, 8: 3}[nz]
    turned = rounds[-shift:] + rounds[:-shift]
    return [
        [(2 * i, 2 * a[i]) for i in range(slabs)] + [(2 * i + 1, 2 * b[i] + 1) for i in range(slabs)]
        for a, b in zip(rounds, turned)
    ]


def shards(block, material, table, mask):
    slabs = lax.axis_size("space")
    ncol, _, nz, ny, nx = block.shape
    scale = 1.0 / (3.0 * nz * slabs * ny * nx)
    swap = [(0, 1), (1, 0)]
    both = ("space", "col")
    other = lax.ppermute(block, "col", swap)
    one, two = edges(block, mask)
    straight = [(2 * i, 2 * i + 2) for i in range(slabs - 1)] + [(2 * i + 3, 2 * i + 1) for i in range(slabs - 1)]
    crossed = [(2 * i + 1, 2 * i + 2) for i in range(slabs - 1)] + [(2 * i + 2, 2 * i + 1) for i in range(slabs - 1)]
    halo_own = lax.ppermute(one, both, straight)
    halo_other = lax.ppermute(two, both, crossed)
    near, edge_u, acc_v, acc_u = middle(block, other, mask, material, table)
    keep_rows, send_rows = finish(near, halo_own, halo_other, mask, material, table, edge_u, acc_v, acc_u)
    rows = keep_rows + lax.ppermute(send_rows, "col", swap)
    rows, halo_other = lax.optimization_barrier((rows, halo_other))
    halo_far = lax.ppermute(halo_other, "col", swap)
    images = []
    for index, pairs in enumerate(exchange_rounds(slabs)):
        arrived = lax.ppermute(rows, both, pairs)
        if 1 <= index <= PARTS:
            held, halo_far = lax.optimization_barrier((rows, halo_far))
            count = ncol // PARTS
            image = image_of(block, halo_own, halo_far, mask, (index - 1) * count, count)
            arrived, image = lax.optimization_barrier((arrived, image))
            images.append(image)
        rows = rows + arrived
    return residual_of(rows, block, images, mask, material, table, scale)


def solution(mesh):
    in_specs = (
        P("col", None, "space", None, None),
        P("space", None, None),
        P(),
        P(None, "space", None, None),
    )
    out_specs = (
        P("col", None, "space", None, None),
        P("col", None),
        P("col", None),
        P("col", None),
    )
    return jax.shard_map(shards, mesh=mesh, in_specs=in_specs, out_specs=out_specs, check_vma=False)
```

time: 817 us -> 77.3 us (0.09)
  the two profiles are of different devices: /device:TPU:8 before, /device:TPU:32 now
where the time goes in v2:
time: 77.3 us; the launch traced here: 77.1 us
  Pallas kernels  28.4 us (37%)
  waiting for transfers between devices  24.4 us (32%)
  starting transfers between devices  20.9 us (27%)
  local copies, waits for them, and re-layouts  2.35 us (3%)
  between operations  1.02 us (1%)
    ppermute x7, waiting for transfers between devices, shards(): arrived = lax.ppermute(rows, both, pairs)  21.6 us
    pallas_call x1, Pallas kernels, middle(): pl.pallas_call(middle_kernel, grid=(ncol // GROUP,), out_shape=outs, in_s...  13.5 us
    ppermute x7, starting transfers between devices, shards(): arrived = lax.ppermute(rows, both, pairs)  11.3 us
    ppermute x1, starting transfers between devices, shards(): halo_other = lax.ppermute(two, both, crossed)  5.81 us
    pallas_call x1, Pallas kernels, residual_of(): pl.pallas_call(functools.partial(residual_kernel, scale), out_shape=(jax....  3.98 us
    pallas_call x1, Pallas kernels, edges(): pl.pallas_call(edges_kernel, out_shape=(shape, shape), in_specs=[HBM, HBM...  3.72 us
    pallas_call x4, Pallas kernels, image_of(): pl.pallas_call(functools.partial(image_kernel, first), out_shape=jax.Shap...  3.57 us
    pallas_call x1, Pallas kernels, finish(): pl.pallas_call(finish_kernel, out_shape=(rows, rows), in_specs=[VMEM, VME...  3.57 us
  transfers between devices with their start and end apart: 12, of which 9 were waited for; matrix products, arithmetic and copies ran while one was open for 0% of the time, Pallas kernels for 27%

profile of v2, /device:TPU:32, one launch (start us, length us, event | category | flops | bytes accessed | tf_op | source)
XLA Modules:
  0.0 77.1 jit_solution(10468282660146418067)
XLA Ops:
  0.8 3.7 %shard_map.76 = (f32[2,16,48,128]{3,2,1,0:T(8,128)}, f32[2,16,48,128]{3,2,1,0:T(8,128)}) custom-call(f32[48,3,4,16,128]{4,3,2,1,0:T(8,128)} %block_ref.11, s32[3,4,16,128]{3,2,1,0:T(8,128)} %mask_ref.15), custom_call_target="tpu_custom_call" | custom-call | tf_op jit(solution)/shard_map/pallas_call | solution.py:90
  4.5 3.4 %collective-permute-start.1 = (f32[2,16,48,128]{3,2,1,0:T(8,128)}, f32[2,16,48,128]{3,2,1,0:T(8,128)S(1)}, u32[]{:S(2)}, u32[]{:S(2)}) collective-permute-start(f32[2,16,48,128]{3,2,1,0:T(8,128)} %get-tuple-element.27), channel_id=1, source_target_pairs={{0,2},{2,4},{4,6},{6,8},{8,10},{10,12},{12,14},{14,16},{16,18},{18... | collective-permute-start | bytes 2359304 | tf_op jit(solution)/shard_map/ppermute | solution.py:474
  7.9 5.8 %collective-permute-start.2 = (f32[2,16,48,128]{3,2,1,0:T(8,128)}, f32[2,16,48,128]{3,2,1,0:T(8,128)S(1)}, u32[]{:S(2)}, u32[]{:S(2)}) collective-permute-start(f32[2,16,48,128]{3,2,1,0:T(8,128)} %get-tuple-element.28), channel_id=1, source_target_pairs={{1,2},{3,4},{5,6},{7,8},{9,10},{11,12},{13,14},{15,16},{17,18},{19... | collective-permute-start | bytes 2359304 | tf_op jit(solution)/shard_map/ppermute | solution.py:475
  13.8 2.3 %copy-done = f32[48,3,4,16,128]{4,3,2,1,0:T(8,128)S(1)} copy-done((f32[48,3,4,16,128]{4,3,2,1,0:T(8,128)S(1)}, f32[48,3,4,16,128]{4,3,2,1,0:T(8,128)}, u32[]{:S(2)}) %copy-start) | copy-done | bytes 4718616
  16.1 13.5 %shard_map.75 = (f32[3,16,96,128]{3,2,1,0:T(8,128)S(1)}, bf16[12,192,512]{2,1,0:T(8,128)(2,1)S(1)}, f32[288,256]{1,0:T(8,128)S(1)}, f32[96,192]{1,0:T(8,128)S(1)}) custom-call(f32[48,3,4,16,128]{4,3,2,1,0:T(8,128)S(1)} %copy-done, f32[48,3,4,16,128]{4,3,2,1,0:T(8,128)} %collective-permute-done.other_ref, s32[3,4,16,128]{3,2,1,0:T(8,128)S(1)} %copy-done.2, ...), custom_call_target="tpu_custom_call" | custom-call | flops 2000000000 | bytes 16000000 | tf_op jit(solution)/shard_map/pallas_call | solution.py:239
  29.7 1.6 %collective-permute-done.2.halo_other_ref = f32[2,16,48,128]{3,2,1,0:T(8,128)S(1)} collective-permute-done((f32[2,16,48,128]{3,2,1,0:T(8,128)}, f32[2,16,48,128]{3,2,1,0:T(8,128)S(1)}, u32[]{:S(2)}, u32[]{:S(2)}) %collective-permute-start.2) | collective-permute-done | bytes 786464 | tf_op jit(solution)/shard_map/ppermute | solution.py:475
  31.2 3.6 %shard_map.77 = (f32[48,256]{1,0:T(8,128)S(1)}, f32[48,256]{1,0:T(8,128)S(1)}) custom-call(f32[3,16,96,128]{3,2,1,0:T(8,128)S(1)} %get-tuple-element.26.near_ref, f32[2,16,48,128]{3,2,1,0:T(8,128)S(1)} %collective-permute-done.1.halo_own_ref.one_ref, f32[2,16,48,128]{3,2,1,0:T(8,128)S(1)} %collective-permute-done.2.halo_other_ref, ...), custom_call_target="tpu_custom_call" | custom-call | tf_op jit(solution)/shard_map/pallas_call | solution.py:316
  34.9 1.2 %collective-permute-done.3 = f32[48,256]{1,0:T(8,128)S(1)} collective-permute-done((f32[48,256]{1,0:T(8,128)S(1)}, f32[48,256]{1,0:T(8,128)S(1)}, u32[]{:S(2)}, u32[]{:S(2)}) %collective-permute-start.3) | collective-permute-done | bytes 49184 | tf_op jit(solution)/shard_map/ppermute | solution.py:478
  36.3 4.1 %collective-permute-done.4 = f32[48,256]{1,0:T(8,128)S(1)} collective-permute-done((f32[48,256]{1,0:T(8,128)S(1)}, f32[48,256]{1,0:T(8,128)S(1)}, u32[]{:S(2)}, u32[]{:S(2)}) %collective-permute-start.4) | collective-permute-done | bytes 49184 | tf_op jit(solution)/shard_map/ppermute | solution.py:483
  40.6 0.9 %shard_map.78.image0_ref = f32[12,3,4,16,128]{4,3,2,1,0:T(8,128)S(1)} custom-call(f32[48,3,4,16,128]{4,3,2,1,0:T(8,128)S(1)} %copy-done.1, f32[2,16,48,128]{3,2,1,0:T(8,128)S(1)} %collective-permute-done.1.halo_own_ref.one_ref, f32[2,16,48,128]{3,2,1,0:T(8,128)S(1)} %collective-permute-done.6.two_ref, s32[3,4,16,128]{3,2,1,0:T(8,128)S(1)} %copy-done.2), custom_call_target="tpu_custom_call" | custom-call | flops 10000000 | bytes 3000000 | tf_op jit(solution)/shard_map/pallas_call | solution.py:380
  41.5 4.4 %collective-permute-done.5 = f32[48,256]{1,0:T(8,128)S(1)} collective-permute-done((f32[48,256]{1,0:T(8,128)S(1)}, f32[48,256]{1,0:T(8,128)S(1)}, u32[]{:S(2)}, u32[]{:S(2)}) %collective-permute-start.5) | collective-permute-done | bytes 49184 | tf_op jit(solution)/shard_map/ppermute | solution.py:483
  45.9 0.9 %shard_map.79.image1_ref = f32[12,3,4,16,128]{4,3,2,1,0:T(8,128)S(1)} custom-call(f32[48,3,4,16,128]{4,3,2,1,0:T(8,128)S(1)} %copy-done.1, f32[2,16,48,128]{3,2,1,0:T(8,128)S(1)} %collective-permute-done.1.halo_own_ref.one_ref, f32[2,16,48,128]{3,2,1,0:T(8,128)S(1)} %collective-permute-done.6.two_ref, s32[3,4,16,128]{3,2,1,0:T(8,128)S(1)} %copy-done.2), custom_call_target="tpu_custom_call" | custom-call | flops 10000000 | bytes 3000000 | tf_op jit(solution)/shard_map/pallas_call | solution.py:380
  46.8 3.2 %collective-permute-done.7 = f32[48,256]{1,0:T(8,128)S(1)} collective-permute-done((f32[48,256]{1,0:T(8,128)S(1)}, f32[48,256]{1,0:T(8,128)S(1)}, u32[]{:S(2)}, u32[]{:S(2)}) %collective-permute-start.7) | collective-permute-done | bytes 49184 | tf_op jit(solution)/shard_map/ppermute | solution.py:483
  50.0 1.8 %collective-permute-start.8 = (f32[48,256]{1,0:T(8,128)S(1)}, f32[48,256]{1,0:T(8,128)S(1)}, u32[]{:S(2)}, u32[]{:S(2)}) collective-permute-start(f32[48,256]{1,0:T(8,128)S(1)} %add.27), channel_id=1, source_target_pairs={{0,24},{2,26},{4,28},{6,30},{8,16},{10,18},{12,20},{14,22},{16,8},... | collective-permute-start | bytes 147464 | tf_op jit(solution)/shard_map/ppermute | solution.py:483
  51.9 0.9 %shard_map.80.image2_ref = f32[12,3,4,16,128]{4,3,2,1,0:T(8,128)S(1)} custom-call(f32[48,3,4,16,128]{4,3,2,1,0:T(8,128)S(1)} %copy-done.1, f32[2,16,48,128]{3,2,1,0:T(8,128)S(1)} %collective-permute-done.1.halo_own_ref.one_ref, f32[2,16,48,128]{3,2,1,0:T(8,128)S(1)} %collective-permute-done.6.two_ref, s32[3,4,16,128]{3,2,1,0:T(8,128)S(1)} %copy-done.2), custom_call_target="tpu_custom_call" | custom-call | flops 10000000 | bytes 3000000 | tf_op jit(solution)/shard_map/pallas_call | solution.py:380
  52.8 2.6 %collective-permute-done.8 = f32[48,256]{1,0:T(8,128)S(1)} collective-permute-done((f32[48,256]{1,0:T(8,128)S(1)}, f32[48,256]{1,0:T(8,128)S(1)}, u32[]{:S(2)}, u32[]{:S(2)}) %collective-permute-start.8) | collective-permute-done | bytes 49184 | tf_op jit(solution)/shard_map/ppermute | solution.py:483
  55.4 0.3 collective-permute-start.9
  55.7 0.9 %shard_map.81.image3_ref = f32[12,3,4,16,128]{4,3,2,1,0:T(8,128)S(1)} custom-call(f32[48,3,4,16,128]{4,3,2,1,0:T(8,128)S(1)} %copy-done.1, f32[2,16,48,128]{3,2,1,0:T(8,128)S(1)} %collective-permute-done.1.halo_own_ref.one_ref, f32[2,16,48,128]{3,2,1,0:T(8,128)S(1)} %collective-permute-done.6.two_ref, s32[3,4,16,128]{3,2,1,0:T(8,128)S(1)} %copy-done.2), custom_call_target="tpu_custom_call" | custom-call | flops 10000000 | bytes 3000000 | tf_op jit(solution)/shard_map/pallas_call | solution.py:380
  56.6 3.2 %collective-permute-done.9 = f32[48,256]{1,0:T(8,128)S(1)} collective-permute-done((f32[48,256]{1,0:T(8,128)S(1)}, f32[48,256]{1,0:T(8,128)S(1)}, u32[]{:S(2)}, u32[]{:S(2)}) %collective-permute-start.9) | collective-permute-done | bytes 49184 | tf_op jit(solution)/shard_map/ppermute | solution.py:483
  59.8 3.3 %collective-permute-start.10 = (f32[48,256]{1,0:T(8,128)S(1)}, f32[48,256]{1,0:T(8,128)S(1)}, u32[]{:S(2)}, u32[]{:S(2)}) collective-permute-start(f32[48,256]{1,0:T(8,128)S(1)} %add.29), channel_id=1, source_target_pairs={{0,64},{2,66},{4,68},{6,70},{8,72},{10,74},{12,76},{14,78},{16,80}... | collective-permute-start | bytes 147464 | tf_op jit(solution)/shard_map/ppermute | solution.py:483
  63.1 2.1 %collective-permute-done.10 = f32[48,256]{1,0:T(8,128)S(1)} collective-permute-done((f32[48,256]{1,0:T(8,128)S(1)}, f32[48,256]{1,0:T(8,128)S(1)}, u32[]{:S(2)}, u32[]{:S(2)}) %collective-permute-start.10) | collective-permute-done | bytes 49184 | tf_op jit(solution)/shard_map/ppermute | solution.py:483
  65.2 5.7 %collective-permute-start.11 = (f32[48,256]{1,0:T(8,128)S(1)}, f32[48,256]{1,0:T(8,128)S(1)}, u32[]{:S(2)}, u32[]{:S(2)}) collective-permute-start(f32[48,256]{1,0:T(8,128)S(1)} %add.30), channel_id=1, source_target_pairs={{0,224},{2,226},{4,228},{6,230},{8,232},{10,234},{12,236},{14,238}... | collective-permute-start | bytes 147464 | tf_op jit(solution)/shard_map/ppermute | solution.py:483
  70.9 2.1 %collective-permute-done.11 = f32[48,256]{1,0:T(8,128)S(1)} collective-permute-done((f32[48,256]{1,0:T(8,128)S(1)}, f32[48,256]{1,0:T(8,128)S(1)}, u32[]{:S(2)}, u32[]{:S(2)}) %collective-permute-start.11) | collective-permute-done | bytes 49184 | tf_op jit(solution)/shard_map/ppermute | solution.py:483
  73.0 4.0 %shard_map.82 = (f32[48,3,4,16,128]{4,3,2,1,0:T(8,128)}, f32[48,96]{1,0:T(8,128)}, f32[48,96]{1,0:T(8,128)}, f32[48,96]{1,0:T(8,128)}) custom-call(f32[48,256]{1,0:T(8,128)S(1)} %add.31.rows_ref, f32[48,3,4,16,128]{4,3,2,1,0:T(8,128)S(1)} %copy-done.1, f32[12,3,4,16,128]{4,3,2,1,0:T(8,128)S(1)} %shard_map.78.image0_ref, ...), custom_call_target="tpu_custom_call" | custom-call | flops 20000000 | bytes 15000000 | tf_op jit(solution)/shard_map/pallas_call | solution.py:434
  (26 shorter events, 0.7 us)
Async XLA Ops:
  0.6 13.1 %copy-start.2 = (s32[3,4,16,128]{3,2,1,0:T(8,128)S(1)}, s32[3,4,16,128]{3,2,1,0:T(8,128)}, u32[]{:S(2)}) copy-start(s32[3,4,16,128]{3,2,1,0:T(8,128)} %mask_ref.15) | copy-start | bytes 294916
  0.6 13.1 %copy-start.3 = (s32[4,16,128]{2,1,0:T(8,128)S(1)}, s32[4,16,128]{2,1,0:T(8,128)}, u32[]{:S(2)}) copy-start(s32[4,16,128]{2,1,0:T(8,128)} %material_ref.5) | copy-start | bytes 98308
  0.7 13.1 %copy-start.4 = (f32[8]{0:T(128)S(1)}, f32[8]{0:T(128)}, u32[]{:S(2)}) copy-start(f32[8]{0:T(128)} %table_ref.5) | copy-start | bytes 100
  0.7 13.1 %collective-permute-start = (f32[48,3,4,16,128]{4,3,2,1,0:T(8,128)}, f32[48,3,4,16,128]{4,3,2,1,0:T(8,128)}, u32[]{:S(2)}, u32[]{:S(2)}) collective-permute-start(f32[48,3,4,16,128]{4,3,2,1,0:T(8,128)} %block_ref.11), channel_id=1, source_target_pairs={{0,1},{1,0},{2,3},{3,2},{4,5},{5,4},{6,7},{7,6},{8,9},{9,8},{10,11... | collective-permute-start | bytes 14155784 | tf_op jit(solution)/shard_map/ppermute | solution.py:470
  4.5 25.2 %collective-permute-start.1 = (f32[2,16,48,128]{3,2,1,0:T(8,128)}, f32[2,16,48,128]{3,2,1,0:T(8,128)S(1)}, u32[]{:S(2)}, u32[]{:S(2)}) collective-permute-start(f32[2,16,48,128]{3,2,1,0:T(8,128)} %get-tuple-element.27), channel_id=1, source_target_pairs={{0,2},{2,4},{4,6},{6,8},{8,10},{10,12},{12,14},{14,16},{16,18},{18... | collective-permute-start | bytes 2359304 | tf_op jit(solution)/shard_map/ppermute | solution.py:474
  7.9 23.3 %collective-permute-start.2 = (f32[2,16,48,128]{3,2,1,0:T(8,128)}, f32[2,16,48,128]{3,2,1,0:T(8,128)S(1)}, u32[]{:S(2)}, u32[]{:S(2)}) collective-permute-start(f32[2,16,48,128]{3,2,1,0:T(8,128)} %get-tuple-element.28), channel_id=1, source_target_pairs={{1,2},{3,4},{5,6},{7,8},{9,10},{11,12},{13,14},{15,16},{17,18},{19... | collective-permute-start | bytes 2359304 | tf_op jit(solution)/shard_map/ppermute | solution.py:475
  13.8 2.3 %copy-start = (f32[48,3,4,16,128]{4,3,2,1,0:T(8,128)S(1)}, f32[48,3,4,16,128]{4,3,2,1,0:T(8,128)}, u32[]{:S(2)}) copy-start(f32[48,3,4,16,128]{4,3,2,1,0:T(8,128)} %block_ref.11) | copy-start | bytes 14155780
  31.2 9.3 %copy-start.1 = (f32[48,3,4,16,128]{4,3,2,1,0:T(8,128)S(1)}, f32[48,3,4,16,128]{4,3,2,1,0:T(8,128)}, u32[]{:S(2)}) copy-start(f32[48,3,4,16,128]{4,3,2,1,0:T(8,128)} %block_ref.11) | copy-start | bytes 14155780
  34.8 1.3 %collective-permute-start.3 = (f32[48,256]{1,0:T(8,128)S(1)}, f32[48,256]{1,0:T(8,128)S(1)}, u32[]{:S(2)}, u32[]{:S(2)}) collective-permute-start(f32[48,256]{1,0:T(8,128)S(1)} %get-tuple-element.33), channel_id=1, source_target_pairs={{0,1},{1,0},{2,3},{3,2},{4,5},{5,4},{6,7},{7,6},{8,9},{9,8},{10,11... | collective-permute-start | bytes 147464 | tf_op jit(solution)/shard_map/ppermute | solution.py:478
  36.1 4.4 %collective-permute-start.6 = (f32[2,16,48,128]{3,2,1,0:T(8,128)S(1)}, f32[2,16,48,128]{3,2,1,0:T(8,128)S(1)}, u32[]{:S(2)}, u32[]{:S(2)}) collective-permute-start(f32[2,16,48,128]{3,2,1,0:T(8,128)S(1)} %collective-permute-done.2.halo_other_ref), channel_id=1, source_target_pairs={{0,1},{1,0},{2,3},{3,2},{4,5},{5,4},{6,7},{7,6},{8,9},{9,8},{10,11... | collective-permute-start | bytes 2359304 | tf_op jit(solution)/shard_map/ppermute | solution.py:480
  36.3 4.1 %collective-permute-start.4 = (f32[48,256]{1,0:T(8,128)S(1)}, f32[48,256]{1,0:T(8,128)S(1)}, u32[]{:S(2)}, u32[]{:S(2)}) collective-permute-start(f32[48,256]{1,0:T(8,128)S(1)} %add.24), channel_id=1, source_target_pairs={{0,2},{2,0},{4,6},{6,4},{8,10},{10,8},{12,14},{14,12},{16,18},{18,... | collective-permute-start | bytes 147464 | tf_op jit(solution)/shard_map/ppermute | solution.py:483
  40.4 5.4 %collective-permute-start.5 = (f32[48,256]{1,0:T(8,128)S(1)}, f32[48,256]{1,0:T(8,128)S(1)}, u32[]{:S(2)}, u32[]{:S(2)}) collective-permute-start(f32[48,256]{1,0:T(8,128)S(1)} %add.25), channel_id=1, source_target_pairs={{0,6},{2,4},{4,2},{6,0},{8,14},{10,12},{12,10},{14,8},{16,22},{18,... | collective-permute-start | bytes 147464 | tf_op jit(solution)/shard_map/ppermute | solution.py:483
  45.8 4.2 %collective-permute-start.7 = (f32[48,256]{1,0:T(8,128)S(1)}, f32[48,256]{1,0:T(8,128)S(1)}, u32[]{:S(2)}, u32[]{:S(2)}) collective-permute-start(f32[48,256]{1,0:T(8,128)S(1)} %add.26), channel_id=1, source_target_pairs={{0,8},{2,10},{4,12},{6,14},{8,0},{10,2},{12,4},{14,6},{16,24},{18,... | collective-permute-start | bytes 147464 | tf_op jit(solution)/shard_map/ppermute | solution.py:483
  50.0 5.4 %collective-permute-start.8 = (f32[48,256]{1,0:T(8,128)S(1)}, f32[48,256]{1,0:T(8,128)S(1)}, u32[]{:S(2)}, u32[]{:S(2)}) collective-permute-start(f32[48,256]{1,0:T(8,128)S(1)} %add.27), channel_id=1, source_target_pairs={{0,24},{2,26},{4,28},{6,30},{8,16},{10,18},{12,20},{14,22},{16,8},... | collective-permute-start | bytes 147464 | tf_op jit(solution)/shard_map/ppermute | solution.py:483
  55.4 4.4 %collective-permute-start.9 = (f32[48,256]{1,0:T(8,128)S(1)}, f32[48,256]{1,0:T(8,128)S(1)}, u32[]{:S(2)}, u32[]{:S(2)}) collective-permute-start(f32[48,256]{1,0:T(8,128)S(1)} %add.28), channel_id=1, source_target_pairs={{0,32},{2,34},{4,36},{6,38},{8,40},{10,42},{12,44},{14,46},{16,48}... | collective-permute-start | bytes 147464 | tf_op jit(solution)/shard_map/ppermute | solution.py:483
  59.8 5.4 %collective-permute-start.10 = (f32[48,256]{1,0:T(8,128)S(1)}, f32[48,256]{1,0:T(8,128)S(1)}, u32[]{:S(2)}, u32[]{:S(2)}) collective-permute-start(f32[48,256]{1,0:T(8,128)S(1)} %add.29), channel_id=1, source_target_pairs={{0,64},{2,66},{4,68},{6,70},{8,72},{10,74},{12,76},{14,78},{16,80}... | collective-permute-start | bytes 147464 | tf_op jit(solution)/shard_map/ppermute | solution.py:483
  65.2 7.7 %collective-permute-start.11 = (f32[48,256]{1,0:T(8,128)S(1)}, f32[48,256]{1,0:T(8,128)S(1)}, u32[]{:S(2)}, u32[]{:S(2)}) collective-permute-start(f32[48,256]{1,0:T(8,128)S(1)} %add.30), channel_id=1, source_target_pairs={{0,224},{2,226},{4,228},{6,230},{8,232},{10,234},{12,236},{14,238}... | collective-permute-start | bytes 147464 | tf_op jit(solution)/shard_map/ppermute | solution.py:483

commit v3 on v2

v3 whole, which is shorter than its diff:
```python
import functools

import jax
import jax.numpy as jnp
from jax import lax
from jax.experimental import pallas as pl
from jax.experimental.pallas import tpu as pltpu
from jax.sharding import PartitionSpec as P

MIB = 1 << 20
GRIDS = {128: (8, 4, 4), 8: (2, 2, 2)}
F32 = jnp.float32
BF16 = jnp.bfloat16
NT = (((1,), (1,)), ((), ()))
VMEM = pl.BlockSpec(memory_space=pltpu.VMEM)
SMEM = pl.BlockSpec(memory_space=pltpu.SMEM)
HBM = pl.BlockSpec(memory_space=pltpu.HBM)
GROUP = 16
LANES = 512
EDGE_LIMIT = 51
OWN_LIMIT = 48
OTHER_LIMIT = 30


def lookup(material, table_ref):
    eps = jnp.zeros(material.shape, F32)
    for index in range(table_ref.shape[0]):
        eps = jnp.where(material == index, table_ref[index], eps)
    return eps


def split(value):
    high = value.astype(BF16)
    return high, (value - high.astype(F32)).astype(BF16)


def ahead_x(field):
    at = lax.broadcasted_iota(jnp.int32, field.shape, 1)
    size = field.shape[1]
    return jnp.where(at == size - 1, 0.0, pltpu.roll(field, size - 1, 1)) - field


def behind_x(field):
    at = lax.broadcasted_iota(jnp.int32, field.shape, 1)
    return jnp.where(at == 0, 0.0, pltpu.roll(field, 1, 1)) - field


def minus(left, right):
    return -right if left is None else left - right


def edges_kernel(block_ref, mask_ref, one_ref, two_ref, first_ref, last_ref, mask_first, mask_last, sems):
    ncol, _, nz, ny, nx = block_ref.shape
    groups = ncol // GROUP
    masks = [
        pltpu.make_async_copy(mask_ref.at[0:2, 0], mask_first, sems.at[0]),
        pltpu.make_async_copy(mask_ref.at[:, nz - 1], mask_last, sems.at[1]),
    ]
    for copy in masks:
        copy.start()
    copies = []
    for group in range(groups):
        some = pl.ds(group * GROUP, GROUP)
        copies.append((
            pltpu.make_async_copy(block_ref.at[some, 0:2, 0], first_ref.at[some], sems.at[2 + 2 * group]),
            pltpu.make_async_copy(block_ref.at[some, :, nz - 1], last_ref.at[some], sems.at[3 + 2 * group]),
        ))
        for copy in copies[-1]:
            copy.start()
    for copy in masks:
        copy.wait()
    swap = lax.axis_index("col") == 1
    slab = lax.axis_index("space")
    lowest = (slab != 0).astype(F32)
    highest = (slab != lax.axis_size("space") - 1).astype(F32)
    first = first_ref.reshape(ncol * 2 * ny, nx)
    last = last_ref.reshape(ncol * 3 * ny, nx)
    for group in range(groups):
        for copy in copies[group]:
            copy.wait()
        out = pl.ds(group * GROUP, GROUP)

        def low(comp, y):
            keep = mask_first[comp, y : y + 1, :].astype(F32) * lowest
            return first[pl.ds((group * GROUP * 2 + comp) * ny + y, GROUP, stride=2 * ny), :] * keep

        def high(comp, y):
            keep = mask_last[comp, y : y + 1, :].astype(F32) * highest
            return last[pl.ds((group * GROUP * 3 + comp) * ny + y, GROUP, stride=3 * ny), :] * keep

        ez = high(2, 0)
        for y in range(ny):
            ez_next = high(2, y + 1) if y + 1 < ny else None
            up0 = high(0, y) + ahead_x(ez)
            up1 = high(1, y) + minus(ez_next, ez)
            down0 = low(0, y)
            down1 = low(1, y)
            one_ref[0, y, out, :] = jnp.where(swap, down0, up0)
            one_ref[1, y, out, :] = jnp.where(swap, down1, up1)
            two_ref[0, y, out, :] = jnp.where(swap, up0, down0)
            two_ref[1, y, out, :] = jnp.where(swap, up1, down1)
            ez = ez_next


def edges(block, mask):
    ncol, _, nz, ny, nx = block.shape
    shape = jax.ShapeDtypeStruct((2, ny, ncol, nx), F32)
    return pl.pallas_call(
        edges_kernel,
        out_shape=(shape, shape),
        in_specs=[HBM, HBM],
        out_specs=[VMEM, VMEM],
        scratch_shapes=[
            pltpu.VMEM((ncol, 2, ny, nx), F32),
            pltpu.VMEM((ncol, 3, ny, nx), F32),
            pltpu.VMEM((2, ny, nx), jnp.int32),
            pltpu.VMEM((3, ny, nx), jnp.int32),
            pltpu.SemaphoreType.DMA((2 + 2 * (ncol // GROUP),)),
        ],
        compiler_params=pltpu.CompilerParams(vmem_limit_bytes=EDGE_LIMIT * MIB),
    )(block, mask)


def place(comp, y, ny, nx):
    at = (comp * ny + y) * nx
    return at // LANES, pl.ds(at % LANES, nx)


def put(ref, row, comp, y, ny, value):
    at, lanes = place(comp, y, ny, value.shape[1])
    high, low = split(value)
    ref[at, pl.ds(row, GROUP), lanes] = high
    ref[at, pl.ds(ref.shape[1] // 2 + row, GROUP), lanes] = low


def parts(first_ref, second_ref, k):
    half = first_ref.shape[1] // 2
    high = jnp.concatenate([first_ref[k, 0:half, :], second_ref[k, 0:half, :]], axis=0)
    low = jnp.concatenate([first_ref[k, half : 2 * half, :], second_ref[k, half : 2 * half, :]], axis=0)
    return high, low


def dots_uv(us, vs, acc_ref):
    def step(k, carry):
        v_high, v_low = parts(*vs, k)
        left = jnp.concatenate([v_high, *parts(*us, k)], axis=0)
        right = jnp.concatenate([v_low, v_high], axis=0)
        acc_ref[...] += lax.dot_general(left, right, NT, preferred_element_type=F32)
        return carry

    lax.fori_loop(0, us[0].shape[0], step, 0, unroll=6)


def dots_uu(us, acc_ref):
    def step(k, carry):
        high, low = parts(*us, k)
        right = jnp.concatenate([high, low], axis=0)
        acc_ref[...] += lax.dot_general(high, right, NT, preferred_element_type=F32)
        return carry

    lax.fori_loop(0, us[0].shape[0], step, 0, unroll=6)


def start_window(src_ref, window_ref, sems):
    copies = []
    for group in range(src_ref.shape[0] // GROUP):
        some = pl.ds(group * GROUP, GROUP)
        layers = pl.ds(lax.axis_index("col"), 3)
        copies.append(pltpu.make_async_copy(src_ref.at[some, :, layers], window_ref.at[some], sems.at[group]))
        copies[-1].start()
    return copies


def maps(mask_ref, material_ref, table_ref, keep_ref, scale_ref, root_ref):
    core = lax.axis_index("col")
    for place_, layer in enumerate((core + 1, 3 * core)):
        root = jnp.sqrt(lookup(material_ref[layer], table_ref))
        root_ref[place_] = root
        for comp in range(3):
            scale_ref[place_, comp] = mask_ref[comp, layer].astype(F32) / root
    for layer in range(3):
        for comp in range(3):
            keep_ref[comp, layer] = mask_ref[comp, core + layer].astype(F32)


def ahead(field, axis):
    size = field.shape[axis]
    at = lax.broadcasted_iota(jnp.int32, field.shape, axis)
    return jnp.where(at == size - 1, 0.0, pltpu.roll(field, size - 1, axis)) - field


def behind(field, axis):
    at = lax.broadcasted_iota(jnp.int32, field.shape, axis)
    return jnp.where(at == 0, 0.0, pltpu.roll(field, 1, axis)) - field


UNROLL = 4


def columns(copies, window_ref, base, keep_ref, scale_ref, root_ref, tmp_ref, near_ref, edge_u, mid_u, mid_v):
    upper = lax.axis_index("col") == 1
    ny, nx = window_ref.shape[3:]
    for group in range(window_ref.shape[0] // GROUP):
        if copies:
            copies[group].wait()

        def body(j, carry):
            def e(comp, layer):
                return window_ref[group * GROUP + j, comp, base + layer] * keep_ref[comp, layer]

            rows = pl.ds(pl.multiple_of(j * ny, ny), ny)

            def store(kind, values):
                for comp, value in enumerate(values):
                    tmp_ref[kind, comp, rows, :] = value

            x0, y0, z0 = (e(comp, 0) for comp in range(3))
            x1, y1, z1 = (e(comp, 1) for comp in range(3))
            x2, y2, z2 = (e(comp, 2) for comp in range(3))
            h01x = ahead(z0, 0) - (y1 - y0)
            h01y = (x1 - x0) - ahead(z0, 1)
            h12x = ahead(z1, 0) - (y2 - y1)
            h12y = (x2 - x1) - ahead(z1, 1)
            h1z = ahead(y1, 1) - ahead(x1, 0)
            store(0, (
                ((h01y - h12y) - behind(h1z, 0)) * scale_ref[0, 0],
                (behind(h1z, 1) - (h01x - h12x)) * scale_ref[0, 1],
                (behind(h12x, 0) - behind(h12y, 1)) * scale_ref[0, 2],
            ))
            store(1, (value * root_ref[0] for value in (x1, y1, z1)))
            xb, yb, zb = (jnp.where(upper, up, low) for up, low in ((x2, x0), (y2, y0), (z2, z0)))
            hbz = ahead(yb, 1) - ahead(xb, 0)
            lowx = jnp.where(upper, h12x, -yb)
            lowy = jnp.where(upper, h12y, xb)
            topx = jnp.where(upper, ahead(zb, 0) + yb, h01x)
            topy = jnp.where(upper, -xb - ahead(zb, 1), h01y)
            store(2, (
                ((lowy - topy) - behind(hbz, 0)) * scale_ref[1, 0],
                (behind(hbz, 1) - (lowx - topx)) * scale_ref[1, 1],
                (behind(topx, 0) - behind(topy, 1)) * scale_ref[1, 2],
            ))
            store(3, (value * root_ref[1] for value in (xb, yb, zb)))
            return carry

        lax.fori_loop(0, GROUP, body, 0, unroll=UNROLL)
        row = group * GROUP
        for comp in range(3):
            for y in range(ny):
                v, u, near, edge = (tmp_ref[kind, comp, pl.ds(y, GROUP, stride=ny), :] for kind in range(4))
                put(mid_v, row, comp, y, ny, v)
                put(mid_u, row, comp, y, ny, u)
                near_ref[comp, y, pl.ds(row, GROUP), :] = near
                put(edge_u, row, comp, y, ny, edge)


def mine_kernel(
    src_ref, mask_ref, material_ref, table_ref,
    near_ref, edge_u, mid_u, mid_v, mass_ref, window_ref, keep_ref, scale_ref, root_ref, tmp_ref, sems,
):
    copies = start_window(src_ref, window_ref, sems)
    maps(mask_ref, material_ref, table_ref, keep_ref, scale_ref, root_ref)
    mass_ref[...] = mask_ref[...].astype(F32) * lookup(material_ref[...], table_ref)[None]
    columns(copies, window_ref, 0, keep_ref, scale_ref, root_ref, tmp_ref, near_ref, edge_u, mid_u, mid_v)


def theirs_kernel(
    src_ref, mask_ref, material_ref, table_ref, own_edge_u, own_mid_u, own_mid_v,
    near_ref, edge_u, acc_v_ref, acc_u_ref, keep_ref, scale_ref, root_ref, tmp_ref, mid_u, mid_v,
):
    maps(mask_ref, material_ref, table_ref, keep_ref, scale_ref, root_ref)
    acc_v_ref[...] = jnp.zeros_like(acc_v_ref)
    acc_u_ref[...] = jnp.zeros_like(acc_u_ref)
    columns(None, src_ref, lax.axis_index("col"), keep_ref, scale_ref, root_ref, tmp_ref, near_ref, edge_u, mid_u, mid_v)
    dots_uv((own_mid_u, mid_u), (own_mid_v, mid_v), acc_v_ref)
    dots_uu((own_mid_u, mid_u), acc_u_ref)
    dots_uu((own_edge_u, edge_u), acc_u_ref)


def common(block, mask):
    ncol, _, nz, ny, nx = block.shape
    near = jax.ShapeDtypeStruct((3, ny, ncol, nx), F32)
    operand = jax.ShapeDtypeStruct((3 * ny * nx // LANES, 2 * ncol, LANES), BF16)
    scratch = [
        pltpu.VMEM((ncol, 3, 3, ny, nx), F32),
        pltpu.VMEM((3, 3, ny, nx), F32),
        pltpu.VMEM((2, 3, ny, nx), F32),
        pltpu.VMEM((2, ny, nx), F32),
        pltpu.VMEM((4, 3, GROUP * ny, nx), F32),
    ]
    return near, operand, scratch, pltpu.SemaphoreType.DMA((ncol // GROUP,))


def mine(block, mask, material, table):
    near, operand, scratch, sems = common(block, mask)
    return pl.pallas_call(
        mine_kernel,
        out_shape=(near, operand, operand, operand, jax.ShapeDtypeStruct(mask.shape, F32)),
        in_specs=[HBM, VMEM, VMEM, SMEM],
        out_specs=[VMEM] * 5,
        scratch_shapes=scratch + [sems],
        compiler_params=pltpu.CompilerParams(vmem_limit_bytes=OWN_LIMIT * MIB),
        cost_estimate=pl.CostEstimate(flops=10**8, bytes_accessed=8 * 10**6, transcendentals=0),
    )(block, mask, material, table)


def theirs(other, mask, material, table, own_edge_u, own_mid_u, own_mid_v):
    ncol = other.shape[0]
    near, operand, scratch, _ = common(other, mask)
    return pl.pallas_call(
        theirs_kernel,
        out_shape=(
            near, operand,
            jax.ShapeDtypeStruct((6 * ncol, 4 * ncol), F32),
            jax.ShapeDtypeStruct((2 * ncol, 4 * ncol), F32),
        ),
        in_specs=[VMEM, VMEM, VMEM, SMEM, VMEM, VMEM, VMEM],
        out_specs=[VMEM] * 4,
        scratch_shapes=scratch[1:] + [pltpu.VMEM(operand.shape, BF16), pltpu.VMEM(operand.shape, BF16)],
        compiler_params=pltpu.CompilerParams(vmem_limit_bytes=OTHER_LIMIT * MIB),
        cost_estimate=pl.CostEstimate(flops=2 * 10**9, bytes_accessed=8 * 10**6, transcendentals=0),
    )(other, mask, material, table, own_edge_u, own_mid_u, own_mid_v)


def pack(ga, gb, gf, side, half):
    rows = slice(side * half, (side + 1) * half)
    near = slice(side * half, (side + 1) * half)
    far = slice((1 - side) * half, (2 - side) * half)
    down = lax.broadcasted_iota(jnp.int32, (half, half), 0)
    across = lax.broadcasted_iota(jnp.int32, (half, half), 1)
    aa, ba, fa = (gram[rows, near] for gram in (ga, gb, gf))
    diag = jnp.sum(jnp.where(down == across, ba, 0.0), axis=1, keepdims=True)
    mixed = jnp.where(across <= down, aa, ba)
    wide = jnp.broadcast_to(diag, (half, 256 - 5 * half))
    return jnp.concatenate([mixed, fa, ga[rows, far], gb[rows, far], gf[rows, far], wide], axis=1)


def halo_rows(near_ref, halo_ref, mask_ref, material_ref, table_ref, scale_ref, out_ref):
    core = lax.axis_index("col")
    ny, nx = mask_ref.shape[2:]
    half = near_ref.shape[2]
    root = jnp.sqrt(lookup(material_ref[3 * core], table_ref))
    for comp in range(3):
        scale_ref[comp] = mask_ref[comp, 3 * core].astype(F32) / root
    scale_ref[2] = scale_ref[2] * core.astype(F32)
    for group in range(half // GROUP):
        row = group * GROUP
        rows = pl.ds(row, GROUP)
        h1_last = None
        for y in range(ny):
            h0 = halo_ref[0, y, rows, :]
            h1 = halo_ref[1, y, rows, :]
            change = (h0, h1, minus(h1_last, h1) + behind_x(h0))
            for comp in range(3):
                value = near_ref[comp, y, rows, :] - change[comp] * scale_ref[comp, y : y + 1, :]
                put(out_ref, row, comp, y, ny, value)
            h1_last = h1


def own_kernel(near_ref, halo_ref, mask_ref, material_ref, table_ref, out_ref, scale_ref):
    halo_rows(near_ref, halo_ref, mask_ref, material_ref, table_ref, scale_ref, out_ref)


def own_rows(near, halo, mask, material, table):
    _, ny, half, nx = near.shape
    return pl.pallas_call(
        own_kernel,
        out_shape=jax.ShapeDtypeStruct((3 * ny * nx // LANES, 2 * half, LANES), BF16),
        in_specs=[VMEM, VMEM, VMEM, VMEM, SMEM],
        out_specs=VMEM,
        scratch_shapes=[pltpu.VMEM((3, ny, nx), F32)],
        compiler_params=pltpu.CompilerParams(vmem_limit_bytes=16 * MIB),
        cost_estimate=pl.CostEstimate(flops=10**7, bytes_accessed=10**6, transcendentals=0),
    )(near, halo, mask, material, table)


def finish_kernel(
    near_ref, halo_ref, mask_ref, material_ref, table_ref, own_v, own_u, other_u, acc_v_ref, acc_u_ref,
    keep_rows_ref, send_rows_ref, scale_ref, other_v, sum_v,
):
    half = near_ref.shape[2]
    n = 2 * half
    halo_rows(near_ref, halo_ref, mask_ref, material_ref, table_ref, scale_ref, other_v)
    sum_v[...] = acc_v_ref[...]
    dots_uv((own_u, other_u), (own_v, other_v), sum_v)
    cross = sum_v[0:n, 0:n]
    gf = sum_v[0:n, n : 2 * n] + (cross + cross.T)
    cross = acc_u_ref[:, n : 2 * n]
    gb = acc_u_ref[:, 0:n] + (cross + cross.T)
    rows = sum_v[n : 2 * n, :] + sum_v[2 * n : 3 * n, :]
    ga = rows[:, 0:n] + rows[:, n : 2 * n]
    keep_rows_ref[...] = pack(ga, gb, gf, 0, half)
    send_rows_ref[...] = pack(ga, gb, gf, 1, half)


def finish(near, halo, mask, material, table, own_v, own_u, other_u, acc_v, acc_u):
    _, ny, half, nx = near.shape
    rows = jax.ShapeDtypeStruct((half, 256), F32)
    return pl.pallas_call(
        finish_kernel,
        out_shape=(rows, rows),
        in_specs=[VMEM, VMEM, VMEM, VMEM, SMEM] + [VMEM] * 5,
        out_specs=[VMEM, VMEM],
        scratch_shapes=[
            pltpu.VMEM((3, ny, nx), F32),
            pltpu.VMEM(own_v.shape, BF16),
            pltpu.VMEM(acc_v.shape, F32),
        ],
        compiler_params=pltpu.CompilerParams(vmem_limit_bytes=24 * MIB),
    )(near, halo, mask, material, table, own_v, own_u, other_u, acc_v, acc_u)


def image_kernel(first, block_ref, one_ref, two_ref, mask_ref, image_ref, keep_ref):
    upper = lax.axis_index("col") == 1
    ncol, _, nz, ny, nx = block_ref.shape
    keep_ref[...] = mask_ref[...].astype(F32)
    ones = one_ref.reshape(2 * ny * ncol, nx)
    twos = two_ref.reshape(2 * ny * ncol, nx)

    def body(j, carry):
        col = first + j

        def e(comp, layer):
            return block_ref[col, comp, layer] * keep_ref[comp, layer]

        at0 = pl.ds(col, ny, stride=ncol)
        at1 = pl.ds(ny * ncol + col, ny, stride=ncol)
        one0, one1, two0, two1 = ones[at0, :], ones[at1, :], twos[at0, :], twos[at1, :]
        x, y, z = (e(comp, 0) for comp in range(3))
        lowy = x - jnp.where(upper, two0, one0)
        lowx = jnp.where(upper, two1, one1) - y
        for layer in range(nz):
            if layer + 1 < nz:
                xn, yn, zn = (e(comp, layer + 1) for comp in range(3))
            else:
                xn, yn, zn = jnp.where(upper, one0, two0), jnp.where(upper, one1, two1), None
            topx = ahead(z, 0) - (yn - y)
            topy = (xn - x) - ahead(z, 1)
            hz = ahead(y, 1) - ahead(x, 0)
            image_ref[j, 0, layer] = ((lowy - topy) - behind(hz, 0)) * keep_ref[0, layer]
            image_ref[j, 1, layer] = (behind(hz, 1) - (lowx - topx)) * keep_ref[1, layer]
            image_ref[j, 2, layer] = (behind(topx, 0) - behind(topy, 1)) * keep_ref[2, layer]
            x, y, z, lowx, lowy = xn, yn, zn, topx, topy
        return carry

    lax.fori_loop(0, image_ref.shape[0], body, 0, unroll=4)


def image_of(block, one, two, mask, first, count):
    _, _, nz, ny, nx = block.shape
    return pl.pallas_call(
        functools.partial(image_kernel, first),
        out_shape=jax.ShapeDtypeStruct((count,) + block.shape[1:], F32),
        in_specs=[VMEM] * 4,
        out_specs=VMEM,
        scratch_shapes=[pltpu.VMEM((3, nz, ny, nx), F32)],
        compiler_params=pltpu.CompilerParams(vmem_limit_bytes=16 * MIB),
        cost_estimate=pl.CostEstimate(flops=10**7, bytes_accessed=3 * 10**6, transcendentals=0),
    )(block, one, two, mask)


PARTS = 3
PIECES = 12


def residual_kernel(
    scale, rows_ref, block_ref, image0_ref, image1_ref, image2_ref, mass_ref,
    out_ref, ga_ref, gb_ref, gf_ref, theta_ref, buffer, sems,
):
    swap = lax.axis_index("col") == 1
    half, total = ga_ref.shape
    down = lax.broadcasted_iota(jnp.int32, (half, half), 0)
    across = lax.broadcasted_iota(jnp.int32, (half, half), 1)
    rows = rows_ref[...] * scale
    mixed, fa, ab, bb, fb = (rows[:, k * half : (k + 1) * half] for k in range(5))
    diag_b = rows[:, 5 * half : 5 * half + 1]
    diag_a = jnp.sum(jnp.where(down == across, mixed, 0.0), axis=1, keepdims=True)
    theta_ref[...] = jnp.broadcast_to(diag_a / diag_b, theta_ref.shape)
    ncol = block_ref.shape[0]
    per = ncol // PIECES
    images = (image0_ref, image1_ref, image2_ref)
    copies = []
    for piece in range(PIECES):
        part, start = divmod(piece * per, ncol // PARTS)
        for j in range(per):
            col = piece * per + j
            theta = theta_ref[col : col + 1, :]
            buffer[col] = images[part][start + j] - theta[None, None] * (mass_ref[...] * block_ref[col])
        some = pl.ds(piece * per, per)
        copies.append(pltpu.make_async_copy(buffer.at[some], out_ref.at[some], sems.at[piece]))
        copies[-1].start()
    flat = mixed.T
    aa = jnp.where(across <= down, mixed, flat)
    ba = jnp.where(across == down, diag_b, jnp.where(across > down, mixed, flat))
    for ref, a, b in ((ga_ref, aa, ab), (gb_ref, ba, bb), (gf_ref, fa, fb)):
        ref[...] = jnp.concatenate([jnp.where(swap, b, a), jnp.where(swap, a, b)], axis=1)
    for copy in copies:
        copy.wait()


def residual_of(rows, block, images, mass, scale):
    ncol, _, nz, ny, nx = block.shape
    gram = jax.ShapeDtypeStruct((ncol, 2 * ncol), F32)
    return pl.pallas_call(
        functools.partial(residual_kernel, scale),
        out_shape=(jax.ShapeDtypeStruct(block.shape, F32), gram, gram, gram),
        in_specs=[VMEM] * (PARTS + 3),
        out_specs=[HBM] + [VMEM] * 3,
        scratch_shapes=[
            pltpu.VMEM((ncol, nx), F32),
            pltpu.VMEM(block.shape, F32),
            pltpu.SemaphoreType.DMA((PIECES,)),
        ],
        compiler_params=pltpu.CompilerParams(vmem_limit_bytes=24 * MIB),
        cost_estimate=pl.CostEstimate(flops=2 * 10**7, bytes_accessed=15 * 10**6, transcendentals=0),
    )(rows, block, *images, mass)


def exchange_rounds(slabs):
    nz, ny, nx = GRIDS[slabs]

    def partners(size, stride, flip):
        return [i + ((i // stride % size) ^ flip) * stride - i // stride % size * stride for i in range(slabs)]

    def flips(size):
        return (1, 2, 3) if size >= 4 else (1,)

    x, y, z = ([partners(size, stride, flip) for flip in flips(size)] for size, stride in ((nx, 1), (ny, nx), (nz, nx * ny)))
    stages = [(x, y), (y, x), (z, z)]
    if nz == 8:
        halves = [partners(nz, nx * ny, 7)]
        stages.append((halves, halves))
    return [
        [
            [(2 * i, 2 * a[i]) for i in range(slabs)] + [(2 * i + 1, 2 * b[i] + 1) for i in range(slabs)]
            for a, b in zip(first, second)
        ]
        for first, second in stages
    ]


def shards(block, material, table, mask):
    slabs = lax.axis_size("space")
    ncol, _, nz, ny, nx = block.shape
    scale = 1.0 / (3.0 * nz * slabs * ny * nx)
    swap = [(0, 1), (1, 0)]
    both = ("space", "col")
    other = lax.ppermute(block, "col", swap)
    one, two = edges(block, mask)
    straight = [pair for i in range(slabs) for pair in ((2 * i, 2 * ((i + 1) % slabs)), (2 * ((i + 1) % slabs) + 1, 2 * i + 1))]
    crossed = [pair for i in range(slabs) for pair in ((2 * i + 1, 2 * ((i + 1) % slabs)), (2 * ((i + 1) % slabs), 2 * i + 1))]
    halo_own = lax.ppermute(one, both, straight)
    halo_other = lax.ppermute(two, both, crossed)
    near_own, own_u, *mid, mass = mine(block, mask, material, table)
    near_other, other_u, acc_v, acc_u = theirs(other, mask, material, table, own_u, *mid)
    near_own, near_other, halo_own, halo_other = lax.optimization_barrier((near_own, near_other, halo_own, halo_other))
    own_v = own_rows(near_own, halo_own, mask, material, table)
    keep_rows, send_rows = finish(near_other, halo_other, mask, material, table, own_v, own_u, other_u, acc_v, acc_u)
    rows = keep_rows + lax.ppermute(send_rows, "col", swap)
    rows, halo_other = lax.optimization_barrier((rows, halo_other))
    halo_far = lax.ppermute(halo_other, "col", swap)
    images = []
    for index, stage in enumerate(exchange_rounds(slabs)):
        arrived = [lax.ppermute(rows, both, pairs) for pairs in stage]
        if index >= 1:
            rows, halo_far = lax.optimization_barrier((rows, halo_far))
            count = ncol // PARTS
            image = image_of(block, halo_own, halo_far, mask, (index - 1) * count, count)
            arrived, image = lax.optimization_barrier((arrived, image))
            images.append(image)
        rows = rows + arrived[0]
        if len(arrived) == 3:
            rows = rows + (arrived[1] + arrived[2])
    return residual_of(rows, block, images, mass, scale)


def solution(mesh):
    in_specs = (
        P("col", None, "space", None, None),
        P("space", None, None),
        P(),
        P(None, "space", None, None),
    )
    out_specs = (
        P("col", None, "space", None, None),
        P("col", None),
        P("col", None),
        P("col", None),
    )
    return jax.shard_map(shards, mesh=mesh, in_specs=in_specs, out_specs=out_specs, check_vma=False)
```

time: 77.3 us -> 73.4 us (0.950)
  the two profiles are of different devices: /device:TPU:32 before, /device:TPU:8 now
where the time goes in v3:
time: 73.4 us; the launch traced here: 73.3 us
  Pallas kernels  27.4 us (37%)
  starting transfers between devices  24.1 us (33%)
  waiting for transfers between devices  19.9 us (27%)
  between operations  0.96 us (1%)
  local copies, waits for them, and re-layouts  0.91 us (1%)
    ppermute x10, starting transfers between devices, shards(): arrived = [lax.ppermute(rows, both, pairs) for pairs in stage]  20.3 us
    ppermute x10, waiting for transfers between devices, shards(): arrived = [lax.ppermute(rows, both, pairs) for pairs in stage]  14 us
    pallas_call x1, Pallas kernels, theirs(): pl.pallas_call(theirs_kernel, out_shape=(near, operand, jax.ShapeDtypeStr...  8.41 us
    pallas_call x1, Pallas kernels, mine(): pl.pallas_call(mine_kernel, out_shape=(near, operand, operand, operand, j...  6.02 us
    ppermute x1, waiting for transfers between devices, shards(): halo_own = lax.ppermute(one, both, straight)  3.85 us
    pallas_call x3, Pallas kernels, image_of(): pl.pallas_call(functools.partial(image_kernel, first), out_shape=jax.Shap...  3.58 us
    pallas_call x1, Pallas kernels, residual_of(): pl.pallas_call(functools.partial(residual_kernel, scale), out_shape=(jax....  3.42 us
    pallas_call x1, Pallas kernels, finish(): pl.pallas_call(finish_kernel, out_shape=(rows, rows), in_specs=[VMEM, VME...  2.89 us
  transfers between devices with their start and end apart: 15, of which 9 were waited for; matrix products, arithmetic and copies ran while one was open for 0% of the time, Pallas kernels for 27%

profile of v3, /device:TPU:8, one launch (start us, length us, event | category | flops | bytes accessed | tf_op | source)
XLA Modules:
  0.0 73.3 jit_solution(14664124314554788379)
XLA Ops:
  1.6 2.1 %shard_map.77 = (f32[2,16,48,128]{3,2,1,0:T(8,128)S(1)}, f32[2,16,48,128]{3,2,1,0:T(8,128)S(1)}) custom-call(f32[48,3,4,16,128]{4,3,2,1,0:T(8,128)} %block_ref.9, s32[3,4,16,128]{3,2,1,0:T(8,128)S(1)} %copy-done), custom_call_target="tpu_custom_call" | custom-call | tf_op jit(solution)/shard_map/pallas_call | solution.py:108
  3.8 1.6 %collective-permute-start.1 = (f32[2,16,48,128]{3,2,1,0:T(8,128)S(1)}, f32[2,16,48,128]{3,2,1,0:T(8,128)S(1)}, u32[]{:S(2)}, u32[]{:S(2)}) collective-permute-start(f32[2,16,48,128]{3,2,1,0:T(8,128)S(1)} %get-tuple-element.44), channel_id=1, source_target_pairs={{0,2},{3,1},{2,4},{5,3},{4,6},{7,5},{6,8},{9,7},{8,10},{11,9},{10,... | collective-permute-start | bytes 2359304 | tf_op jit(solution)/shard_map/ppermute | solution.py:551
  5.3 1.8 %collective-permute-start.2 = (f32[2,16,48,128]{3,2,1,0:T(8,128)S(1)}, f32[2,16,48,128]{3,2,1,0:T(8,128)S(1)}, u32[]{:S(2)}, u32[]{:S(2)}) collective-permute-start(f32[2,16,48,128]{3,2,1,0:T(8,128)S(1)} %get-tuple-element.45), channel_id=1, source_target_pairs={{1,2},{2,1},{3,4},{4,3},{5,6},{6,5},{7,8},{8,7},{9,10},{10,9},{11,... | collective-permute-start | bytes 2359304 | tf_op jit(solution)/shard_map/ppermute | solution.py:552
  7.2 6.0 %shard_map.75 = (f32[3,16,48,128]{3,2,1,0:T(8,128)S(1)}, bf16[12,96,512]{2,1,0:T(8,128)(2,1)S(1)}, bf16[12,96,512]{2,1,0:T(8,128)(2,1)S(1)}, bf16[12,96,512]{2,1,0:T(8,128)(2,1)S(1)}, f32[3,4,16,128]{3,2,1,0:T(8,128)S(1)}) custom-call(f32[48,3,4,16,128]{4,3,2,1,0:T(8,128)} %block_ref.9, s32[3,4,16,128]{3,2,1,0:T(8,128)S(1)} %copy-done.1, ...), custom_call_target="tpu_custom_call" | custom-call | flops 100000000 | bytes 8000000 | tf_op jit(solution)/shard_map/pallas_call | solution.py:295
  13.2 8.4 %shard_map.76 = (f32[3,16,48,128]{3,2,1,0:T(8,128)S(1)}, bf16[12,96,512]{2,1,0:T(8,128)(2,1)S(1)}, f32[288,192]{1,0:T(8,128)S(1)}, f32[96,192]{1,0:T(8,128)S(1)}) custom-call(f32[48,3,4,16,128]{4,3,2,1,0:T(8,128)S(1)} %collective-permute-done.src_ref, s32[3,4,16,128]{3,2,1,0:T(8,128)S(1)} %copy-done.1, s32[4,16,128]{2,1,0:T(8,128)S(1)} %copy-done.2, ...), custom_call_target="tpu_custom_call" | custom-call | flops 2000000000 | bytes 8000000 | tf_op jit(solution)/shard_map/pallas_call | solution.py:309
  21.6 3.8 %collective-permute-done.1.halo_ref.one_ref = f32[2,16,48,128]{3,2,1,0:T(8,128)S(1)} collective-permute-done((f32[2,16,48,128]{3,2,1,0:T(8,128)S(1)}, f32[2,16,48,128]{3,2,1,0:T(8,128)S(1)}, u32[]{:S(2)}, u32[]{:S(2)}) %collective-permute-start.1) | collective-permute-done | bytes 786464 | tf_op jit(solution)/shard_map/ppermute | solution.py:551
  27.3 2.9 %shard_map.79 = (f32[48,256]{1,0:T(8,128)S(1)}, f32[48,256]{1,0:T(8,128)S(1)}) custom-call(f32[3,16,48,128]{3,2,1,0:T(8,128)S(1)} %get-tuple-element.46.near_ref, f32[2,16,48,128]{3,2,1,0:T(8,128)S(1)} %collective-permute-done.2.halo_ref, s32[3,4,16,128]{3,2,1,0:T(8,128)S(1)} %copy-done.1, s32[4,16,128]{2,1,0:T(8,128)S(1)} %copy-done.2, f32[8]{0:T(128)S(1)} %copy-done.3, ...), custom_call_target="tpu_custom_call" | custom-call | tf_op jit(solution)/shard_map/pallas_call | solution.py:398
  30.3 1.2 %collective-permute-done.3 = f32[48,256]{1,0:T(8,128)S(1)} collective-permute-done((f32[48,256]{1,0:T(8,128)S(1)}, f32[48,256]{1,0:T(8,128)S(1)}, u32[]{:S(2)}, u32[]{:S(2)}) %collective-permute-start.3) | collective-permute-done | bytes 49184 | tf_op jit(solution)/shard_map/ppermute | solution.py:558
  31.7 3.4 %collective-permute-start.5 = (f32[48,256]{1,0:T(8,128)S(1)}, f32[48,256]{1,0:T(8,128)S(1)}, u32[]{:S(2)}, u32[]{:S(2)}) collective-permute-start(f32[48,256]{1,0:T(8,128)S(1)} %add.33), channel_id=1, source_target_pairs={{0,4},{2,6},{4,0},{6,2},{8,12},{10,14},{12,8},{14,10},{16,20},{18,... | collective-permute-start | bytes 147464 | tf_op jit(solution)/shard_map/ppermute | solution.py:563
  35.2 1.2 %collective-permute-start.6 = (f32[48,256]{1,0:T(8,128)S(1)}, f32[48,256]{1,0:T(8,128)S(1)}, u32[]{:S(2)}, u32[]{:S(2)}) collective-permute-start(f32[48,256]{1,0:T(8,128)S(1)} %add.33), channel_id=1, source_target_pairs={{0,6},{2,4},{4,2},{6,0},{8,14},{10,12},{12,10},{14,8},{16,22},{18,... | collective-permute-start | bytes 147464 | tf_op jit(solution)/shard_map/ppermute | solution.py:563
  36.4 1.3 %collective-permute-done.5 = f32[48,256]{1,0:T(8,128)S(1)} collective-permute-done((f32[48,256]{1,0:T(8,128)S(1)}, f32[48,256]{1,0:T(8,128)S(1)}, u32[]{:S(2)}, u32[]{:S(2)}) %collective-permute-start.5) | collective-permute-done | bytes 49184 | tf_op jit(solution)/shard_map/ppermute | solution.py:563
  37.8 2.7 %collective-permute-done.6 = f32[48,256]{1,0:T(8,128)S(1)} collective-permute-done((f32[48,256]{1,0:T(8,128)S(1)}, f32[48,256]{1,0:T(8,128)S(1)}, u32[]{:S(2)}, u32[]{:S(2)}) %collective-permute-start.6) | collective-permute-done | bytes 49184 | tf_op jit(solution)/shard_map/ppermute | solution.py:563
  40.5 1.7 %collective-permute-start.10 = (f32[48,256]{1,0:T(8,128)S(1)}, f32[48,256]{1,0:T(8,128)S(1)}, u32[]{:S(2)}, u32[]{:S(2)}) collective-permute-start(f32[48,256]{1,0:T(8,128)S(1)} %add_add_fusion.2), channel_id=1, source_target_pairs={{0,24},{2,26},{4,28},{6,30},{8,16},{10,18},{12,20},{14,22},{16,8},... | collective-permute-start | bytes 147464 | tf_op jit(solution)/shard_map/ppermute | solution.py:563
  42.2 4.0 %collective-permute-start.8 = (f32[48,256]{1,0:T(8,128)S(1)}, f32[48,256]{1,0:T(8,128)S(1)}, u32[]{:S(2)}, u32[]{:S(2)}) collective-permute-start(f32[48,256]{1,0:T(8,128)S(1)} %add_add_fusion.2), channel_id=1, source_target_pairs={{0,8},{2,10},{4,12},{6,14},{8,0},{10,2},{12,4},{14,6},{16,24},{18,... | collective-permute-start | bytes 147464 | tf_op jit(solution)/shard_map/ppermute | solution.py:563
  46.2 1.3 %collective-permute-start.9 = (f32[48,256]{1,0:T(8,128)S(1)}, f32[48,256]{1,0:T(8,128)S(1)}, u32[]{:S(2)}, u32[]{:S(2)}) collective-permute-start(f32[48,256]{1,0:T(8,128)S(1)} %add_add_fusion.2), channel_id=1, source_target_pairs={{0,16},{2,18},{4,20},{6,22},{8,24},{10,26},{12,28},{14,30},{16,0},... | collective-permute-start | bytes 147464 | tf_op jit(solution)/shard_map/ppermute | solution.py:563
  47.5 1.2 %shard_map.80.image0_ref = f32[16,3,4,16,128]{4,3,2,1,0:T(8,128)S(1)} custom-call(f32[48,3,4,16,128]{4,3,2,1,0:T(8,128)S(1)} %bitcast.1, f32[2,16,48,128]{3,2,1,0:T(8,128)S(1)} %collective-permute-done.1.halo_ref.one_ref, f32[2,16,48,128]{3,2,1,0:T(8,128)S(1)} %collective-permute-done.7.two_ref, s32[3,4,16,128]{3,2,1,0:T(8,128)S(1)} %copy-done.1), custom_call_target="tpu_custom_call" | custom-call | flops 10000000 | bytes 3000000 | tf_op jit(solution)/shard_map/pallas_call | solution.py:450
  48.7 3.0 %collective-permute-done.9 = f32[48,256]{1,0:T(8,128)S(1)} collective-permute-done((f32[48,256]{1,0:T(8,128)S(1)}, f32[48,256]{1,0:T(8,128)S(1)}, u32[]{:S(2)}, u32[]{:S(2)}) %collective-permute-start.9) | collective-permute-done | bytes 49184 | tf_op jit(solution)/shard_map/ppermute | solution.py:563
  51.8 2.0 %collective-permute-start.11 = (f32[48,256]{1,0:T(8,128)S(1)}, f32[48,256]{1,0:T(8,128)S(1)}, u32[]{:S(2)}, u32[]{:S(2)}) collective-permute-start(f32[48,256]{1,0:T(8,128)S(1)} %add_add_fusion.1), channel_id=1, source_target_pairs={{0,32},{2,34},{4,36},{6,38},{8,40},{10,42},{12,44},{14,46},{16,48}... | collective-permute-start | bytes 147464 | tf_op jit(solution)/shard_map/ppermute | solution.py:563
  53.8 4.7 %collective-permute-start.12 = (f32[48,256]{1,0:T(8,128)S(1)}, f32[48,256]{1,0:T(8,128)S(1)}, u32[]{:S(2)}, u32[]{:S(2)}) collective-permute-start(f32[48,256]{1,0:T(8,128)S(1)} %add_add_fusion.1), channel_id=1, source_target_pairs={{0,64},{2,66},{4,68},{6,70},{8,72},{10,74},{12,76},{14,78},{16,80}... | collective-permute-start | bytes 147464 | tf_op jit(solution)/shard_map/ppermute | solution.py:563
  59.6 1.4 %collective-permute-done.12 = f32[48,256]{1,0:T(8,128)S(1)} collective-permute-done((f32[48,256]{1,0:T(8,128)S(1)}, f32[48,256]{1,0:T(8,128)S(1)}, u32[]{:S(2)}, u32[]{:S(2)}) %collective-permute-start.12) | collective-permute-done | bytes 49184 | tf_op jit(solution)/shard_map/ppermute | solution.py:563
  61.1 3.2 %collective-permute-done.13 = f32[48,256]{1,0:T(8,128)S(1)} collective-permute-done((f32[48,256]{1,0:T(8,128)S(1)}, f32[48,256]{1,0:T(8,128)S(1)}, u32[]{:S(2)}, u32[]{:S(2)}) %collective-permute-start.13) | collective-permute-done | bytes 49184 | tf_op jit(solution)/shard_map/ppermute | solution.py:563
  64.3 2.0 %collective-permute-start.14 = (f32[48,256]{1,0:T(8,128)S(1)}, f32[48,256]{1,0:T(8,128)S(1)}, u32[]{:S(2)}, u32[]{:S(2)}) collective-permute-start(f32[48,256]{1,0:T(8,128)S(1)} %add_add_fusion), channel_id=1, source_target_pairs={{0,224},{2,226},{4,228},{6,230},{8,232},{10,234},{12,236},{14,238}... | collective-permute-start | bytes 147464 | tf_op jit(solution)/shard_map/ppermute | solution.py:563
  67.5 2.2 %collective-permute-done.14 = f32[48,256]{1,0:T(8,128)S(1)} collective-permute-done((f32[48,256]{1,0:T(8,128)S(1)}, f32[48,256]{1,0:T(8,128)S(1)}, u32[]{:S(2)}, u32[]{:S(2)}) %collective-permute-start.14) | collective-permute-done | bytes 49184 | tf_op jit(solution)/shard_map/ppermute | solution.py:563
  69.7 3.4 %shard_map.83 = (f32[48,3,4,16,128]{4,3,2,1,0:T(8,128)}, f32[48,96]{1,0:T(8,128)}, f32[48,96]{1,0:T(8,128)}, f32[48,96]{1,0:T(8,128)}) custom-call(f32[48,256]{1,0:T(8,128)S(1)} %add.43.rows_ref, f32[48,3,4,16,128]{4,3,2,1,0:T(8,128)S(1)} %bitcast.1, f32[16,3,4,16,128]{4,3,2,1,0:T(8,128)S(1)} %shard_map.80.image0_ref, ...), custom_call_target="tpu_custom_call" | custom-call | flops 20000000 | bytes 15000000 | tf_op jit(solution)/shard_map/pallas_call | solution.py:503
  (33 shorter events, 5.6 us)
Async XLA Ops:
  0.6 12.6 %collective-permute-start = (f32[48,3,4,16,128]{4,3,2,1,0:T(8,128)}, f32[48,3,4,16,128]{4,3,2,1,0:T(8,128)S(1)}, u32[]{:S(2)}, u32[]{:S(2)}) collective-permute-start(f32[48,3,4,16,128]{4,3,2,1,0:T(8,128)} %block_ref.9), channel_id=1, source_target_pairs={{0,1},{1,0},{2,3},{3,2},{4,5},{5,4},{6,7},{7,6},{8,9},{9,8},{10,11... | collective-permute-start | bytes 14155784 | tf_op jit(solution)/shard_map/ppermute | solution.py:547
  0.7 0.9 %copy-start = (s32[3,4,16,128]{3,2,1,0:T(8,128)S(1)}, s32[3,4,16,128]{3,2,1,0:T(8,128)}, u32[]{:S(2)}) copy-start(s32[3,4,16,128]{3,2,1,0:T(8,128)} %mask_ref.15) | copy-start | bytes 294916
  1.6 5.5 %copy-start.1 = (s32[3,4,16,128]{3,2,1,0:T(8,128)S(1)}, s32[3,4,16,128]{3,2,1,0:T(8,128)}, u32[]{:S(2)}) copy-start(s32[3,4,16,128]{3,2,1,0:T(8,128)} %mask_ref.15) | copy-start | bytes 294916
  1.6 5.5 %copy-start.2 = (s32[4,16,128]{2,1,0:T(8,128)S(1)}, s32[4,16,128]{2,1,0:T(8,128)}, u32[]{:S(2)}) copy-start(s32[4,16,128]{2,1,0:T(8,128)} %material_ref.7) | copy-start | bytes 98308
  1.6 5.5 %copy-start.3 = (f32[8]{0:T(128)S(1)}, f32[8]{0:T(128)}, u32[]{:S(2)}) copy-start(f32[8]{0:T(128)} %table_ref.7) | copy-start | bytes 100
  3.8 21.7 %collective-permute-start.1 = (f32[2,16,48,128]{3,2,1,0:T(8,128)S(1)}, f32[2,16,48,128]{3,2,1,0:T(8,128)S(1)}, u32[]{:S(2)}, u32[]{:S(2)}) collective-permute-start(f32[2,16,48,128]{3,2,1,0:T(8,128)S(1)} %get-tuple-element.44), channel_id=1, source_target_pairs={{0,2},{3,1},{2,4},{5,3},{4,6},{7,5},{6,8},{9,7},{8,10},{11,9},{10,... | collective-permute-start | bytes 2359304 | tf_op jit(solution)/shard_map/ppermute | solution.py:551
  5.3 21.0 %collective-permute-start.2 = (f32[2,16,48,128]{3,2,1,0:T(8,128)S(1)}, f32[2,16,48,128]{3,2,1,0:T(8,128)S(1)}, u32[]{:S(2)}, u32[]{:S(2)}) collective-permute-start(f32[2,16,48,128]{3,2,1,0:T(8,128)S(1)} %get-tuple-element.45), channel_id=1, source_target_pairs={{1,2},{2,1},{3,4},{4,3},{5,6},{6,5},{7,8},{8,7},{9,10},{10,9},{11,... | collective-permute-start | bytes 2359304 | tf_op jit(solution)/shard_map/ppermute | solution.py:552
  13.2 34.3 %slice-start = ((s8[4718592]{0:T(1024)(128)(4,1)}), s8[524288]{0:T(1024)(128)(4,1)S(1)}, s32[]{:S(2)}) async-start(s8[4718592]{0:T(1024)(128)(4,1)} %bitcast), calls=%async_computation | async-start | bytes 1048576
  26.4 21.1 %slice-start.1 = ((s8[4718592]{0:T(1024)(128)(4,1)}), s8[4194304]{0:T(1024)(128)(4,1)S(1)}, s32[]{:S(2)}) async-start(s8[4718592]{0:T(1024)(128)(4,1)} %bitcast), calls=%async_computation.1 | async-start | bytes 8388608
  30.2 1.3 %collective-permute-start.3 = (f32[48,256]{1,0:T(8,128)S(1)}, f32[48,256]{1,0:T(8,128)S(1)}, u32[]{:S(2)}, u32[]{:S(2)}) collective-permute-start(f32[48,256]{1,0:T(8,128)S(1)} %get-tuple-element.54), channel_id=1, source_target_pairs={{0,1},{1,0},{2,3},{3,2},{4,5},{5,4},{6,7},{7,6},{8,9},{9,8},{10,11... | collective-permute-start | bytes 147464 | tf_op jit(solution)/shard_map/ppermute | solution.py:558
  31.5 16.0 %collective-permute-start.7 = (f32[2,16,48,128]{3,2,1,0:T(8,128)S(1)}, f32[2,16,48,128]{3,2,1,0:T(8,128)S(1)}, u32[]{:S(2)}, u32[]{:S(2)}) collective-permute-start(f32[2,16,48,128]{3,2,1,0:T(8,128)S(1)} %collective-permute-done.2.halo_ref), channel_id=1, source_target_pairs={{0,1},{1,0},{2,3},{3,2},{4,5},{5,4},{6,7},{7,6},{8,9},{9,8},{10,11... | collective-permute-start | bytes 2359304 | tf_op jit(solution)/shard_map/ppermute | solution.py:560
  31.7 4.7 %collective-permute-start.4 = (f32[48,256]{1,0:T(8,128)S(1)}, f32[48,256]{1,0:T(8,128)S(1)}, u32[]{:S(2)}, u32[]{:S(2)}) collective-permute-start(f32[48,256]{1,0:T(8,128)S(1)} %add.33), channel_id=1, source_target_pairs={{0,2},{2,0},{4,6},{6,4},{8,10},{10,8},{12,14},{14,12},{16,18},{18,... | collective-permute-start | bytes 147464 | tf_op jit(solution)/shard_map/ppermute | solution.py:563
  31.7 6.0 %collective-permute-start.5 = (f32[48,256]{1,0:T(8,128)S(1)}, f32[48,256]{1,0:T(8,128)S(1)}, u32[]{:S(2)}, u32[]{:S(2)}) collective-permute-start(f32[48,256]{1,0:T(8,128)S(1)} %add.33), channel_id=1, source_target_pairs={{0,4},{2,6},{4,0},{6,2},{8,12},{10,14},{12,8},{14,10},{16,20},{18,... | collective-permute-start | bytes 147464 | tf_op jit(solution)/shard_map/ppermute | solution.py:563
  35.2 5.3 %collective-permute-start.6 = (f32[48,256]{1,0:T(8,128)S(1)}, f32[48,256]{1,0:T(8,128)S(1)}, u32[]{:S(2)}, u32[]{:S(2)}) collective-permute-start(f32[48,256]{1,0:T(8,128)S(1)} %add.33), channel_id=1, source_target_pairs={{0,6},{2,4},{4,2},{6,0},{8,14},{10,12},{12,10},{14,8},{16,22},{18,... | collective-permute-start | bytes 147464 | tf_op jit(solution)/shard_map/ppermute | solution.py:563
  40.5 8.2 %collective-permute-start.10 = (f32[48,256]{1,0:T(8,128)S(1)}, f32[48,256]{1,0:T(8,128)S(1)}, u32[]{:S(2)}, u32[]{:S(2)}) collective-permute-start(f32[48,256]{1,0:T(8,128)S(1)} %add_add_fusion.2), channel_id=1, source_target_pairs={{0,24},{2,26},{4,28},{6,30},{8,16},{10,18},{12,20},{14,22},{16,8},... | collective-permute-start | bytes 147464 | tf_op jit(solution)/shard_map/ppermute | solution.py:563
  42.2 6.6 %collective-permute-start.8 = (f32[48,256]{1,0:T(8,128)S(1)}, f32[48,256]{1,0:T(8,128)S(1)}, u32[]{:S(2)}, u32[]{:S(2)}) collective-permute-start(f32[48,256]{1,0:T(8,128)S(1)} %add_add_fusion.2), channel_id=1, source_target_pairs={{0,8},{2,10},{4,12},{6,14},{8,0},{10,2},{12,4},{14,6},{16,24},{18,... | collective-permute-start | bytes 147464 | tf_op jit(solution)/shard_map/ppermute | solution.py:563
  46.2 5.6 %collective-permute-start.9 = (f32[48,256]{1,0:T(8,128)S(1)}, f32[48,256]{1,0:T(8,128)S(1)}, u32[]{:S(2)}, u32[]{:S(2)}) collective-permute-start(f32[48,256]{1,0:T(8,128)S(1)} %add_add_fusion.2), channel_id=1, source_target_pairs={{0,16},{2,18},{4,20},{6,22},{8,24},{10,26},{12,28},{14,30},{16,0},... | collective-permute-start | bytes 147464 | tf_op jit(solution)/shard_map/ppermute | solution.py:563
  51.8 7.9 %collective-permute-start.11 = (f32[48,256]{1,0:T(8,128)S(1)}, f32[48,256]{1,0:T(8,128)S(1)}, u32[]{:S(2)}, u32[]{:S(2)}) collective-permute-start(f32[48,256]{1,0:T(8,128)S(1)} %add_add_fusion.1), channel_id=1, source_target_pairs={{0,32},{2,34},{4,36},{6,38},{8,40},{10,42},{12,44},{14,46},{16,48}... | collective-permute-start | bytes 147464 | tf_op jit(solution)/shard_map/ppermute | solution.py:563
  53.8 7.3 %collective-permute-start.12 = (f32[48,256]{1,0:T(8,128)S(1)}, f32[48,256]{1,0:T(8,128)S(1)}, u32[]{:S(2)}, u32[]{:S(2)}) collective-permute-start(f32[48,256]{1,0:T(8,128)S(1)} %add_add_fusion.1), channel_id=1, source_target_pairs={{0,64},{2,66},{4,68},{6,70},{8,72},{10,74},{12,76},{14,78},{16,80}... | collective-permute-start | bytes 147464 | tf_op jit(solution)/shard_map/ppermute | solution.py:563
  58.4 5.9 %collective-permute-start.13 = (f32[48,256]{1,0:T(8,128)S(1)}, f32[48,256]{1,0:T(8,128)S(1)}, u32[]{:S(2)}, u32[]{:S(2)}) collective-permute-start(f32[48,256]{1,0:T(8,128)S(1)} %add_add_fusion.1), channel_id=1, source_target_pairs={{0,96},{2,98},{4,100},{6,102},{8,104},{10,106},{12,108},{14,110},{... | collective-permute-start | bytes 147464 | tf_op jit(solution)/shard_map/ppermute | solution.py:563
  64.3 5.4 %collective-permute-start.14 = (f32[48,256]{1,0:T(8,128)S(1)}, f32[48,256]{1,0:T(8,128)S(1)}, u32[]{:S(2)}, u32[]{:S(2)}) collective-permute-start(f32[48,256]{1,0:T(8,128)S(1)} %add_add_fusion), channel_id=1, source_target_pairs={{0,224},{2,226},{4,228},{6,230},{8,232},{10,234},{12,236},{14,238}... | collective-permute-start | bytes 147464 | tf_op jit(solution)/shard_map/ppermute | solution.py:563

commit v4 on v3

--- a/solution.py
+++ b/solution.py
@@ -521,21 +521,17 @@
     def partners(size, stride, flip):
         return [i + ((i // stride % size) ^ flip) * stride - i // stride % size * stride for i in range(slabs)]
 
-    def flips(size):
-        return (1, 2, 3) if size >= 4 else (1,)
-
-    x, y, z = ([partners(size, stride, flip) for flip in flips(size)] for size, stride in ((nx, 1), (ny, nx), (nz, nx * ny)))
-    stages = [(x, y), (y, x), (z, z)]
-    if nz == 8:
-        halves = [partners(nz, nx * ny, 7)]
-        stages.append((halves, halves))
-    return [
-        [
-            [(2 * i, 2 * a[i]) for i in range(slabs)] + [(2 * i + 1, 2 * b[i] + 1) for i in range(slabs)]
-            for a, b in zip(first, second)
-        ]
-        for first, second in stages
-    ]
+    def stage(first, second, flips):
+        exchanges = {}
+        for flip in flips:
+            a, b = (partners(size, stride, flip) for size, stride in (first, second))
+            exchanges[flip] = [(2 * i, 2 * a[i]) for i in range(slabs)] + [(2 * i + 1, 2 * b[i] + 1) for i in range(slabs)]
+        return exchanges
+
+    x, y, z = (nx, 1), (ny, nx), (nz, nx * ny)
+    if nx < 4:
+        return [stage(x, y, (1,)), stage(y, x, (1,)), stage(z, z, (1,))]
+    return [stage(x, y, (3, 2, 1)), stage(y, x, (2, 1, 3)), stage(z, z, (3, 2, 1)), stage(z, z, (7,))]
 
 
 def shards(block, material, table, mask):
@@ -552,7 +548,7 @@
     halo_other = lax.ppermute(two, both, crossed)
     near_own, own_u, *mid, mass = mine(block, mask, material, table)
     near_other, other_u, acc_v, acc_u = theirs(other, mask, material, table, own_u, *mid)
-    near_own, near_other, halo_own, halo_other = lax.optimization_barrier((near_own, near_other, halo_own, halo_other))
+    near_own, near_other, halo_own = lax.optimization_barrier((near_own, near_other, halo_own))
     own_v = own_rows(near_own, halo_own, mask, material, table)
     keep_rows, send_rows = finish(near_other, halo_other, mask, material, table, own_v, own_u, other_u, acc_v, acc_u)
     rows = keep_rows + lax.ppermute(send_rows, "col", swap)
@@ -560,16 +556,16 @@
     halo_far = lax.ppermute(halo_other, "col", swap)
     images = []
     for index, stage in enumerate(exchange_rounds(slabs)):
-        arrived = [lax.ppermute(rows, both, pairs) for pairs in stage]
+        arrived = {flip: lax.ppermute(rows, both, pairs) for flip, pairs in stage.items()}
         if index >= 1:
             rows, halo_far = lax.optimization_barrier((rows, halo_far))
             count = ncol // PARTS
             image = image_of(block, halo_own, halo_far, mask, (index - 1) * count, count)
             arrived, image = lax.optimization_barrier((arrived, image))
             images.append(image)
-        rows = rows + arrived[0]
+        rows = rows + (arrived[1] if 1 in arrived else arrived[7])
         if len(arrived) == 3:
-            rows = rows + (arrived[1] + arrived[2])
+            rows = rows + (arrived[2] + arrived[3])
     return residual_of(rows, block, images, mass, scale)
 
 

time: 73.4 us -> 72.5 us (0.988)
  waiting for transfers between devices: 19.9 us -> 18.4 us
    ppermute x1, waiting for transfers between devices: 0.9 us -> 0.01 us  [shards(): halo_other = lax.ppermute(two, both, crossed)]
  transfers between devices with their start and end apart: 15 -> 15, of which waited for: 9 -> 8; matrix products, arithmetic and copies ran while one was open for 0% -> 0% of each run, Pallas kernels for 27% -> 29%
where the time goes in v4:
time: 72.5 us; the launch traced here: 72.4 us
  Pallas kernels  27.4 us (38%)
  starting transfers between devices  24.7 us (34%)
  waiting for transfers between devices  18.4 us (25%)
  between operations  0.97 us (1%)
  local copies, waits for them, and re-layouts  0.91 us (1%)
    ppermute x10, starting transfers between devices, shards(): lax.ppermute(rows, both, pairs)  21 us
    ppermute x10, waiting for transfers between devices, shards(): lax.ppermute(rows, both, pairs)  13.3 us
    pallas_call x1, Pallas kernels, theirs(): pl.pallas_call(theirs_kernel, out_shape=(near, operand, jax.ShapeDtypeStr...  8.41 us
    pallas_call x1, Pallas kernels, mine(): pl.pallas_call(mine_kernel, out_shape=(near, operand, operand, operand, j...  6.02 us
    ppermute x1, waiting for transfers between devices, shards(): halo_own = lax.ppermute(one, both, straight)  3.85 us
    pallas_call x3, Pallas kernels, image_of(): pl.pallas_call(functools.partial(image_kernel, first), out_shape=jax.Shap...  3.58 us
    pallas_call x1, Pallas kernels, residual_of(): pl.pallas_call(functools.partial(residual_kernel, scale), out_shape=(jax....  3.42 us
    pallas_call x1, Pallas kernels, finish(): pl.pallas_call(finish_kernel, out_shape=(rows, rows), in_specs=[VMEM, VME...  2.89 us
  transfers between devices with their start and end apart: 15, of which 8 were waited for; matrix products, arithmetic and copies ran while one was open for 0% of the time, Pallas kernels for 29%

profile of v4, /device:TPU:8, one launch (start us, length us, event | category | flops | bytes accessed | tf_op | source)
XLA Modules:
  0.0 72.4 jit_solution(11512911804353623034)
XLA Ops:
  1.6 2.1 %shard_map.77 = (f32[2,16,48,128]{3,2,1,0:T(8,128)S(1)}, f32[2,16,48,128]{3,2,1,0:T(8,128)S(1)}) custom-call(f32[48,3,4,16,128]{4,3,2,1,0:T(8,128)} %block_ref.9, s32[3,4,16,128]{3,2,1,0:T(8,128)S(1)} %copy-done), custom_call_target="tpu_custom_call" | custom-call | tf_op jit(solution)/shard_map/pallas_call | solution.py:108
  3.8 1.6 %collective-permute-start.1 = (f32[2,16,48,128]{3,2,1,0:T(8,128)S(1)}, f32[2,16,48,128]{3,2,1,0:T(8,128)S(1)}, u32[]{:S(2)}, u32[]{:S(2)}) collective-permute-start(f32[2,16,48,128]{3,2,1,0:T(8,128)S(1)} %get-tuple-element.43), channel_id=1, source_target_pairs={{0,2},{3,1},{2,4},{5,3},{4,6},{7,5},{6,8},{9,7},{8,10},{11,9},{10,... | collective-permute-start | bytes 2359304 | tf_op jit(solution)/shard_map/ppermute | solution.py:547
  5.3 1.8 %collective-permute-start.2 = (f32[2,16,48,128]{3,2,1,0:T(8,128)S(1)}, f32[2,16,48,128]{3,2,1,0:T(8,128)S(1)}, u32[]{:S(2)}, u32[]{:S(2)}) collective-permute-start(f32[2,16,48,128]{3,2,1,0:T(8,128)S(1)} %get-tuple-element.45), channel_id=1, source_target_pairs={{1,2},{2,1},{3,4},{4,3},{5,6},{6,5},{7,8},{8,7},{9,10},{10,9},{11,... | collective-permute-start | bytes 2359304 | tf_op jit(solution)/shard_map/ppermute | solution.py:548
  7.2 6.0 %shard_map.75 = (f32[3,16,48,128]{3,2,1,0:T(8,128)S(1)}, bf16[12,96,512]{2,1,0:T(8,128)(2,1)S(1)}, bf16[12,96,512]{2,1,0:T(8,128)(2,1)S(1)}, bf16[12,96,512]{2,1,0:T(8,128)(2,1)S(1)}, f32[3,4,16,128]{3,2,1,0:T(8,128)S(1)}) custom-call(f32[48,3,4,16,128]{4,3,2,1,0:T(8,128)} %block_ref.9, s32[3,4,16,128]{3,2,1,0:T(8,128)S(1)} %copy-done.1, ...), custom_call_target="tpu_custom_call" | custom-call | flops 100000000 | bytes 8000000 | tf_op jit(solution)/shard_map/pallas_call | solution.py:295
  13.2 8.4 %shard_map.76 = (f32[3,16,48,128]{3,2,1,0:T(8,128)S(1)}, bf16[12,96,512]{2,1,0:T(8,128)(2,1)S(1)}, f32[288,192]{1,0:T(8,128)S(1)}, f32[96,192]{1,0:T(8,128)S(1)}) custom-call(f32[48,3,4,16,128]{4,3,2,1,0:T(8,128)S(1)} %collective-permute-done.src_ref, s32[3,4,16,128]{3,2,1,0:T(8,128)S(1)} %copy-done.1, s32[4,16,128]{2,1,0:T(8,128)S(1)} %copy-done.2, ...), custom_call_target="tpu_custom_call" | custom-call | flops 2000000000 | bytes 8000000 | tf_op jit(solution)/shard_map/pallas_call | solution.py:309
  21.6 3.8 %collective-permute-done.1.halo_ref.one_ref = f32[2,16,48,128]{3,2,1,0:T(8,128)S(1)} collective-permute-done((f32[2,16,48,128]{3,2,1,0:T(8,128)S(1)}, f32[2,16,48,128]{3,2,1,0:T(8,128)S(1)}, u32[]{:S(2)}, u32[]{:S(2)}) %collective-permute-start.1) | collective-permute-done | bytes 786464 | tf_op jit(solution)/shard_map/ppermute | solution.py:547
  26.4 2.9 %shard_map.79 = (f32[48,256]{1,0:T(8,128)S(1)}, f32[48,256]{1,0:T(8,128)S(1)}) custom-call(f32[3,16,48,128]{3,2,1,0:T(8,128)S(1)} %get-tuple-element.44.near_ref, f32[2,16,48,128]{3,2,1,0:T(8,128)S(1)} %collective-permute-done.2.halo_ref, s32[3,4,16,128]{3,2,1,0:T(8,128)S(1)} %copy-done.1, s32[4,16,128]{2,1,0:T(8,128)S(1)} %copy-done.2, f32[8]{0:T(128)S(1)} %copy-done.3, ...), custom_call_target="tpu_custom_call" | custom-call | tf_op jit(solution)/shard_map/pallas_call | solution.py:398
  29.4 1.2 %collective-permute-done.3 = f32[48,256]{1,0:T(8,128)S(1)} collective-permute-done((f32[48,256]{1,0:T(8,128)S(1)}, f32[48,256]{1,0:T(8,128)S(1)}, u32[]{:S(2)}, u32[]{:S(2)}) %collective-permute-start.3) | collective-permute-done | bytes 49184 | tf_op jit(solution)/shard_map/ppermute | solution.py:554
  30.8 3.4 %collective-permute-start.5 = (f32[48,256]{1,0:T(8,128)S(1)}, f32[48,256]{1,0:T(8,128)S(1)}, u32[]{:S(2)}, u32[]{:S(2)}) collective-permute-start(f32[48,256]{1,0:T(8,128)S(1)} %add.33), channel_id=1, source_target_pairs={{0,4},{2,6},{4,0},{6,2},{8,12},{10,14},{12,8},{14,10},{16,20},{18,... | collective-permute-start | bytes 147464 | tf_op jit(solution)/shard_map/ppermute | solution.py:559
  34.3 1.3 %collective-permute-start.6 = (f32[48,256]{1,0:T(8,128)S(1)}, f32[48,256]{1,0:T(8,128)S(1)}, u32[]{:S(2)}, u32[]{:S(2)}) collective-permute-start(f32[48,256]{1,0:T(8,128)S(1)} %add.33), channel_id=1, source_target_pairs={{0,6},{2,4},{4,2},{6,0},{8,14},{10,12},{12,10},{14,8},{16,22},{18,... | collective-permute-start | bytes 147464 | tf_op jit(solution)/shard_map/ppermute | solution.py:559
  35.5 1.3 %collective-permute-done.5 = f32[48,256]{1,0:T(8,128)S(1)} collective-permute-done((f32[48,256]{1,0:T(8,128)S(1)}, f32[48,256]{1,0:T(8,128)S(1)}, u32[]{:S(2)}, u32[]{:S(2)}) %collective-permute-start.5) | collective-permute-done | bytes 49184 | tf_op jit(solution)/shard_map/ppermute | solution.py:559
  36.9 2.7 %collective-permute-done.6 = f32[48,256]{1,0:T(8,128)S(1)} collective-permute-done((f32[48,256]{1,0:T(8,128)S(1)}, f32[48,256]{1,0:T(8,128)S(1)}, u32[]{:S(2)}, u32[]{:S(2)}) %collective-permute-start.6) | collective-permute-done | bytes 49184 | tf_op jit(solution)/shard_map/ppermute | solution.py:559
  39.6 1.7 %collective-permute-start.10 = (f32[48,256]{1,0:T(8,128)S(1)}, f32[48,256]{1,0:T(8,128)S(1)}, u32[]{:S(2)}, u32[]{:S(2)}) collective-permute-start(f32[48,256]{1,0:T(8,128)S(1)} %add_add_fusion.2), channel_id=1, source_target_pairs={{0,24},{2,26},{4,28},{6,30},{8,16},{10,18},{12,20},{14,22},{16,8},... | collective-permute-start | bytes 147464 | tf_op jit(solution)/shard_map/ppermute | solution.py:559
  41.2 4.0 %collective-permute-start.8 = (f32[48,256]{1,0:T(8,128)S(1)}, f32[48,256]{1,0:T(8,128)S(1)}, u32[]{:S(2)}, u32[]{:S(2)}) collective-permute-start(f32[48,256]{1,0:T(8,128)S(1)} %add_add_fusion.2), channel_id=1, source_target_pairs={{0,8},{2,10},{4,12},{6,14},{8,0},{10,2},{12,4},{14,6},{16,24},{18,... | collective-permute-start | bytes 147464 | tf_op jit(solution)/shard_map/ppermute | solution.py:559
  45.3 2.0 %collective-permute-start.9 = (f32[48,256]{1,0:T(8,128)S(1)}, f32[48,256]{1,0:T(8,128)S(1)}, u32[]{:S(2)}, u32[]{:S(2)}) collective-permute-start(f32[48,256]{1,0:T(8,128)S(1)} %add_add_fusion.2), channel_id=1, source_target_pairs={{0,16},{2,18},{4,20},{6,22},{8,24},{10,26},{12,28},{14,30},{16,0},... | collective-permute-start | bytes 147464 | tf_op jit(solution)/shard_map/ppermute | solution.py:559
  47.3 1.2 %shard_map.80.image0_ref = f32[16,3,4,16,128]{4,3,2,1,0:T(8,128)S(1)} custom-call(f32[48,3,4,16,128]{4,3,2,1,0:T(8,128)S(1)} %bitcast.1, f32[2,16,48,128]{3,2,1,0:T(8,128)S(1)} %collective-permute-done.1.halo_ref.one_ref, f32[2,16,48,128]{3,2,1,0:T(8,128)S(1)} %collective-permute-done.7.two_ref, s32[3,4,16,128]{3,2,1,0:T(8,128)S(1)} %copy-done.1), custom_call_target="tpu_custom_call" | custom-call | flops 10000000 | bytes 3000000 | tf_op jit(solution)/shard_map/pallas_call | solution.py:450
  48.5 2.4 %collective-permute-done.9 = f32[48,256]{1,0:T(8,128)S(1)} collective-permute-done((f32[48,256]{1,0:T(8,128)S(1)}, f32[48,256]{1,0:T(8,128)S(1)}, u32[]{:S(2)}, u32[]{:S(2)}) %collective-permute-start.9) | collective-permute-done | bytes 49184 | tf_op jit(solution)/shard_map/ppermute | solution.py:559
  50.9 2.0 %collective-permute-start.11 = (f32[48,256]{1,0:T(8,128)S(1)}, f32[48,256]{1,0:T(8,128)S(1)}, u32[]{:S(2)}, u32[]{:S(2)}) collective-permute-start(f32[48,256]{1,0:T(8,128)S(1)} %add_add_fusion.1), channel_id=1, source_target_pairs={{0,32},{2,34},{4,36},{6,38},{8,40},{10,42},{12,44},{14,46},{16,48}... | collective-permute-start | bytes 147464 | tf_op jit(solution)/shard_map/ppermute | solution.py:559
  52.9 4.7 %collective-permute-start.12 = (f32[48,256]{1,0:T(8,128)S(1)}, f32[48,256]{1,0:T(8,128)S(1)}, u32[]{:S(2)}, u32[]{:S(2)}) collective-permute-start(f32[48,256]{1,0:T(8,128)S(1)} %add_add_fusion.1), channel_id=1, source_target_pairs={{0,64},{2,66},{4,68},{6,70},{8,72},{10,74},{12,76},{14,78},{16,80}... | collective-permute-start | bytes 147464 | tf_op jit(solution)/shard_map/ppermute | solution.py:559
  58.7 1.4 %collective-permute-done.12 = f32[48,256]{1,0:T(8,128)S(1)} collective-permute-done((f32[48,256]{1,0:T(8,128)S(1)}, f32[48,256]{1,0:T(8,128)S(1)}, u32[]{:S(2)}, u32[]{:S(2)}) %collective-permute-start.12) | collective-permute-done | bytes 49184 | tf_op jit(solution)/shard_map/ppermute | solution.py:559
  60.2 3.2 %collective-permute-done.13 = f32[48,256]{1,0:T(8,128)S(1)} collective-permute-done((f32[48,256]{1,0:T(8,128)S(1)}, f32[48,256]{1,0:T(8,128)S(1)}, u32[]{:S(2)}, u32[]{:S(2)}) %collective-permute-start.13) | collective-permute-done | bytes 49184 | tf_op jit(solution)/shard_map/ppermute | solution.py:559
  63.4 2.0 %collective-permute-start.14 = (f32[48,256]{1,0:T(8,128)S(1)}, f32[48,256]{1,0:T(8,128)S(1)}, u32[]{:S(2)}, u32[]{:S(2)}) collective-permute-start(f32[48,256]{1,0:T(8,128)S(1)} %add_add_fusion), channel_id=1, source_target_pairs={{0,224},{2,226},{4,228},{6,230},{8,232},{10,234},{12,236},{14,238}... | collective-permute-start | bytes 147464 | tf_op jit(solution)/shard_map/ppermute | solution.py:559
  66.6 2.2 %collective-permute-done.14 = f32[48,256]{1,0:T(8,128)S(1)} collective-permute-done((f32[48,256]{1,0:T(8,128)S(1)}, f32[48,256]{1,0:T(8,128)S(1)}, u32[]{:S(2)}, u32[]{:S(2)}) %collective-permute-start.14) | collective-permute-done | bytes 49184 | tf_op jit(solution)/shard_map/ppermute | solution.py:559
  68.8 3.4 %shard_map.83 = (f32[48,3,4,16,128]{4,3,2,1,0:T(8,128)}, f32[48,96]{1,0:T(8,128)}, f32[48,96]{1,0:T(8,128)}, f32[48,96]{1,0:T(8,128)}) custom-call(f32[48,256]{1,0:T(8,128)S(1)} %add.43.rows_ref, f32[48,3,4,16,128]{4,3,2,1,0:T(8,128)S(1)} %bitcast.1, f32[16,3,4,16,128]{4,3,2,1,0:T(8,128)S(1)} %shard_map.80.image0_ref, ...), custom_call_target="tpu_custom_call" | custom-call | flops 20000000 | bytes 15000000 | tf_op jit(solution)/shard_map/pallas_call | solution.py:503
  (33 shorter events, 4.7 us)
Async XLA Ops:
  0.6 12.6 %collective-permute-start = (f32[48,3,4,16,128]{4,3,2,1,0:T(8,128)}, f32[48,3,4,16,128]{4,3,2,1,0:T(8,128)S(1)}, u32[]{:S(2)}, u32[]{:S(2)}) collective-permute-start(f32[48,3,4,16,128]{4,3,2,1,0:T(8,128)} %block_ref.9), channel_id=1, source_target_pairs={{0,1},{1,0},{2,3},{3,2},{4,5},{5,4},{6,7},{7,6},{8,9},{9,8},{10,11... | collective-permute-start | bytes 14155784 | tf_op jit(solution)/shard_map/ppermute | solution.py:543
  0.7 0.9 %copy-start = (s32[3,4,16,128]{3,2,1,0:T(8,128)S(1)}, s32[3,4,16,128]{3,2,1,0:T(8,128)}, u32[]{:S(2)}) copy-start(s32[3,4,16,128]{3,2,1,0:T(8,128)} %mask_ref.15) | copy-start | bytes 294916
  1.6 5.5 %copy-start.1 = (s32[3,4,16,128]{3,2,1,0:T(8,128)S(1)}, s32[3,4,16,128]{3,2,1,0:T(8,128)}, u32[]{:S(2)}) copy-start(s32[3,4,16,128]{3,2,1,0:T(8,128)} %mask_ref.15) | copy-start | bytes 294916
  1.6 5.5 %copy-start.2 = (s32[4,16,128]{2,1,0:T(8,128)S(1)}, s32[4,16,128]{2,1,0:T(8,128)}, u32[]{:S(2)}) copy-start(s32[4,16,128]{2,1,0:T(8,128)} %material_ref.7) | copy-start | bytes 98308
  1.6 5.5 %copy-start.3 = (f32[8]{0:T(128)S(1)}, f32[8]{0:T(128)}, u32[]{:S(2)}) copy-start(f32[8]{0:T(128)} %table_ref.7) | copy-start | bytes 100
  3.8 21.7 %collective-permute-start.1 = (f32[2,16,48,128]{3,2,1,0:T(8,128)S(1)}, f32[2,16,48,128]{3,2,1,0:T(8,128)S(1)}, u32[]{:S(2)}, u32[]{:S(2)}) collective-permute-start(f32[2,16,48,128]{3,2,1,0:T(8,128)S(1)} %get-tuple-element.43), channel_id=1, source_target_pairs={{0,2},{3,1},{2,4},{5,3},{4,6},{7,5},{6,8},{9,7},{8,10},{11,9},{10,... | collective-permute-start | bytes 2359304 | tf_op jit(solution)/shard_map/ppermute | solution.py:547
  5.3 21.0 %collective-permute-start.2 = (f32[2,16,48,128]{3,2,1,0:T(8,128)S(1)}, f32[2,16,48,128]{3,2,1,0:T(8,128)S(1)}, u32[]{:S(2)}, u32[]{:S(2)}) collective-permute-start(f32[2,16,48,128]{3,2,1,0:T(8,128)S(1)} %get-tuple-element.45), channel_id=1, source_target_pairs={{1,2},{2,1},{3,4},{4,3},{5,6},{6,5},{7,8},{8,7},{9,10},{10,9},{11,... | collective-permute-start | bytes 2359304 | tf_op jit(solution)/shard_map/ppermute | solution.py:548
  13.2 34.0 %slice-start = ((s8[4718592]{0:T(1024)(128)(4,1)}), s8[524288]{0:T(1024)(128)(4,1)S(1)}, s32[]{:S(2)}) async-start(s8[4718592]{0:T(1024)(128)(4,1)} %bitcast), calls=%async_computation | async-start | bytes 1048576
  25.5 21.8 %slice-start.1 = ((s8[4718592]{0:T(1024)(128)(4,1)}), s8[4194304]{0:T(1024)(128)(4,1)S(1)}, s32[]{:S(2)}) async-start(s8[4718592]{0:T(1024)(128)(4,1)} %bitcast), calls=%async_computation.1 | async-start | bytes 8388608
  29.3 1.3 %collective-permute-start.3 = (f32[48,256]{1,0:T(8,128)S(1)}, f32[48,256]{1,0:T(8,128)S(1)}, u32[]{:S(2)}, u32[]{:S(2)}) collective-permute-start(f32[48,256]{1,0:T(8,128)S(1)} %get-tuple-element.52), channel_id=1, source_target_pairs={{0,1},{1,0},{2,3},{3,2},{4,5},{5,4},{6,7},{7,6},{8,9},{9,8},{10,11... | collective-permute-start | bytes 147464 | tf_op jit(solution)/shard_map/ppermute | solution.py:554
  30.6 16.6 %collective-permute-start.7 = (f32[2,16,48,128]{3,2,1,0:T(8,128)S(1)}, f32[2,16,48,128]{3,2,1,0:T(8,128)S(1)}, u32[]{:S(2)}, u32[]{:S(2)}) collective-permute-start(f32[2,16,48,128]{3,2,1,0:T(8,128)S(1)} %collective-permute-done.2.halo_ref), channel_id=1, source_target_pairs={{0,1},{1,0},{2,3},{3,2},{4,5},{5,4},{6,7},{7,6},{8,9},{9,8},{10,11... | collective-permute-start | bytes 2359304 | tf_op jit(solution)/shard_map/ppermute | solution.py:556
  30.8 4.7 %collective-permute-start.4 = (f32[48,256]{1,0:T(8,128)S(1)}, f32[48,256]{1,0:T(8,128)S(1)}, u32[]{:S(2)}, u32[]{:S(2)}) collective-permute-start(f32[48,256]{1,0:T(8,128)S(1)} %add.33), channel_id=1, source_target_pairs={{0,2},{2,0},{4,6},{6,4},{8,10},{10,8},{12,14},{14,12},{16,18},{18,... | collective-permute-start | bytes 147464 | tf_op jit(solution)/shard_map/ppermute | solution.py:559
  30.8 6.0 %collective-permute-start.5 = (f32[48,256]{1,0:T(8,128)S(1)}, f32[48,256]{1,0:T(8,128)S(1)}, u32[]{:S(2)}, u32[]{:S(2)}) collective-permute-start(f32[48,256]{1,0:T(8,128)S(1)} %add.33), channel_id=1, source_target_pairs={{0,4},{2,6},{4,0},{6,2},{8,12},{10,14},{12,8},{14,10},{16,20},{18,... | collective-permute-start | bytes 147464 | tf_op jit(solution)/shard_map/ppermute | solution.py:559
  34.3 5.3 %collective-permute-start.6 = (f32[48,256]{1,0:T(8,128)S(1)}, f32[48,256]{1,0:T(8,128)S(1)}, u32[]{:S(2)}, u32[]{:S(2)}) collective-permute-start(f32[48,256]{1,0:T(8,128)S(1)} %add.33), channel_id=1, source_target_pairs={{0,6},{2,4},{4,2},{6,0},{8,14},{10,12},{12,10},{14,8},{16,22},{18,... | collective-permute-start | bytes 147464 | tf_op jit(solution)/shard_map/ppermute | solution.py:559
  39.6 8.9 %collective-permute-start.10 = (f32[48,256]{1,0:T(8,128)S(1)}, f32[48,256]{1,0:T(8,128)S(1)}, u32[]{:S(2)}, u32[]{:S(2)}) collective-permute-start(f32[48,256]{1,0:T(8,128)S(1)} %add_add_fusion.2), channel_id=1, source_target_pairs={{0,24},{2,26},{4,28},{6,30},{8,16},{10,18},{12,20},{14,22},{16,8},... | collective-permute-start | bytes 147464 | tf_op jit(solution)/shard_map/ppermute | solution.py:559
  41.2 7.2 %collective-permute-start.8 = (f32[48,256]{1,0:T(8,128)S(1)}, f32[48,256]{1,0:T(8,128)S(1)}, u32[]{:S(2)}, u32[]{:S(2)}) collective-permute-start(f32[48,256]{1,0:T(8,128)S(1)} %add_add_fusion.2), channel_id=1, source_target_pairs={{0,8},{2,10},{4,12},{6,14},{8,0},{10,2},{12,4},{14,6},{16,24},{18,... | collective-permute-start | bytes 147464 | tf_op jit(solution)/shard_map/ppermute | solution.py:559
  45.3 5.6 %collective-permute-start.9 = (f32[48,256]{1,0:T(8,128)S(1)}, f32[48,256]{1,0:T(8,128)S(1)}, u32[]{:S(2)}, u32[]{:S(2)}) collective-permute-start(f32[48,256]{1,0:T(8,128)S(1)} %add_add_fusion.2), channel_id=1, source_target_pairs={{0,16},{2,18},{4,20},{6,22},{8,24},{10,26},{12,28},{14,30},{16,0},... | collective-permute-start | bytes 147464 | tf_op jit(solution)/shard_map/ppermute | solution.py:559
  50.9 7.8 %collective-permute-start.11 = (f32[48,256]{1,0:T(8,128)S(1)}, f32[48,256]{1,0:T(8,128)S(1)}, u32[]{:S(2)}, u32[]{:S(2)}) collective-permute-start(f32[48,256]{1,0:T(8,128)S(1)} %add_add_fusion.1), channel_id=1, source_target_pairs={{0,32},{2,34},{4,36},{6,38},{8,40},{10,42},{12,44},{14,46},{16,48}... | collective-permute-start | bytes 147464 | tf_op jit(solution)/shard_map/ppermute | solution.py:559
  52.9 7.3 %collective-permute-start.12 = (f32[48,256]{1,0:T(8,128)S(1)}, f32[48,256]{1,0:T(8,128)S(1)}, u32[]{:S(2)}, u32[]{:S(2)}) collective-permute-start(f32[48,256]{1,0:T(8,128)S(1)} %add_add_fusion.1), channel_id=1, source_target_pairs={{0,64},{2,66},{4,68},{6,70},{8,72},{10,74},{12,76},{14,78},{16,80}... | collective-permute-start | bytes 147464 | tf_op jit(solution)/shard_map/ppermute | solution.py:559
  57.5 5.9 %collective-permute-start.13 = (f32[48,256]{1,0:T(8,128)S(1)}, f32[48,256]{1,0:T(8,128)S(1)}, u32[]{:S(2)}, u32[]{:S(2)}) collective-permute-start(f32[48,256]{1,0:T(8,128)S(1)} %add_add_fusion.1), channel_id=1, source_target_pairs={{0,96},{2,98},{4,100},{6,102},{8,104},{10,106},{12,108},{14,110},{... | collective-permute-start | bytes 147464 | tf_op jit(solution)/shard_map/ppermute | solution.py:559
  63.4 5.4 %collective-permute-start.14 = (f32[48,256]{1,0:T(8,128)S(1)}, f32[48,256]{1,0:T(8,128)S(1)}, u32[]{:S(2)}, u32[]{:S(2)}) collective-permute-start(f32[48,256]{1,0:T(8,128)S(1)} %add_add_fusion), channel_id=1, source_target_pairs={{0,224},{2,226},{4,228},{6,230},{8,232},{10,234},{12,236},{14,238}... | collective-permute-start | bytes 147464 | tf_op jit(solution)/shard_map/ppermute | solution.py:559

commit v5 on v3

--- a/solution.py
+++ b/solution.py
@@ -522,7 +522,7 @@
         return [i + ((i // stride % size) ^ flip) * stride - i // stride % size * stride for i in range(slabs)]
 
     def flips(size):
-        return (1, 2, 3) if size >= 4 else (1,)
+        return (3, 2, 1) if size >= 4 else (1,)
 
     x, y, z = ([partners(size, stride, flip) for flip in flips(size)] for size, stride in ((nx, 1), (ny, nx), (nz, nx * ny)))
     stages = [(x, y), (y, x), (z, z)]
@@ -552,7 +552,7 @@
     halo_other = lax.ppermute(two, both, crossed)
     near_own, own_u, *mid, mass = mine(block, mask, material, table)
     near_other, other_u, acc_v, acc_u = theirs(other, mask, material, table, own_u, *mid)
-    near_own, near_other, halo_own, halo_other = lax.optimization_barrier((near_own, near_other, halo_own, halo_other))
+    near_own, near_other, halo_own = lax.optimization_barrier((near_own, near_other, halo_own))
     own_v = own_rows(near_own, halo_own, mask, material, table)
     keep_rows, send_rows = finish(near_other, halo_other, mask, material, table, own_v, own_u, other_u, acc_v, acc_u)
     rows = keep_rows + lax.ppermute(send_rows, "col", swap)
@@ -567,9 +567,9 @@
             image = image_of(block, halo_own, halo_far, mask, (index - 1) * count, count)
             arrived, image = lax.optimization_barrier((arrived, image))
             images.append(image)
-        rows = rows + arrived[0]
+        rows = rows + arrived[-1]
         if len(arrived) == 3:
-            rows = rows + (arrived[1] + arrived[2])
+            rows = rows + (arrived[1] + arrived[0])
     return residual_of(rows, block, images, mass, scale)
 
 

time: 73.4 us -> 71.1 us (0.969); the launches traced: 73.3 us -> 70.3 us
  waiting for transfers between devices: 19.9 us -> 15.8 us
  starting transfers between devices: 24.1 us -> 25.2 us
    ppermute x10, waiting for transfers between devices: 14 us -> 10.7 us  [shards(): arrived = [lax.ppermute(rows, both, pairs) for pairs in stage]]
    ppermute x10, starting transfers between devices: 20.3 us -> 21.5 us  [shards(): arrived = [lax.ppermute(rows, both, pairs) for pairs in stage]]
    ppermute x1, waiting for transfers between devices: 0.9 us -> 0.01 us  [shards(): halo_other = lax.ppermute(two, both, crossed)]
  transfers between devices with their start and end apart: 15 -> 15, of which waited for: 9 -> 9; matrix products, arithmetic and copies ran while one was open for 0% -> 0% of each run, Pallas kernels for 27% -> 30%
where the time goes in v5:
time: 71.1 us; the launch traced here: 70.3 us
  Pallas kernels  27.4 us (39%)
  starting transfers between devices  25.2 us (35%)
  waiting for transfers between devices  15.8 us (22%)
  between operations  0.95 us (1%)
  local copies, waits for them, and re-layouts  0.91 us (1%)
    ppermute x10, starting transfers between devices, shards(): arrived = [lax.ppermute(rows, both, pairs) for pairs in stage]  21.5 us
    ppermute x10, waiting for transfers between devices, shards(): arrived = [lax.ppermute(rows, both, pairs) for pairs in stage]  10.7 us
    pallas_call x1, Pallas kernels, theirs(): pl.pallas_call(theirs_kernel, out_shape=(near, operand, jax.ShapeDtypeStr...  8.41 us
    pallas_call x1, Pallas kernels, mine(): pl.pallas_call(mine_kernel, out_shape=(near, operand, operand, operand, j...  6.02 us
    ppermute x1, waiting for transfers between devices, shards(): halo_own = lax.ppermute(one, both, straight)  3.85 us
    pallas_call x3, Pallas kernels, image_of(): pl.pallas_call(functools.partial(image_kernel, first), out_shape=jax.Shap...  3.58 us
    pallas_call x1, Pallas kernels, residual_of(): pl.pallas_call(functools.partial(residual_kernel, scale), out_shape=(jax....  3.42 us
    pallas_call x1, Pallas kernels, finish(): pl.pallas_call(finish_kernel, out_shape=(rows, rows), in_specs=[VMEM, VME...  2.89 us
  transfers between devices with their start and end apart: 15, of which 9 were waited for; matrix products, arithmetic and copies ran while one was open for 0% of the time, Pallas kernels for 30%

profile of v5, /device:TPU:8, one launch (start us, length us, event | category | flops | bytes accessed | tf_op | source)
XLA Modules:
  0.0 70.3 jit_solution(1918568034556201370)
XLA Ops:
  1.6 2.1 %shard_map.77 = (f32[2,16,48,128]{3,2,1,0:T(8,128)S(1)}, f32[2,16,48,128]{3,2,1,0:T(8,128)S(1)}) custom-call(f32[48,3,4,16,128]{4,3,2,1,0:T(8,128)} %block_ref.9, s32[3,4,16,128]{3,2,1,0:T(8,128)S(1)} %copy-done), custom_call_target="tpu_custom_call" | custom-call | tf_op jit(solution)/shard_map/pallas_call | solution.py:108
  3.8 1.6 %collective-permute-start.1 = (f32[2,16,48,128]{3,2,1,0:T(8,128)S(1)}, f32[2,16,48,128]{3,2,1,0:T(8,128)S(1)}, u32[]{:S(2)}, u32[]{:S(2)}) collective-permute-start(f32[2,16,48,128]{3,2,1,0:T(8,128)S(1)} %get-tuple-element.43), channel_id=1, source_target_pairs={{0,2},{3,1},{2,4},{5,3},{4,6},{7,5},{6,8},{9,7},{8,10},{11,9},{10,... | collective-permute-start | bytes 2359304 | tf_op jit(solution)/shard_map/ppermute | solution.py:551
  5.3 1.8 %collective-permute-start.2 = (f32[2,16,48,128]{3,2,1,0:T(8,128)S(1)}, f32[2,16,48,128]{3,2,1,0:T(8,128)S(1)}, u32[]{:S(2)}, u32[]{:S(2)}) collective-permute-start(f32[2,16,48,128]{3,2,1,0:T(8,128)S(1)} %get-tuple-element.45), channel_id=1, source_target_pairs={{1,2},{2,1},{3,4},{4,3},{5,6},{6,5},{7,8},{8,7},{9,10},{10,9},{11,... | collective-permute-start | bytes 2359304 | tf_op jit(solution)/shard_map/ppermute | solution.py:552
  7.2 6.0 %shard_map.75 = (f32[3,16,48,128]{3,2,1,0:T(8,128)S(1)}, bf16[12,96,512]{2,1,0:T(8,128)(2,1)S(1)}, bf16[12,96,512]{2,1,0:T(8,128)(2,1)S(1)}, bf16[12,96,512]{2,1,0:T(8,128)(2,1)S(1)}, f32[3,4,16,128]{3,2,1,0:T(8,128)S(1)}) custom-call(f32[48,3,4,16,128]{4,3,2,1,0:T(8,128)} %block_ref.9, s32[3,4,16,128]{3,2,1,0:T(8,128)S(1)} %copy-done.1, ...), custom_call_target="tpu_custom_call" | custom-call | flops 100000000 | bytes 8000000 | tf_op jit(solution)/shard_map/pallas_call | solution.py:295
  13.2 8.4 %shard_map.76 = (f32[3,16,48,128]{3,2,1,0:T(8,128)S(1)}, bf16[12,96,512]{2,1,0:T(8,128)(2,1)S(1)}, f32[288,192]{1,0:T(8,128)S(1)}, f32[96,192]{1,0:T(8,128)S(1)}) custom-call(f32[48,3,4,16,128]{4,3,2,1,0:T(8,128)S(1)} %collective-permute-done.src_ref, s32[3,4,16,128]{3,2,1,0:T(8,128)S(1)} %copy-done.1, s32[4,16,128]{2,1,0:T(8,128)S(1)} %copy-done.2, ...), custom_call_target="tpu_custom_call" | custom-call | flops 2000000000 | bytes 8000000 | tf_op jit(solution)/shard_map/pallas_call | solution.py:309
  21.6 3.8 %collective-permute-done.1.halo_ref.one_ref = f32[2,16,48,128]{3,2,1,0:T(8,128)S(1)} collective-permute-done((f32[2,16,48,128]{3,2,1,0:T(8,128)S(1)}, f32[2,16,48,128]{3,2,1,0:T(8,128)S(1)}, u32[]{:S(2)}, u32[]{:S(2)}) %collective-permute-start.1) | collective-permute-done | bytes 786464 | tf_op jit(solution)/shard_map/ppermute | solution.py:551
  25.5 0.9 %shard_map.78.own_v = bf16[12,96,512]{2,1,0:T(8,128)(2,1)S(1)} custom-call(f32[3,16,48,128]{3,2,1,0:T(8,128)S(1)} %get-tuple-element.46.near_ref, f32[2,16,48,128]{3,2,1,0:T(8,128)S(1)} %collective-permute-done.1.halo_ref.one_ref, s32[3,4,16,128]{3,2,1,0:T(8,128)S(1)} %copy-done.1, s32[4,16,128]{2,1,0:T(8,128)S(1)} %copy-done.2, f32[8]{0:T(128)S(1)} %copy-done.3), custom_call_target="tpu_custom_call" | custom-call | flops 10000000 | bytes 1000000 | tf_op jit(solution)/shard_map/pallas_call | solution.py:365
  26.4 2.9 %shard_map.79 = (f32[48,256]{1,0:T(8,128)S(1)}, f32[48,256]{1,0:T(8,128)S(1)}) custom-call(f32[3,16,48,128]{3,2,1,0:T(8,128)S(1)} %get-tuple-element.44.near_ref, f32[2,16,48,128]{3,2,1,0:T(8,128)S(1)} %collective-permute-done.2.halo_ref, s32[3,4,16,128]{3,2,1,0:T(8,128)S(1)} %copy-done.1, s32[4,16,128]{2,1,0:T(8,128)S(1)} %copy-done.2, f32[8]{0:T(128)S(1)} %copy-done.3, ...), custom_call_target="tpu_custom_call" | custom-call | tf_op jit(solution)/shard_map/pallas_call | solution.py:398
  29.4 1.2 %collective-permute-done.3 = f32[48,256]{1,0:T(8,128)S(1)} collective-permute-done((f32[48,256]{1,0:T(8,128)S(1)}, f32[48,256]{1,0:T(8,128)S(1)}, u32[]{:S(2)}, u32[]{:S(2)}) %collective-permute-start.3) | collective-permute-done | bytes 49184 | tf_op jit(solution)/shard_map/ppermute | solution.py:558
  30.8 3.4 %collective-permute-start.5 = (f32[48,256]{1,0:T(8,128)S(1)}, f32[48,256]{1,0:T(8,128)S(1)}, u32[]{:S(2)}, u32[]{:S(2)}) collective-permute-start(f32[48,256]{1,0:T(8,128)S(1)} %add.33), channel_id=1, source_target_pairs={{0,4},{2,6},{4,0},{6,2},{8,12},{10,14},{12,8},{14,10},{16,20},{18,... | collective-permute-start | bytes 147464 | tf_op jit(solution)/shard_map/ppermute | solution.py:563
  34.3 1.3 %collective-permute-start.6 = (f32[48,256]{1,0:T(8,128)S(1)}, f32[48,256]{1,0:T(8,128)S(1)}, u32[]{:S(2)}, u32[]{:S(2)}) collective-permute-start(f32[48,256]{1,0:T(8,128)S(1)} %add.33), channel_id=1, source_target_pairs={{0,6},{2,4},{4,2},{6,0},{8,14},{10,12},{12,10},{14,8},{16,22},{18,... | collective-permute-start | bytes 147464 | tf_op jit(solution)/shard_map/ppermute | solution.py:563
  35.5 1.3 %collective-permute-done.5 = f32[48,256]{1,0:T(8,128)S(1)} collective-permute-done((f32[48,256]{1,0:T(8,128)S(1)}, f32[48,256]{1,0:T(8,128)S(1)}, u32[]{:S(2)}, u32[]{:S(2)}) %collective-permute-start.5) | collective-permute-done | bytes 49184 | tf_op jit(solution)/shard_map/ppermute | solution.py:563
  36.9 2.7 %collective-permute-done.6 = f32[48,256]{1,0:T(8,128)S(1)} collective-permute-done((f32[48,256]{1,0:T(8,128)S(1)}, f32[48,256]{1,0:T(8,128)S(1)}, u32[]{:S(2)}, u32[]{:S(2)}) %collective-permute-start.6) | collective-permute-done | bytes 49184 | tf_op jit(solution)/shard_map/ppermute | solution.py:563
  39.6 5.6 %collective-permute-start.10 = (f32[48,256]{1,0:T(8,128)S(1)}, f32[48,256]{1,0:T(8,128)S(1)}, u32[]{:S(2)}, u32[]{:S(2)}) collective-permute-start(f32[48,256]{1,0:T(8,128)S(1)} %add_add_fusion.2), channel_id=1, source_target_pairs={{0,8},{2,10},{4,12},{6,14},{8,0},{10,2},{12,4},{14,6},{16,24},{18,... | collective-permute-start | bytes 147464 | tf_op jit(solution)/shard_map/ppermute | solution.py:563
  45.2 2.2 %collective-permute-start.9 = (f32[48,256]{1,0:T(8,128)S(1)}, f32[48,256]{1,0:T(8,128)S(1)}, u32[]{:S(2)}, u32[]{:S(2)}) collective-permute-start(f32[48,256]{1,0:T(8,128)S(1)} %add_add_fusion.2), channel_id=1, source_target_pairs={{0,16},{2,18},{4,20},{6,22},{8,24},{10,26},{12,28},{14,30},{16,0},... | collective-permute-start | bytes 147464 | tf_op jit(solution)/shard_map/ppermute | solution.py:563
  47.4 1.2 %shard_map.80.image0_ref = f32[16,3,4,16,128]{4,3,2,1,0:T(8,128)S(1)} custom-call(f32[48,3,4,16,128]{4,3,2,1,0:T(8,128)S(1)} %bitcast.1, f32[2,16,48,128]{3,2,1,0:T(8,128)S(1)} %collective-permute-done.1.halo_ref.one_ref, f32[2,16,48,128]{3,2,1,0:T(8,128)S(1)} %collective-permute-done.7.two_ref, s32[3,4,16,128]{3,2,1,0:T(8,128)S(1)} %copy-done.1), custom_call_target="tpu_custom_call" | custom-call | flops 10000000 | bytes 3000000 | tf_op jit(solution)/shard_map/pallas_call | solution.py:450
  49.3 1.5 %collective-permute-done.9 = f32[48,256]{1,0:T(8,128)S(1)} collective-permute-done((f32[48,256]{1,0:T(8,128)S(1)}, f32[48,256]{1,0:T(8,128)S(1)}, u32[]{:S(2)}, u32[]{:S(2)}) %collective-permute-start.9) | collective-permute-done | bytes 49184 | tf_op jit(solution)/shard_map/ppermute | solution.py:563
  50.8 5.4 %collective-permute-start.11 = (f32[48,256]{1,0:T(8,128)S(1)}, f32[48,256]{1,0:T(8,128)S(1)}, u32[]{:S(2)}, u32[]{:S(2)}) collective-permute-start(f32[48,256]{1,0:T(8,128)S(1)} %add_add_fusion.1), channel_id=1, source_target_pairs={{0,96},{2,98},{4,100},{6,102},{8,104},{10,106},{12,108},{14,110},{... | collective-permute-start | bytes 147464 | tf_op jit(solution)/shard_map/ppermute | solution.py:563
  56.8 1.2 %shard_map.81.image1_ref = f32[16,3,4,16,128]{4,3,2,1,0:T(8,128)S(1)} custom-call(f32[48,3,4,16,128]{4,3,2,1,0:T(8,128)S(1)} %bitcast.1, f32[2,16,48,128]{3,2,1,0:T(8,128)S(1)} %collective-permute-done.1.halo_ref.one_ref, f32[2,16,48,128]{3,2,1,0:T(8,128)S(1)} %collective-permute-done.7.two_ref, s32[3,4,16,128]{3,2,1,0:T(8,128)S(1)} %copy-done.1), custom_call_target="tpu_custom_call" | custom-call | flops 10000000 | bytes 3000000 | tf_op jit(solution)/shard_map/pallas_call | solution.py:450
  58.2 3.0 %collective-permute-done.12 = f32[48,256]{1,0:T(8,128)S(1)} collective-permute-done((f32[48,256]{1,0:T(8,128)S(1)}, f32[48,256]{1,0:T(8,128)S(1)}, u32[]{:S(2)}, u32[]{:S(2)}) %collective-permute-start.12) | collective-permute-done | bytes 49184 | tf_op jit(solution)/shard_map/ppermute | solution.py:563
  61.3 3.0 %collective-permute-start.14 = (f32[48,256]{1,0:T(8,128)S(1)}, f32[48,256]{1,0:T(8,128)S(1)}, u32[]{:S(2)}, u32[]{:S(2)}) collective-permute-start(f32[48,256]{1,0:T(8,128)S(1)} %add_add_fusion), channel_id=1, source_target_pairs={{0,224},{2,226},{4,228},{6,230},{8,232},{10,234},{12,236},{14,238}... | collective-permute-start | bytes 147464 | tf_op jit(solution)/shard_map/ppermute | solution.py:563
  64.2 1.2 %shard_map.82.image2_ref = f32[16,3,4,16,128]{4,3,2,1,0:T(8,128)S(1)} custom-call(f32[48,3,4,16,128]{4,3,2,1,0:T(8,128)S(1)} %bitcast.1, f32[2,16,48,128]{3,2,1,0:T(8,128)S(1)} %collective-permute-done.1.halo_ref.one_ref, f32[2,16,48,128]{3,2,1,0:T(8,128)S(1)} %collective-permute-done.7.two_ref, s32[3,4,16,128]{3,2,1,0:T(8,128)S(1)} %copy-done.1), custom_call_target="tpu_custom_call" | custom-call | flops 10000000 | bytes 3000000 | tf_op jit(solution)/shard_map/pallas_call | solution.py:450
  65.4 1.2 %collective-permute-done.14 = f32[48,256]{1,0:T(8,128)S(1)} collective-permute-done((f32[48,256]{1,0:T(8,128)S(1)}, f32[48,256]{1,0:T(8,128)S(1)}, u32[]{:S(2)}, u32[]{:S(2)}) %collective-permute-start.14) | collective-permute-done | bytes 49184 | tf_op jit(solution)/shard_map/ppermute | solution.py:563
  66.7 3.4 %shard_map.83 = (f32[48,3,4,16,128]{4,3,2,1,0:T(8,128)}, f32[48,96]{1,0:T(8,128)}, f32[48,96]{1,0:T(8,128)}, f32[48,96]{1,0:T(8,128)}) custom-call(f32[48,256]{1,0:T(8,128)S(1)} %add.43.rows_ref, f32[48,3,4,16,128]{4,3,2,1,0:T(8,128)S(1)} %bitcast.1, f32[16,3,4,16,128]{4,3,2,1,0:T(8,128)S(1)} %shard_map.80.image0_ref, ...), custom_call_target="tpu_custom_call" | custom-call | flops 20000000 | bytes 15000000 | tf_op jit(solution)/shard_map/pallas_call | solution.py:503
  (33 shorter events, 2.9 us)
Async XLA Ops:
  0.6 12.6 %collective-permute-start = (f32[48,3,4,16,128]{4,3,2,1,0:T(8,128)}, f32[48,3,4,16,128]{4,3,2,1,0:T(8,128)S(1)}, u32[]{:S(2)}, u32[]{:S(2)}) collective-permute-start(f32[48,3,4,16,128]{4,3,2,1,0:T(8,128)} %block_ref.9), channel_id=1, source_target_pairs={{0,1},{1,0},{2,3},{3,2},{4,5},{5,4},{6,7},{7,6},{8,9},{9,8},{10,11... | collective-permute-start | bytes 14155784 | tf_op jit(solution)/shard_map/ppermute | solution.py:547
  0.7 0.9 %copy-start = (s32[3,4,16,128]{3,2,1,0:T(8,128)S(1)}, s32[3,4,16,128]{3,2,1,0:T(8,128)}, u32[]{:S(2)}) copy-start(s32[3,4,16,128]{3,2,1,0:T(8,128)} %mask_ref.15) | copy-start | bytes 294916
  1.6 5.5 %copy-start.1 = (s32[3,4,16,128]{3,2,1,0:T(8,128)S(1)}, s32[3,4,16,128]{3,2,1,0:T(8,128)}, u32[]{:S(2)}) copy-start(s32[3,4,16,128]{3,2,1,0:T(8,128)} %mask_ref.15) | copy-start | bytes 294916
  1.6 5.5 %copy-start.2 = (s32[4,16,128]{2,1,0:T(8,128)S(1)}, s32[4,16,128]{2,1,0:T(8,128)}, u32[]{:S(2)}) copy-start(s32[4,16,128]{2,1,0:T(8,128)} %material_ref.7) | copy-start | bytes 98308
  1.6 5.5 %copy-start.3 = (f32[8]{0:T(128)S(1)}, f32[8]{0:T(128)}, u32[]{:S(2)}) copy-start(f32[8]{0:T(128)} %table_ref.7) | copy-start | bytes 100
  3.8 21.7 %collective-permute-start.1 = (f32[2,16,48,128]{3,2,1,0:T(8,128)S(1)}, f32[2,16,48,128]{3,2,1,0:T(8,128)S(1)}, u32[]{:S(2)}, u32[]{:S(2)}) collective-permute-start(f32[2,16,48,128]{3,2,1,0:T(8,128)S(1)} %get-tuple-element.43), channel_id=1, source_target_pairs={{0,2},{3,1},{2,4},{5,3},{4,6},{7,5},{6,8},{9,7},{8,10},{11,9},{10,... | collective-permute-start | bytes 2359304 | tf_op jit(solution)/shard_map/ppermute | solution.py:551
  5.3 21.0 %collective-permute-start.2 = (f32[2,16,48,128]{3,2,1,0:T(8,128)S(1)}, f32[2,16,48,128]{3,2,1,0:T(8,128)S(1)}, u32[]{:S(2)}, u32[]{:S(2)}) collective-permute-start(f32[2,16,48,128]{3,2,1,0:T(8,128)S(1)} %get-tuple-element.45), channel_id=1, source_target_pairs={{1,2},{2,1},{3,4},{4,3},{5,6},{6,5},{7,8},{8,7},{9,10},{10,9},{11,... | collective-permute-start | bytes 2359304 | tf_op jit(solution)/shard_map/ppermute | solution.py:552
  13.2 34.1 %slice-start = ((s8[4718592]{0:T(1024)(128)(4,1)}), s8[524288]{0:T(1024)(128)(4,1)S(1)}, s32[]{:S(2)}) async-start(s8[4718592]{0:T(1024)(128)(4,1)} %bitcast), calls=%async_computation | async-start | bytes 1048576
  25.5 21.9 %slice-start.1 = ((s8[4718592]{0:T(1024)(128)(4,1)}), s8[4194304]{0:T(1024)(128)(4,1)S(1)}, s32[]{:S(2)}) async-start(s8[4718592]{0:T(1024)(128)(4,1)} %bitcast), calls=%async_computation.1 | async-start | bytes 8388608
  29.3 1.3 %collective-permute-start.3 = (f32[48,256]{1,0:T(8,128)S(1)}, f32[48,256]{1,0:T(8,128)S(1)}, u32[]{:S(2)}, u32[]{:S(2)}) collective-permute-start(f32[48,256]{1,0:T(8,128)S(1)} %get-tuple-element.52), channel_id=1, source_target_pairs={{0,1},{1,0},{2,3},{3,2},{4,5},{5,4},{6,7},{7,6},{8,9},{9,8},{10,11... | collective-permute-start | bytes 147464 | tf_op jit(solution)/shard_map/ppermute | solution.py:558
  30.6 16.7 %collective-permute-start.7 = (f32[2,16,48,128]{3,2,1,0:T(8,128)S(1)}, f32[2,16,48,128]{3,2,1,0:T(8,128)S(1)}, u32[]{:S(2)}, u32[]{:S(2)}) collective-permute-start(f32[2,16,48,128]{3,2,1,0:T(8,128)S(1)} %collective-permute-done.2.halo_ref), channel_id=1, source_target_pairs={{0,1},{1,0},{2,3},{3,2},{4,5},{5,4},{6,7},{7,6},{8,9},{9,8},{10,11... | collective-permute-start | bytes 2359304 | tf_op jit(solution)/shard_map/ppermute | solution.py:560
  30.8 4.7 %collective-permute-start.4 = (f32[48,256]{1,0:T(8,128)S(1)}, f32[48,256]{1,0:T(8,128)S(1)}, u32[]{:S(2)}, u32[]{:S(2)}) collective-permute-start(f32[48,256]{1,0:T(8,128)S(1)} %add.33), channel_id=1, source_target_pairs={{0,2},{2,0},{4,6},{6,4},{8,10},{10,8},{12,14},{14,12},{16,18},{18,... | collective-permute-start | bytes 147464 | tf_op jit(solution)/shard_map/ppermute | solution.py:563
  30.8 6.0 %collective-permute-start.5 = (f32[48,256]{1,0:T(8,128)S(1)}, f32[48,256]{1,0:T(8,128)S(1)}, u32[]{:S(2)}, u32[]{:S(2)}) collective-permute-start(f32[48,256]{1,0:T(8,128)S(1)} %add.33), channel_id=1, source_target_pairs={{0,4},{2,6},{4,0},{6,2},{8,12},{10,14},{12,8},{14,10},{16,20},{18,... | collective-permute-start | bytes 147464 | tf_op jit(solution)/shard_map/ppermute | solution.py:563
  34.3 5.3 %collective-permute-start.6 = (f32[48,256]{1,0:T(8,128)S(1)}, f32[48,256]{1,0:T(8,128)S(1)}, u32[]{:S(2)}, u32[]{:S(2)}) collective-permute-start(f32[48,256]{1,0:T(8,128)S(1)} %add.33), channel_id=1, source_target_pairs={{0,6},{2,4},{4,2},{6,0},{8,14},{10,12},{12,10},{14,8},{16,22},{18,... | collective-permute-start | bytes 147464 | tf_op jit(solution)/shard_map/ppermute | solution.py:563
  39.6 9.0 %collective-permute-start.10 = (f32[48,256]{1,0:T(8,128)S(1)}, f32[48,256]{1,0:T(8,128)S(1)}, u32[]{:S(2)}, u32[]{:S(2)}) collective-permute-start(f32[48,256]{1,0:T(8,128)S(1)} %add_add_fusion.2), channel_id=1, source_target_pairs={{0,8},{2,10},{4,12},{6,14},{8,0},{10,2},{12,4},{14,6},{16,24},{18,... | collective-permute-start | bytes 147464 | tf_op jit(solution)/shard_map/ppermute | solution.py:563
  45.2 4.1 %collective-permute-start.8 = (f32[48,256]{1,0:T(8,128)S(1)}, f32[48,256]{1,0:T(8,128)S(1)}, u32[]{:S(2)}, u32[]{:S(2)}) collective-permute-start(f32[48,256]{1,0:T(8,128)S(1)} %add_add_fusion.2), channel_id=1, source_target_pairs={{0,24},{2,26},{4,28},{6,30},{8,16},{10,18},{12,20},{14,22},{16,8},... | collective-permute-start | bytes 147464 | tf_op jit(solution)/shard_map/ppermute | solution.py:563
  45.2 5.6 %collective-permute-start.9 = (f32[48,256]{1,0:T(8,128)S(1)}, f32[48,256]{1,0:T(8,128)S(1)}, u32[]{:S(2)}, u32[]{:S(2)}) collective-permute-start(f32[48,256]{1,0:T(8,128)S(1)} %add_add_fusion.2), channel_id=1, source_target_pairs={{0,16},{2,18},{4,20},{6,22},{8,24},{10,26},{12,28},{14,30},{16,0},... | collective-permute-start | bytes 147464 | tf_op jit(solution)/shard_map/ppermute | solution.py:563
  50.8 7.5 %collective-permute-start.11 = (f32[48,256]{1,0:T(8,128)S(1)}, f32[48,256]{1,0:T(8,128)S(1)}, u32[]{:S(2)}, u32[]{:S(2)}) collective-permute-start(f32[48,256]{1,0:T(8,128)S(1)} %add_add_fusion.1), channel_id=1, source_target_pairs={{0,96},{2,98},{4,100},{6,102},{8,104},{10,106},{12,108},{14,110},{... | collective-permute-start | bytes 147464 | tf_op jit(solution)/shard_map/ppermute | solution.py:563
  56.2 5.1 %collective-permute-start.12 = (f32[48,256]{1,0:T(8,128)S(1)}, f32[48,256]{1,0:T(8,128)S(1)}, u32[]{:S(2)}, u32[]{:S(2)}) collective-permute-start(f32[48,256]{1,0:T(8,128)S(1)} %add_add_fusion.1), channel_id=1, source_target_pairs={{0,64},{2,66},{4,68},{6,70},{8,72},{10,74},{12,76},{14,78},{16,80}... | collective-permute-start | bytes 147464 | tf_op jit(solution)/shard_map/ppermute | solution.py:563
  56.2 5.1 %collective-permute-start.13 = (f32[48,256]{1,0:T(8,128)S(1)}, f32[48,256]{1,0:T(8,128)S(1)}, u32[]{:S(2)}, u32[]{:S(2)}) collective-permute-start(f32[48,256]{1,0:T(8,128)S(1)} %add_add_fusion.1), channel_id=1, source_target_pairs={{0,32},{2,34},{4,36},{6,38},{8,40},{10,42},{12,44},{14,46},{16,48}... | collective-permute-start | bytes 147464 | tf_op jit(solution)/shard_map/ppermute | solution.py:563
  61.3 5.4 %collective-permute-start.14 = (f32[48,256]{1,0:T(8,128)S(1)}, f32[48,256]{1,0:T(8,128)S(1)}, u32[]{:S(2)}, u32[]{:S(2)}) collective-permute-start(f32[48,256]{1,0:T(8,128)S(1)} %add_add_fusion), channel_id=1, source_target_pairs={{0,224},{2,226},{4,228},{6,230},{8,232},{10,234},{12,236},{14,238}... | collective-permute-start | bytes 147464 | tf_op jit(solution)/shard_map/ppermute | solution.py:563
